TPU v7x, 512 devices: a whole 4x8x8 slice. The times are simulated.
512 devices in a mesh: series: 8 (over x, core), tm: 64 (over z, y).
Axes of the slice: x: 4, y: 8, z: 8, core: 2. Of those that a mesh axis runs over, the one named last changes fastest.
Arguments:
- panel: float32 [1024, 32768], P('series', 'tm'), may hold values from -6 to 6
- observed: int32 [1024, 256], P('series', 'tm'), may hold values 0 or 1
- start_time: float32 [64, 32768], P(None, 'tm'), may hold values from -0.125 to 0.125
- ar_weight: float32 [64, 14], replicated, may hold values from -0.3 to 0.3
- lags: int32 [14], replicated, may hold values from 1 to 2016, as said below
Outputs:
- series_factors: float32 [1024, 64], P('series')
- time_factors: float32 [64, 32768], P(None, 'tm')
Inputs may be any that keep to these rules, and one draw needn't show every extreme that they name: `lags`: entries 0 to 11 are distinct values of 1 to 24; entry 12 lies in 256 to 511; entry 13 equals 2016.
All inputs are finite; a program needn't handle non-finite values. No bound on the sum of `observed` on one device may be relied on, other than what follows from the above.
Results may differ from a plain program's by a relative error of at most 0.0003.
Values sent between devices are 32-bit elements; how exact they have to be, the bound alone decides.
No kernel may reach another device: no remote copies, remote signals or barrier semaphores. Data moves between devices by JAX's collectives and lax.ppermute only.
A program may use at most 64 MiB of HBM per device.

v0:
```python
import jax
import jax.numpy as jnp
from jax import lax
from jax.sharding import PartitionSpec as P

TILE = 128


HIGH = lax.Precision.HIGHEST
ridge_factor = 1.0
ridge_time = 0.05
ar_strength = 0.25


def shifted(value, axis, by):
    length = lax.axis_size(axis)
    pairs = [(i, i + by) for i in range(length) if 0 <= i + by < length]
    return lax.ppermute(value, axis, pairs)


def solve_cells(gram_flat, rhs):
    count = rhs.shape[0]
    rank = rhs.shape[1]
    mats = gram_flat.reshape(count, rank, rank) + ridge_factor * jnp.eye(rank, dtype=jnp.float32)
    chol = jnp.linalg.cholesky(mats)

    def single(lower, vector):
        return jax.scipy.linalg.cho_solve((lower, True), vector)

    return jax.vmap(single)(chol, rhs)


def far_slabs(field, sign):
    slabs = []
    for distance in (1, 2, 3, 4):
        slabs.append(shifted(field, "tm", sign * distance))
    return slabs


def per_device(panel, observed, start_time, ar_weight, lags):
    cells, span = panel.shape
    rank = start_time.shape[0]
    per_dev = span // TILE
    count_lags = lags.shape[0]
    cells_all = cells * lax.axis_size("series")
    flags = observed.astype(jnp.float32)
    masked = panel * jnp.repeat(flags, TILE, axis=1)
    tiles_x = start_time.reshape(rank, per_dev, TILE)
    grams = jnp.einsum("kbt,jbt->bkj", tiles_x, tiles_x, precision=HIGH).reshape(
        per_dev, rank * rank
    )
    part_rhs = jnp.dot(masked, start_time.T, precision=HIGH)
    part_gram = jnp.dot(flags, grams, precision=HIGH)
    cell_gram, cell_rhs = lax.psum((part_gram, part_rhs), "tm")
    factors = solve_cells(cell_gram, cell_rhs)
    outer = (factors[:, :, None] * factors[:, None, :]).reshape(cells, rank * rank)
    part_h = jnp.dot(flags.T, outer, precision=HIGH)
    part_time = jnp.dot(factors.T, masked, precision=HIGH)
    sum_h, sum_time = lax.psum((part_h, part_time), "series")
    tile_h = (sum_h / cells_all).reshape(per_dev, rank, rank)
    rhs_time = sum_time / cells_all
    longest = 4 * span - span // 16
    global_steps = lax.axis_index("tm") * span + jnp.arange(span, dtype=jnp.int32)
    valid = (global_steps >= longest).astype(jnp.float32)[None, :]

    def apply(field):
        data = jnp.einsum(
            "bkj,jbt->kbt", tile_h, field.reshape(rank, per_dev, TILE), precision=HIGH
        ).reshape(rank, span)
        behind = far_slabs(field, 1)
        context = jnp.concatenate([behind[3], behind[2], behind[1], behind[0], field], axis=1)
        lagged = jnp.zeros((rank, span), jnp.float32)
        for index in range(count_lags):
            start = 4 * span - lags[index]
            lagged = lagged + ar_weight[:, index : index + 1] * lax.dynamic_slice_in_dim(
                context, start, span, 1
            )
        errors = valid * (field - lagged)
        ahead = far_slabs(errors, -1)
        later = jnp.concatenate([errors, ahead[0], ahead[1], ahead[2], ahead[3]], axis=1)
        back = errors
        for index in range(count_lags):
            start = lags[index]
            back = back - ar_weight[:, index : index + 1] * lax.dynamic_slice_in_dim(
                later, start, span, 1
            )
        return data + ridge_time * field + ar_strength * back

    solution = start_time
    residual = rhs_time - apply(solution)
    direction = residual
    norm_now = lax.psum(jnp.sum(residual * residual), "tm")
    for step in range(3):
        image = apply(direction)
        alpha = norm_now / lax.psum(jnp.sum(direction * image), "tm")
        solution = solution + alpha * direction
        residual = residual - alpha * image
        norm_next = lax.psum(jnp.sum(residual * residual), "tm")
        direction = residual + norm_next / norm_now * direction
        norm_now = norm_next
    return (factors, solution)


def solution(mesh):
    placed = (P("series", "tm"), P("series", "tm"), P(None, "tm"), P(), P())
    return jax.shard_map(
        per_device,
        mesh=mesh,
        in_specs=placed,
        out_specs=(P("series", None), P(None, "tm")),
        check_vma=False,
    )
```

profile of v0, /device:TPU:270, one launch (start us, length us, event | category | flops | bytes accessed | tf_op | source)
XLA Modules:
  0.0 2179.8 jit_solution(9670283137631917033)
XLA Ops:
  7.2 6.8 collective-permute-start
  16.9 4.5 collective-permute-start.2
  30.4 4.6 copy.42
  85.6 5.5 collective-permute-start.5
  91.2 272.8 %psum.71 = f32[128,64]{0,1:T(8,128)} all-reduce(f32[128,64]{0,1:T(8,128)S(1)} %fusion.22), channel_id=1, replica_groups=mesh['series'=8,'tm'=64] {'tm'}, use_global_device_ids=true, to_apply=%region_3.4 | all-reduce | flops 8192 | bytes 65536 | tf_op jit(solution)/shard_map/psum | solution.py:54
  363.9 4.5 collective-permute-start.6
  373.9 5.1 broadcast_add_fusion
  378.9 5.7 copy.44
  384.6 6.9 fusion
  391.5 752.2 %custom-call.11 = f32[128,64,64]{2,1,0:T(8,128)} custom-call(f32[128,64,64]{2,1,0:T(8,128)} %fusion), custom_call_target="Cholesky" | custom-call | tf_op jit(solution)/shard_map/jit(cholesky)/cholesky | solution.py:25
  1150.7 67.2 %custom-call.12 = f32[128,1,64,64]{0,2,3,1:T(8,128)S(1)} custom-call(f32[128,1,64,64]{0,3,2,1:T(8,128)} %select_bitcast_fusion), custom_call_target="InvertDiagBlocksLowerTriangular" | custom-call | tf_op jit(solution)/shard_map/vmap(jit(_cho_solve))/triangular_solve | solution.py:28
  1224.1 71.1 %all-reduce.7.cloned.1.call-done = (f32[4,4096]{1,0:T(4,128)}, f32[64,512]{1,0:T(8,128)}) async-done(((f32[4,4096]{1,0:T(4,128)}, f32[64,512]{1,0:T(8,128)}), (f32[4,4096]{1,0:T(4,128)}, f32[64,512]{1,0:T(8,128)})) %all-reduce.7.cloned.1.call-update) | async-done | bytes 196624 | tf_op jit(solution)/shard_map/psum | solution.py:59
  1298.2 6.5 collective-permute-start.8
  1307.2 4.3 collective-permute-start.10
  1315.0 7.9 collective-permute-done.9
  1323.0 6.2 collective-permute-done.10
  1330.7 4.4 collective-permute-start.12
  1341.3 5.0 collective-permute-start.15
  1346.3 13.6 collective-permute-done.14
  1361.4 138.4 %all-reduce = (f32[]{:T(128)}, f32[]{:T(128)}) all-reduce(f32[]{:T(128)} %get-tuple-element.3, f32[]{:T(128)} %get-tuple-element.2), channel_id=1, replica_groups=mesh['series'=8,'tm'=64] {'tm'}, use_global_device_ids=true, to_apply=%region_7.8 | all-reduce | flops 2 | bytes 16 | tf_op jit(solution)/shard_map/psum | solution.py:92
  1501.8 145.6 %psum.76 = f32[]{:T(128)} all-reduce(f32[]{:T(128)} %get-tuple-element.14), channel_id=1, replica_groups=mesh['series'=8,'tm'=64] {'tm'}, use_global_device_ids=true, to_apply=%region_11.12 | all-reduce | flops 1 | bytes 8 | tf_op jit(solution)/shard_map/psum | solution.py:98
  1656.4 5.2 collective-permute-done.16
  1677.1 5.1 collective-permute-start.22
  1682.2 7.3 collective-permute-start.23
  1689.7 4.8 collective-permute-done.23
  1695.9 141.0 %psum.77 = f32[]{:T(128)} all-reduce(f32[]{:T(128)} %get-tuple-element.10), channel_id=1, replica_groups=mesh['series'=8,'tm'=64] {'tm'}, use_global_device_ids=true, to_apply=%region_13.14 | all-reduce | flops 1 | bytes 8 | tf_op jit(solution)/shard_map/psum | solution.py:95
  1839.0 142.8 %psum.78 = f32[]{:T(128)} all-reduce(f32[]{:T(128)} %multiply_reduce_fusion), channel_id=1, replica_groups=mesh['series'=8,'tm'=64] {'tm'}, use_global_device_ids=true, to_apply=%region_15.16 | all-reduce | flops 1 | bytes 8 | tf_op jit(solution)/shard_map/psum | solution.py:98
  1991.0 5.3 collective-permute-done.24
  2010.4 5.5 collective-permute-start.30
  2016.0 6.8 collective-permute-start.31
  2022.9 5.3 collective-permute-done.31
  2029.5 141.4 %psum.79 = f32[]{:T(128)} all-reduce(f32[]{:T(128)} %fusion.5), channel_id=1, replica_groups=mesh['series'=8,'tm'=64] {'tm'}, use_global_device_ids=true, to_apply=%region_17.18 | all-reduce | flops 1 | bytes 8 | tf_op jit(solution)/shard_map/psum | solution.py:95
  (192 shorter events, 104.8 us)
Async XLA Ops:
  7.2 366.7 %all-reduce.5.cloned.1.call-start = ((), (), s32[]{:S(2)}) async-start(), calls=%async_computation | async-start | bytes 8388608 | tf_op jit(solution)/shard_map/psum | solution.py:54
  7.2 47.6 %collective-permute-start = (f32[64,512]{1,0:T(8,128)}, f32[64,512]{1,0:T(8,128)S(1)}, u32[]{:S(2)}, u32[]{:S(2)}) collective-permute-start(f32[64,512]{1,0:T(8,128)} %param.7), channel_id=1, source_target_pairs={{0,4},{1,5},{2,6},{3,7},{4,8},{5,9},{6,10},{7,11},{8,12},{9,13},{1... | collective-permute-start | bytes 393224 | tf_op jit(solution)/shard_map/ppermute | solution.py:18
  14.1 40.8 %collective-permute-start.1 = (f32[64,512]{1,0:T(8,128)}, f32[64,512]{1,0:T(8,128)S(1)}, u32[]{:S(2)}, u32[]{:S(2)}) collective-permute-start(f32[64,512]{1,0:T(8,128)} %param.7), channel_id=1, source_target_pairs={{0,3},{1,4},{2,5},{3,6},{4,7},{5,8},{6,9},{7,10},{8,11},{9,12},{10... | collective-permute-start | bytes 393224 | tf_op jit(solution)/shard_map/ppermute | solution.py:18
  16.9 38.0 %collective-permute-start.2 = (f32[64,512]{1,0:T(8,128)}, f32[64,512]{1,0:T(8,128)S(1)}, u32[]{:S(2)}, u32[]{:S(2)}) collective-permute-start(f32[64,512]{1,0:T(8,128)} %param.7), channel_id=1, source_target_pairs={{0,2},{1,3},{2,4},{3,5},{4,6},{5,7},{6,8},{7,9},{8,10},{9,11},{10,... | collective-permute-start | bytes 393224 | tf_op jit(solution)/shard_map/ppermute | solution.py:18
  21.4 33.5 %collective-permute-start.3 = (f32[64,512]{1,0:T(8,128)}, f32[64,512]{1,0:T(8,128)S(1)}, u32[]{:S(2)}, u32[]{:S(2)}) collective-permute-start(f32[64,512]{1,0:T(8,128)} %param.7), channel_id=1, source_target_pairs={{0,1},{1,2},{2,3},{3,4},{4,5},{5,6},{6,7},{7,8},{8,9},{9,10},{10,1... | collective-permute-start | bytes 393224 | tf_op jit(solution)/shard_map/ppermute | solution.py:18
  35.1 1260.0 %all-reduce.7.cloned.1.call-start = ((), (), s32[]{:S(2)}) async-start(), calls=%async_computation.1 | async-start | bytes 393216 | tf_op jit(solution)/shard_map/psum | solution.py:59
  55.8 314.7 %collective-permute-start.4 = (f32[64,512]{1,0:T(8,128)S(1)}, f32[64,512]{1,0:T(8,128)S(1)}, u32[]{:S(2)}, u32[]{:S(2)}) collective-permute-start(f32[64,512]{1,0:T(8,128)S(1)} %get-tuple-element.20), channel_id=1, source_target_pairs={{1,0},{2,1},{3,2},{4,3},{5,4},{6,5},{7,6},{8,7},{9,8},{10,9},{11,1... | collective-permute-start | bytes 393224 | tf_op jit(solution)/shard_map/ppermute | solution.py:18
  85.6 284.9 %collective-permute-start.5 = (f32[64,512]{1,0:T(8,128)S(1)}, f32[64,512]{1,0:T(8,128)S(1)}, u32[]{:S(2)}, u32[]{:S(2)}) collective-permute-start(f32[64,512]{1,0:T(8,128)S(1)} %get-tuple-element.20), channel_id=1, source_target_pairs={{2,0},{3,1},{4,2},{5,3},{6,4},{7,5},{8,6},{9,7},{10,8},{11,9},{12,... | collective-permute-start | bytes 393224 | tf_op jit(solution)/shard_map/ppermute | solution.py:18
  368.4 854.8 %collective-permute-start.7 = (f32[64,512]{1,0:T(8,128)S(1)}, f32[64,512]{1,0:T(8,128)}, u32[]{:S(2)}, u32[]{:S(2)}) collective-permute-start(f32[64,512]{1,0:T(8,128)S(1)} %get-tuple-element.20), channel_id=1, source_target_pairs={{4,0},{5,1},{6,2},{7,3},{8,4},{9,5},{10,6},{11,7},{12,8},{13,9},{1... | collective-permute-start | bytes 393224 | tf_op jit(solution)/shard_map/ppermute | solution.py:18
  1298.2 16.8 collective-permute-start.8
  1304.7 18.3 collective-permute-start.9
  1307.2 21.9 %collective-permute-start.10 = (f32[64,512]{1,0:T(8,128)S(1)}, f32[64,512]{1,0:T(8,128)S(1)}, u32[]{:S(2)}, u32[]{:S(2)}) collective-permute-start(f32[64,512]{1,0:T(8,128)S(1)} %fusion.9), channel_id=1, source_target_pairs={{0,2},{1,3},{2,4},{3,5},{4,6},{5,7},{6,8},{7,9},{8,10},{9,11},{10,... | collective-permute-start | bytes 393224 | tf_op jit(solution)/shard_map/ppermute | solution.py:18
  1311.6 18.3 collective-permute-start.11
  1330.7 15.5 collective-permute-start.12
  1338.3 21.6 collective-permute-start.14
  1341.3 18.6 collective-permute-start.15
  1648.7 12.9 collective-permute-start.16
  1650.7 14.2 collective-permute-start.17
  1652.6 15.1 collective-permute-start.18
  1654.5 13.2 collective-permute-start.19
  1668.5 21.0 collective-permute-start.20
  1672.9 16.7 collective-permute-start.21
  1677.1 12.5 collective-permute-start.22
  1682.2 12.2 collective-permute-start.23
  1983.3 13.0 collective-permute-start.24
  1985.2 12.5 collective-permute-start.25
  1987.1 14.7 collective-permute-start.26
  1989.0 12.8 collective-permute-start.27
  2002.6 20.1 collective-permute-start.28
  2006.5 16.3 collective-permute-start.29
  2010.4 12.4 collective-permute-start.30
  2016.0 12.2 collective-permute-start.31
  (34 other events, 1494.5 us)
Sparse Core Ops, SparseCore 0:
  35.2 169.2 all-reduce.4
  1223.3 71.8 all-reduce.6
where the time goes:
time: 2180 us
  blocking collectives  982 us (45%)
  other arithmetic  849 us (39%)
  waiting for transfers between devices  135 us (6%)
  starting transfers between devices  120 us (6%)
  between operations  65.6 us (3%)
    another operation x4, other arithmetic, solve_cells(): chol = jnp.linalg.cholesky(mats)  754 us
    psum x2, blocking collectives, per_device(): norm_next = lax.psum(jnp.sum(residual * residual), 'tm')  288 us
    psum x2, blocking collectives, per_device(): alpha = norm_now / lax.psum(jnp.sum(direction * image), 'tm')  282 us
    psum x1, blocking collectives, per_device(): cell_gram, cell_rhs = lax.psum((part_gram, part_rhs), 'tm')  273 us
    psum x1, blocking collectives, per_device(): norm_now = lax.psum(jnp.sum(residual * residual), 'tm')  138 us
    ppermute x32, starting transfers between devices, shifted(): return lax.ppermute(value, axis, pairs)  120 us
    psum x1, waiting for transfers between devices, per_device(): sum_h, sum_time = lax.psum((part_h, part_time), 'series')  71.1 us
    another operation x4, other arithmetic, single(): return jax.scipy.linalg.cho_solve((lower, True), vector)  69.9 us
  transfers between devices with their start and end apart: 34, of which 14 were waited for; matrix products, arithmetic and copies ran while one was open for 40% of the time, Pallas kernels for 0%

commit v1 on v0

v1 whole, which is shorter than its diff:
```python
import functools

import jax
import jax.numpy as jnp
from jax import lax
from jax.experimental import pallas as pl
from jax.experimental.pallas import tpu as pltpu
from jax.sharding import Mesh, PartitionSpec as P

HIGH = lax.Precision.HIGHEST
TILE = 128
LAGS = 14
LONGEST = 2016
RIDGE_FACTOR = 1.0
RIDGE_TIME = 0.05
AR = 0.25
TM = ("tz", "ty")
F32 = jnp.float32
VMEM = pl.BlockSpec(memory_space=pltpu.VMEM)
SMEM = pl.BlockSpec(memory_space=pltpu.SMEM)


def struct(*shape):
    return jax.ShapeDtypeStruct(shape, F32)


def iota(shape, dim):
    return lax.broadcasted_iota(jnp.int32, shape, dim)


def call(kernel, outs, ins, scratch=()):
    specs = [SMEM if a.dtype == jnp.int32 and a.ndim == 1 else VMEM for a in ins]
    return pl.pallas_call(
        kernel,
        out_shape=outs,
        in_specs=specs,
        out_specs=jax.tree.map(lambda _: VMEM, outs),
        scratch_shapes=list(scratch),
        compiler_params=pltpu.CompilerParams(vmem_limit_bytes=32 * 1024 * 1024),
    )(*ins)


def dot(a, b, dims):
    return lax.dot_general(a, b, (dims, ((), ())), precision=HIGH, preferred_element_type=F32)


def front_kernel(panel_ref, obs_ref, x_ref, out_ref):
    flags = obs_ref[...].astype(F32)
    x = x_ref[...]
    row = iota((32, 128), 0)
    col = iota((32, 128), 1) % 64
    keep = (col < 32) | (col - 32 >= row)
    diag_at = iota((64, 128), 0) == iota((64, 128), 1) % 64
    left = iota((64, 128), 1) < 64
    packs, diags, lanes = [], [], []
    masked = []
    for b in range(4):
        xb = x[:, b * TILE : (b + 1) * TILE]
        gram = dot(xb, xb, ((1,), (1,)))
        twice = jnp.concatenate([gram, gram], axis=1)
        packs.append(jnp.where(keep, twice[32:64], pltpu.roll(twice[0:32], 32, axis=1)))
        diags.append(jnp.sum(jnp.where(diag_at, twice, 0.0), axis=0, keepdims=True))
        flag = flags[:, b : b + 1]
        lanes.append(jnp.where(left, flag[0:64], flag[64:128]))
        masked.append(panel_ref[:, b * TILE : (b + 1) * TILE] * flag)
    rhs = dot(jnp.concatenate(masked, axis=1), x, ((1,), (1,)))
    rhs = jnp.concatenate([rhs[0:64], rhs[64:128]], axis=1)
    diag = lanes[0] * diags[0] + lanes[1] * diags[1] + lanes[2] * diags[2] + lanes[3] * diags[3]
    sub = iota((8, 128), 0)
    for j in range(64):
        total = packs[0] * lanes[0][j : j + 1]
        for b in range(1, 4):
            total = total + packs[b] * lanes[b][j : j + 1]
        out_ref[j, 0:32, :] = total
        tail = jnp.where(sub == 0, diag[j : j + 1], jnp.where(sub == 1, rhs[j : j + 1], 0.0))
        out_ref[j, 32:40, :] = tail


def solve_kernel(parts_ref, out_ref):
    total = parts_ref[0]
    for j in range(1, 64):
        total = total + parts_ref[j]
    pack = total[0:32]
    diag = total[32:33]
    rhs = total[33:34]
    flipped = jnp.concatenate([pack, pack, pack, pack], axis=0).T
    row = iota((32, 128), 0)
    lane = iota((32, 128), 1)
    group = lane // 32
    col = lane % 32
    first = lane < 64
    upper_t = jnp.where(first, flipped[32:64], flipped[96:128])
    cross = jnp.where(first, flipped[0:32], flipped[64:96])
    odd = group % 2 == 1
    top_left = jnp.where(col < row, pltpu.roll(pack, 96, axis=1), jnp.where(col == row, diag, upper_t))
    top = jnp.where(odd, cross, top_left)
    bottom = jnp.where(odd & (col < row), upper_t, pack)
    eye = (iota((64, 128), 0) == iota((64, 128), 1) % 64).astype(F32)
    mat = jnp.concatenate([top, bottom], axis=0) + RIDGE_FACTOR * eye
    blocks = [mat[8 * i : 8 * i + 8] for i in range(8)]
    side = jnp.broadcast_to(rhs, (8, 128))
    half = iota((8, 128), 1) < 64
    within = iota((8, 128), 1) % 64

    def spread(value, k):
        return jnp.where(half, value[:, k : k + 1], value[:, 64 + k : 65 + k])

    for k in range(64):
        i, r = divmod(k, 8)
        pivot_row = jnp.broadcast_to(blocks[i][r : r + 1], (8, 128))
        inverse = 1.0 / spread(pivot_row, k)
        factor = jnp.where(within == k, 1.0 - inverse, pivot_row * inverse)
        side = side - spread(side, k) * factor
        for m in range(i if r < 7 else i + 1, 8):
            blocks[m] = blocks[m] - spread(blocks[m], k) * factor
    out_ref[...] = jnp.broadcast_to(side[0:1][None], out_ref.shape)


def normal_kernel(scale, gathered_ref, panel_ref, obs_ref, factors_ref, out_ref):
    gathered = gathered_ref[...]
    factors = jnp.concatenate([gathered[:, 0:64], gathered[:, 64:128]], axis=0)
    factors_ref[...] = factors
    flags = obs_ref[...].astype(F32)
    for b in range(4):
        flag = flags[:, b : b + 1]
        out_ref[:, b * TILE : (b + 1) * TILE] = scale * dot(
            factors, panel_ref[:, b * TILE : (b + 1) * TILE] * flag, ((0,), (0,))
        )
    for pair in range(2):
        halves = [dot(factors * flags[:, b : b + 1], factors, ((0,), (0,))) for b in (2 * pair, 2 * pair + 1)]
        out_ref[:, 512 + 128 * pair : 640 + 128 * pair] = scale * jnp.concatenate(halves, axis=1)


def lagged(read, count, lags_ref, weight_ref, ahead):
    lane = iota((8, 128), 1)
    sums = [None] * count
    for index in range(LAGS):
        lag = lags_ref[index]
        if ahead:
            start = lag // 128
            shift = lag % 128
        else:
            back = (lag + 127) // 128
            start = -back
            shift = back * 128 - lag
        cut = 128 - shift
        weight = weight_ref[index]
        own = lane < cut
        turn = jnp.where(cut == 128, 0, cut)
        low = pltpu.roll(read(start), turn, axis=1)
        for j in range(count):
            high = pltpu.roll(read(start + j + 1), turn, axis=1)
            term = weight * jnp.where(own, low, high)
            sums[j] = term if sums[j] is None else sums[j] + term
            low = high
    return sums


def residuals(read, count, first_step, steps_all, meta_ref, weight_ref):
    past = lagged(read, count, meta_ref, weight_ref, False)
    lane = iota((8, 128), 1)
    out = []
    for j in range(count):
        step = first_step + 128 * j + lane
        out.append(jnp.where((step >= LONGEST) & (step < steps_all), read(j) - past[j], 0.0))
    return out


def ar_part(read, first_step, steps_all, meta_ref, weight_ref, errors_ref):
    errors = residuals(read, 20, first_step, steps_all, meta_ref, weight_ref)
    for j in range(20):
        errors_ref[j] = errors[j]
    later = lagged(lambda j: errors_ref[j], 4, meta_ref, weight_ref, True)
    return [errors[j] - later[j] for j in range(4)]


def start_kernel(steps_all, sums_ref, x_ref, near_ref, weight_ref, meta_ref, out_ref, h_ref, context_ref, errors_ref):
    slab, y = meta_ref[LAGS], meta_ref[LAGS + 1]
    fill_context(near_ref, context_ref)
    base = 16 + 4 * y
    total = sums_ref[0]
    for j in range(1, 8):
        total = total + sums_ref[j]

    def read(j):
        return context_ref[base + j]

    back = ar_part(read, slab * 512, steps_all, meta_ref, weight_ref, errors_ref)
    for q in range(4):
        h = total[:, 512 + 64 * q : 576 + 64 * q]
        h_ref[q] = h
        image = dot(h, x_ref[:, q * 128 : (q + 1) * 128], ((1,), (0,))) + RIDGE_TIME * read(q) + AR * back[q]
        value = total[:, q * 128 : (q + 1) * 128] - image
        for j in range(8):
            out_ref[j, q] = value


def fill_context(near_refs, context_ref):
    middle, before, after = near_refs
    for j in range(16):
        context_ref[j] = before[j]
        if after is not None:
            context_ref[48 + j] = after[j]
    for j in range(32):
        context_ref[16 + j] = middle[j]


def data_part(h_ref, wide_ref, q):
    return dot(h_ref[q], wide_ref[:, q].reshape(64, 128), ((1,), (0,)))


def image_kernel(
    steps_all, middle_ref, before_ref, after_ref, wide_ref, h_ref, weight_ref, theta_ref, meta_ref,
    out_ref, context_ref, errors_ref,
):
    slab, y = meta_ref[LAGS], meta_ref[LAGS + 1]
    fill_context((middle_ref, before_ref, after_ref), context_ref)
    base = 16 + 4 * y

    def read(j):
        return context_ref[base + j]

    back = ar_part(read, slab * 512, steps_all, meta_ref, weight_ref, errors_ref)
    theta = theta_ref[...]
    for q in range(4):
        own = read(q)
        value = data_part(h_ref, wide_ref, q) + (RIDGE_TIME - theta) * own + AR * back[q]
        for j in range(8):
            out_ref[j, q] = value


def two_sum(a, b):
    s = a + b
    t = s - a
    return s, (a - (s - t)) + (b - t)


def pair_add(a, b):
    s, e = two_sum(a[0], b[0])
    e = e + (a[1] + b[1])
    high = s + e
    return high, e - (high - s)


def split(a):
    c = a * 4097.0
    high = c - (c - a)
    return high, a - high


def pair_mul(a, b):
    p = a[0] * b[0]
    ah, al = split(a[0])
    bh, bl = split(b[0])
    e = ((ah * bh - p) + ah * bl + al * bh) + al * bl
    e = e + (a[0] * b[1] + a[1] * b[0])
    high = p + e
    return high, e - (high - p)


def pair_neg(a):
    return -a[0], -a[1]


def pair_sub(a, b):
    return pair_add(a, pair_neg(b))


def pair_div(a, b):
    first = a[0] / b[0]
    zero = jnp.zeros_like(first)
    rest = pair_sub(a, pair_mul(b, (first, zero)))
    second = rest[0] / b[0]
    return two_sum(first, second)


def pair_tree(values):
    while len(values) > 1:
        values = [
            pair_add(values[i], values[i + 1]) if i + 1 < len(values) else values[i]
            for i in range(0, len(values), 2)
        ]
    return values[0]


def moment_kernel(
    steps_all, middle_ref, before_ref, wide_ref, h_ref, weight_ref, u0_ref, u1_ref, u2_ref, meta_ref,
    out_ref, context_ref,
):
    slab, y = meta_ref[LAGS], meta_ref[LAGS + 1]
    fill_context((middle_ref, before_ref, None), context_ref)
    base = 16 + 4 * y

    def read(j):
        return context_ref[base + j]

    errors = residuals(read, 4, slab * 512, steps_all, meta_ref, weight_ref)
    sums = [jnp.zeros((8, 128), F32)] * 7
    for q in range(4):
        u0, u1, u2 = u0_ref[0, q], u1_ref[0, q], u2_ref[0, q]
        image = data_part(h_ref, wide_ref, q) + RIDGE_TIME * u2
        terms = [u0 * u0, u0 * u1, u0 * u2, u1 * u1, u1 * u2, u2 * u2, u2 * image + AR * (errors[q] * errors[q])]
        sums = [a + b for a, b in zip(sums, terms)]
    zero = jnp.zeros((8, 128), F32)
    sub = iota((8, 128), 0)
    packed = (zero, zero)
    for i in range(7):
        pair = (sums[i], zero)
        for by in (4, 2, 1):
            pair = pair_add(pair, (pltpu.roll(pair[0], by, axis=0), pltpu.roll(pair[1], by, axis=0)))
        packed = (jnp.where(sub == i, pair[0], packed[0]), jnp.where(sub == i, pair[1], packed[1]))
    for by in (64, 32, 16, 8, 4, 2, 1):
        packed = pair_add(packed, (pltpu.roll(packed[0], by, axis=1), pltpu.roll(packed[1], by, axis=1)))
    value = jnp.where(iota((8, 128), 1) < 64, packed[0], packed[1])
    out_ref[...] = jnp.broadcast_to(value[None], out_ref.shape)


def sum_pairs(parts_ref, count):
    half = iota((8, 128), 1) < 64
    pairs = []
    for j in range(count):
        part = parts_ref[j]
        other = pltpu.roll(part, 64, axis=1)
        pairs.append((jnp.where(half, part, other), jnp.where(half, other, part)))
    return pair_tree(pairs)


def join_kernel(parts_ref, out_ref):
    high, low = sum_pairs(parts_ref, 8)
    value = jnp.where(iota((8, 128), 1) < 64, high, low)
    out_ref[...] = jnp.broadcast_to(value[None], out_ref.shape)


def finish_kernel(parts_ref, theta_ref, x_ref, wide0_ref, wide1_ref, wide2_ref, out_ref):
    high, low = sum_pairs(parts_ref, 64)

    def moment(i):
        return tuple(jnp.broadcast_to(a[i : i + 1], (8, 128)) for a in (high, low))

    g00, g01, g02, g11, g12, g22, m22 = [moment(i) for i in range(7)]
    theta = (theta_ref[...], jnp.zeros((8, 128), F32))
    m00 = pair_add(g01, pair_mul(theta, g00))
    m01 = pair_add(g11, pair_mul(theta, g01))
    m02 = pair_add(g12, pair_mul(theta, g02))
    m11 = pair_add(g12, pair_mul(theta, g11))
    m12 = pair_add(g22, pair_mul(theta, g12))
    l10 = pair_div(m01, m00)
    l20 = pair_div(m02, m00)
    d1 = pair_sub(m11, pair_mul(l10, m01))
    n12 = pair_sub(m12, pair_mul(l10, m02))
    y1 = pair_sub(g01, pair_mul(l10, g00))
    l21 = pair_div(n12, d1)
    d2 = pair_sub(pair_sub(m22, pair_mul(l20, m02)), pair_mul(l21, n12))
    y2 = pair_sub(pair_sub(g02, pair_mul(l20, g00)), pair_mul(l21, y1))
    tiny = 1e-12
    c2 = jnp.where(d2[0] > tiny * m22[0], y2[0] / d2[0], 0.0)
    zero = jnp.zeros_like(c2)
    c1 = pair_sub(pair_div(y1, d1), pair_mul(l21, (c2, zero)))
    c1 = jnp.where(d1[0] > tiny * m11[0], c1[0], 0.0)
    c0 = pair_div(g00, m00)
    c0 = pair_sub(c0, pair_mul(l10, (c1, zero)))
    c0 = pair_sub(c0, pair_mul(l20, (c2, zero)))[0]
    for s in range(8):
        for q in range(4):
            at = (slice(8 * s, 8 * s + 8), slice(128 * q, 128 * q + 128))
            step = c0 * wide0_ref[s, q] + c1 * wide1_ref[s, q] + c2 * wide2_ref[s, q]
            out_ref[at] = x_ref[at] + step


def ring(length, by):
    return [(i, (i + by) % length) for i in range(length)]


def planes(spread, both):
    middle = lax.all_to_all(spread, "ty", 0, 0).reshape(32, 8, 128)
    count = lax.axis_size("tz")
    before = lax.ppermute(middle[16:32], "tz", ring(count, 1))
    after = lax.ppermute(middle[0:16], "tz", ring(count, -1)) if both else None
    return middle, before, after


def per_device(panel, observed, start_time, ar_weight, lags):
    cells = panel.shape[0]
    steps_all = 64 * 512
    cells_all = cells * 8
    series = lax.axis_index("series")
    y = lax.axis_index("ty")
    slab = lax.axis_index("tz") * 8 + y
    meta = jnp.concatenate([lags, jnp.stack([slab, y]).astype(jnp.int32)])
    own_weight = lax.dynamic_slice_in_dim(ar_weight, 8 * series, 8, 0)
    weight = jnp.broadcast_to(own_weight.T[:, :, None], (LAGS, 8, 128))
    theta = RIDGE_TIME + AR * (1.0 + jnp.sum(ar_weight * ar_weight) / 64.0)
    theta = jnp.broadcast_to(theta, (8, 128))
    context = pltpu.VMEM((64, 8, 128), F32)
    errors = pltpu.VMEM((20, 8, 128), F32)

    own_x = lax.dynamic_slice_in_dim(start_time, 8 * series, 8, 0).reshape(8, 4, 128).transpose(1, 0, 2)
    near_x = planes(jnp.broadcast_to(own_x[None], (8, 4, 8, 128)), True)

    parts = call(front_kernel, struct(64, 40, 128), (panel, observed, start_time))
    parts = lax.all_to_all(parts, TM, 0, 0)
    solved = call(solve_kernel, struct(64, 1, 128), (parts,))
    gathered = lax.all_to_all(solved, TM, 0, 0).reshape(64, 128)
    factors, normal = call(
        functools.partial(normal_kernel, 1.0 / cells_all),
        (struct(cells, 64), struct(64, 768)),
        (gathered, panel, observed),
    )
    sums = lax.all_to_all(normal.reshape(8, 8, 768), "series", 0, 0)

    def begin(sums, x, middle, before, after, weight, meta, out, h, ctx, err):
        start_kernel(steps_all, sums, x, (middle, before, after), weight, meta, out, h, ctx, err)

    u0, h = call(
        begin,
        (struct(8, 4, 8, 128), struct(4, 8, 64)),
        (sums, start_time, *near_x, weight, meta),
        (context, errors),
    )
    middle, before, after = planes(u0, True)
    wide0 = lax.all_to_all(u0, "series", 0, 0)
    image = functools.partial(image_kernel, steps_all)
    u1 = call(
        image, struct(8, 4, 8, 128), (middle, before, after, wide0, h, weight, theta, meta), (context, errors)
    )
    middle, before, after = planes(u1, True)
    wide1 = lax.all_to_all(u1, "series", 0, 0)
    u2 = call(
        image, struct(8, 4, 8, 128), (middle, before, after, wide1, h, weight, theta, meta), (context, errors)
    )
    middle, before, _ = planes(u2, False)
    wide2 = lax.all_to_all(u2, "series", 0, 0)
    moments = call(
        functools.partial(moment_kernel, steps_all),
        struct(8, 8, 128),
        (middle, before, wide2, h, weight, u0, u1, u2, meta),
        (context,),
    )
    moments = lax.all_to_all(moments, "series", 0, 0)
    moments = call(join_kernel, struct(64, 8, 128), (moments,))
    moments = lax.all_to_all(moments, TM, 0, 0)
    result = call(finish_kernel, struct(64, 512), (moments, theta, start_time, wide0, wide1, wide2))
    return (factors, result)


def solution(mesh):
    grid = Mesh(mesh.devices.reshape(8, 8, 8), ("series", "tz", "ty"))
    return jax.shard_map(
        per_device,
        mesh=grid,
        in_specs=(P("series", TM), P("series", TM), P(None, TM), P(), P()),
        out_specs=(P("series", None), P(None, TM)),
        check_vma=False,
    )
```

time: 2180 us -> 230 us (0.11)
  the two profiles are of different devices: /device:TPU:270 before, /device:TPU:1 now
where the time goes in v1:
time: 230 us; the launch traced here: 228 us
  starting transfers between devices  85.5 us (37%)
  waiting for transfers between devices  70.9 us (31%)
  blocking collectives  42.6 us (19%)
  Pallas kernels  22.3 us (10%)
  local copies, waits for them, and re-layouts  4.22 us (2%)
    all_to_all x1, waiting for transfers between devices, per_device(): parts = lax.all_to_all(parts, TM, 0, 0)  33.1 us
    all_to_all x3, blocking collectives, planes(): middle = lax.all_to_all(spread, 'ty', 0, 0).reshape(32, 8, 128)  33.1 us
    pallas_call x9, Pallas kernels, call(): pl.pallas_call(kernel, out_shape=outs, in_specs=specs, out_specs=jax.tree...  22.3 us
    all_to_all x1, starting transfers between devices, per_device(): parts = lax.all_to_all(parts, TM, 0, 0)  17.1 us
    ppermute x3, starting transfers between devices, planes(): after = lax.ppermute(middle[0:16], 'tz', ring(count, -1)) if both else None  14.6 us
    all_to_all x1, waiting for transfers between devices, per_device(): moments = lax.all_to_all(moments, TM, 0, 0)  11.9 us
    all_to_all x1, waiting for transfers between devices, per_device(): gathered = lax.all_to_all(solved, TM, 0, 0).reshape(64, 128)  10.7 us
    all_to_all x1, blocking collectives, per_device(): moments = lax.all_to_all(moments, 'series', 0, 0)  9.54 us
  transfers between devices with their start and end apart: 15, of which 11 were waited for; matrix products, arithmetic and copies ran while one was open for 1% of the time, Pallas kernels for 1%

profile of v1, /device:TPU:1, one launch (start us, length us, event | category | flops | bytes accessed | tf_op | source)
XLA Modules:
  0.0 227.7 jit_solution(17171284249726098793)
XLA Ops:
  3.3 2.1 shard_map.68
  5.4 17.1 %all-to-all-start = ((f32[64,40,128]{2,1,0:T(8,128)}), f32[64,40,128]{2,1,0:T(8,128)S(1)}, u32[]{:S(2)}, u32[]{:S(2)}) async-start(f32[64,40,128]{2,1,0:T(8,128)} %shard_map.68), calls=%async_computation | async-start | bytes 2621440 | tf_op jit(solution)/shard_map/all_to_all | solution.py:401
  22.6 33.1 %all-to-all-done.parts_ref = f32[64,40,128]{2,1,0:T(8,128)S(1)} async-done(((f32[64,40,128]{2,1,0:T(8,128)}), f32[64,40,128]{2,1,0:T(8,128)S(1)}, u32[]{:S(2)}, u32[]{:S(2)}) %all-to-all-start) | async-done | bytes 1310752 | tf_op jit(solution)/shard_map/all_to_all | solution.py:401
  55.7 9.5 %shard_map.69 = f32[64,1,128]{2,1,0:T(1,128)} custom-call(f32[64,40,128]{2,1,0:T(8,128)S(1)} %all-to-all-done.parts_ref), custom_call_target="tpu_custom_call" | custom-call | tf_op jit(solution)/shard_map/pallas_call | solution.py:33
  65.3 7.8 %all-to-all-start.1 = ((f32[64,1,128]{2,1,0:T(1,128)}), f32[64,1,128]{2,1,0:T(1,128)S(1)}, u32[]{:S(2)}, u32[]{:S(2)}) async-start(f32[64,1,128]{2,1,0:T(1,128)} %shard_map.69), calls=%async_computation.1 | async-start | bytes 65536 | tf_op jit(solution)/shard_map/all_to_all | solution.py:403
  73.1 10.7 %all-to-all-done.1 = f32[64,1,128]{2,1,0:T(1,128)S(1)} async-done(((f32[64,1,128]{2,1,0:T(1,128)}), f32[64,1,128]{2,1,0:T(1,128)S(1)}, u32[]{:S(2)}, u32[]{:S(2)}) %all-to-all-start.1) | async-done | bytes 32800 | tf_op jit(solution)/shard_map/all_to_all | solution.py:403
  84.5 3.4 %all-to-all-start.3 = ((f32[8,4,8,128]{3,2,1,0:T(8,128)}), f32[8,4,8,128]{3,2,1,0:T(8,128)S(1)}, u32[]{:S(2)}, u32[]{:S(2)}) async-start(f32[8,4,8,128]{3,2,1,0:T(8,128)} %broadcast_in_dim.6), calls=%async_computation.3 | async-start | bytes 262144 | tf_op jit(solution)/shard_map/all_to_all | solution.py:375
  88.0 1.4 shard_map.70
  89.4 6.4 %all-to-all-done.3 = f32[8,4,8,128]{3,2,1,0:T(8,128)S(1)} async-done(((f32[8,4,8,128]{3,2,1,0:T(8,128)}), f32[8,4,8,128]{3,2,1,0:T(8,128)S(1)}, u32[]{:S(2)}, u32[]{:S(2)}) %all-to-all-start.3) | async-done | bytes 131104 | tf_op jit(solution)/shard_map/all_to_all | solution.py:375
  95.8 8.7 %all-to-all-start.2 = ((f32[8,8,768]{2,1,0:T(8,128)}), f32[8,8,768]{2,1,0:T(8,128)S(1)}, u32[]{:S(2)}, u32[]{:S(2)}) async-start(f32[8,8,768]{2,1,0:T(8,128)} %bitcast.1), calls=%async_computation.2 | async-start | bytes 393216 | tf_op jit(solution)/shard_map/all_to_all | solution.py:409
  104.5 2.2 collective-permute-start
  106.8 4.2 %collective-permute-start.1 = (f32[16,8,128]{2,1,0:T(8,128)S(1)}, f32[16,8,128]{2,1,0:T(8,128)S(1)}, u32[]{:S(2)}, u32[]{:S(2)}) collective-permute-start(f32[16,8,128]{2,1,0:T(8,128)S(1)} %bitcast.30), channel_id=1, source_target_pairs={{0,56},{8,0},{16,8},{24,16},{32,24},{40,32},{48,40},{56,48},{1,57}... | collective-permute-start | bytes 196616 | tf_op jit(solution)/shard_map/ppermute | solution.py:378
  112.4 1.9 shard_map.71
  114.3 11.0 %all_to_all.60 = f32[8,4,8,128]{3,2,1,0:T(8,128)S(1)} all-to-all(f32[8,4,8,128]{3,2,1,0:T(8,128)} %get-tuple-element.8.u0_ref), channel_id=1, replica_groups=mesh['series'=8,'tz'=8,'ty'=8] {'ty'}, dimensions={0} | all-to-all | bytes 262144 | tf_op jit(solution)/shard_map/all_to_all | solution.py:375
  125.3 7.2 %all-to-all-start.5 = ((f32[8,4,8,128]{3,2,1,0:T(8,128)}), f32[8,4,8,128]{3,2,1,0:T(8,128)S(1)}, u32[]{:S(2)}, u32[]{:S(2)}) async-start(f32[8,4,8,128]{3,2,1,0:T(8,128)} %get-tuple-element.8.u0_ref), calls=%async_computation.5 | async-start | bytes 262144 | tf_op jit(solution)/shard_map/all_to_all | solution.py:421
  132.6 2.0 collective-permute-start.2
  134.6 5.1 %collective-permute-start.3 = (f32[16,8,128]{2,1,0:T(8,128)S(1)}, f32[16,8,128]{2,1,0:T(8,128)S(1)}, u32[]{:S(2)}, u32[]{:S(2)}) collective-permute-start(f32[16,8,128]{2,1,0:T(8,128)S(1)} %bitcast.27), channel_id=1, source_target_pairs={{0,56},{8,0},{16,8},{24,16},{32,24},{40,32},{48,40},{56,48},{1,57}... | collective-permute-start | bytes 196616 | tf_op jit(solution)/shard_map/ppermute | solution.py:378
  141.2 1.8 shard_map.72.u1_ref
  143.1 11.0 %all_to_all.61 = f32[8,4,8,128]{3,2,1,0:T(8,128)S(1)} all-to-all(f32[8,4,8,128]{3,2,1,0:T(8,128)} %shard_map.72.u1_ref), channel_id=1, replica_groups=mesh['series'=8,'tz'=8,'ty'=8] {'ty'}, dimensions={0} | all-to-all | bytes 262144 | tf_op jit(solution)/shard_map/all_to_all | solution.py:375
  154.1 6.8 %all-to-all-start.7 = ((f32[8,4,8,128]{3,2,1,0:T(8,128)}), f32[8,4,8,128]{3,2,1,0:T(8,128)S(1)}, u32[]{:S(2)}, u32[]{:S(2)}) async-start(f32[8,4,8,128]{3,2,1,0:T(8,128)} %shard_map.72.u1_ref), calls=%async_computation.7 | async-start | bytes 262144 | tf_op jit(solution)/shard_map/all_to_all | solution.py:427
  160.9 1.9 collective-permute-start.4
  162.8 5.2 %collective-permute-start.5 = (f32[16,8,128]{2,1,0:T(8,128)S(1)}, f32[16,8,128]{2,1,0:T(8,128)S(1)}, u32[]{:S(2)}, u32[]{:S(2)}) collective-permute-start(f32[16,8,128]{2,1,0:T(8,128)S(1)} %bitcast.29), channel_id=1, source_target_pairs={{0,56},{8,0},{16,8},{24,16},{32,24},{40,32},{48,40},{56,48},{1,57}... | collective-permute-start | bytes 196616 | tf_op jit(solution)/shard_map/ppermute | solution.py:378
  169.5 1.8 shard_map.73.u2_ref
  171.3 11.0 %all_to_all.62 = f32[8,4,8,128]{3,2,1,0:T(8,128)S(1)} all-to-all(f32[8,4,8,128]{3,2,1,0:T(8,128)} %shard_map.73.u2_ref), channel_id=1, replica_groups=mesh['series'=8,'tz'=8,'ty'=8] {'ty'}, dimensions={0} | all-to-all | bytes 262144 | tf_op jit(solution)/shard_map/all_to_all | solution.py:375
  182.4 6.8 %all-to-all-start.9 = ((f32[8,4,8,128]{3,2,1,0:T(8,128)}), f32[8,4,8,128]{3,2,1,0:T(8,128)S(1)}, u32[]{:S(2)}, u32[]{:S(2)}) async-start(f32[8,4,8,128]{3,2,1,0:T(8,128)} %shard_map.73.u2_ref), calls=%async_computation.9 | async-start | bytes 262144 | tf_op jit(solution)/shard_map/all_to_all | solution.py:432
  189.2 2.0 collective-permute-start.6
  191.2 3.3 %all-to-all-done.9.wide_ref.wide2_ref = f32[8,4,8,128]{3,2,1,0:T(8,128)S(1)} async-done(((f32[8,4,8,128]{3,2,1,0:T(8,128)}), f32[8,4,8,128]{3,2,1,0:T(8,128)S(1)}, u32[]{:S(2)}, u32[]{:S(2)}) %all-to-all-start.9) | async-done | bytes 131104 | tf_op jit(solution)/shard_map/all_to_all | solution.py:432
  194.4 2.4 %collective-permute-done.6.before_ref = f32[16,8,128]{2,1,0:T(8,128)S(1)} collective-permute-done((f32[16,8,128]{2,1,0:T(8,128)S(1)}, f32[16,8,128]{2,1,0:T(8,128)S(1)}, u32[]{:S(2)}, u32[]{:S(2)}) %collective-permute-start.6) | collective-permute-done | bytes 65568 | tf_op jit(solution)/shard_map/ppermute | solution.py:377
  196.8 1.8 shard_map.74
  198.7 9.5 %all_to_all.63.parts_ref = f32[8,8,128]{2,1,0:T(8,128)S(1)} all-to-all(f32[8,8,128]{2,1,0:T(8,128)S(1)} %shard_map.74), channel_id=1, replica_groups=mesh['series'=8,'tz'=8,'ty'=8] {'series'}, dimensions={0} | all-to-all | bytes 65536 | tf_op jit(solution)/shard_map/all_to_all | solution.py:439
  209.0 5.0 %all-to-all-start.11 = ((f32[64,8,128]{2,1,0:T(8,128)}), f32[64,8,128]{2,1,0:T(8,128)S(1)}, u32[]{:S(2)}, u32[]{:S(2)}) async-start(f32[64,8,128]{2,1,0:T(8,128)} %shard_map.75), calls=%async_computation.11 | async-start | bytes 524288 | tf_op jit(solution)/shard_map/all_to_all | solution.py:441
  214.7 11.9 %all-to-all-done.11.parts_ref = f32[64,8,128]{2,1,0:T(8,128)S(1)} async-done(((f32[64,8,128]{2,1,0:T(8,128)}), f32[64,8,128]{2,1,0:T(8,128)S(1)}, u32[]{:S(2)}, u32[]{:S(2)}) %all-to-all-start.11) | async-done | bytes 262176 | tf_op jit(solution)/shard_map/all_to_all | solution.py:441
  (36 shorter events, 9.7 us)
Async XLA Ops:
  1.4 0.9 copy-start
  2.3 0.9 copy-start.2
  5.4 50.3 %all-to-all-start = ((f32[64,40,128]{2,1,0:T(8,128)}), f32[64,40,128]{2,1,0:T(8,128)S(1)}, u32[]{:S(2)}, u32[]{:S(2)}) async-start(f32[64,40,128]{2,1,0:T(8,128)} %shard_map.68), calls=%async_computation | async-start | bytes 2621440 | tf_op jit(solution)/shard_map/all_to_all | solution.py:401
  22.5 50.5 %copy-start.1 = (f32[64,512]{1,0:T(8,128)S(1)}, f32[64,512]{1,0:T(8,128)}, u32[]{:S(2)}) copy-start(f32[64,512]{1,0:T(8,128)} %x_ref.3) | copy-start | bytes 393220
  22.5 65.3 %copy-start.4 = (f32[64,14]{0,1:T(8,128)S(1)}, f32[64,14]{0,1:T(8,128)}, u32[]{:S(2)}) copy-start(f32[64,14]{0,1:T(8,128)} %param.8) | copy-start | bytes 10756
  22.6 65.4 %copy-start.3 = (f32[128,512]{1,0:T(8,128)S(1)}, f32[128,512]{1,0:T(8,128)}, u32[]{:S(2)}) copy-start(f32[128,512]{1,0:T(8,128)} %panel_ref.3) | copy-start | bytes 786436
  22.6 88.5 %copy-start.5 = (s32[14]{0:T(128)S(1)}, s32[14]{0:T(128)}, u32[]{:S(2)}) copy-start(s32[14]{0:T(128)} %param.9) | copy-start | bytes 172
  65.3 18.6 %all-to-all-start.1 = ((f32[64,1,128]{2,1,0:T(1,128)}), f32[64,1,128]{2,1,0:T(1,128)S(1)}, u32[]{:S(2)}, u32[]{:S(2)}) async-start(f32[64,1,128]{2,1,0:T(1,128)} %shard_map.69), calls=%async_computation.1 | async-start | bytes 65536 | tf_op jit(solution)/shard_map/all_to_all | solution.py:403
  84.5 11.3 %all-to-all-start.3 = ((f32[8,4,8,128]{3,2,1,0:T(8,128)}), f32[8,4,8,128]{3,2,1,0:T(8,128)S(1)}, u32[]{:S(2)}, u32[]{:S(2)}) async-start(f32[8,4,8,128]{3,2,1,0:T(8,128)} %broadcast_in_dim.6), calls=%async_computation.3 | async-start | bytes 262144 | tf_op jit(solution)/shard_map/all_to_all | solution.py:375
  95.8 16.6 %all-to-all-start.2 = ((f32[8,8,768]{2,1,0:T(8,128)}), f32[8,8,768]{2,1,0:T(8,128)S(1)}, u32[]{:S(2)}, u32[]{:S(2)}) async-start(f32[8,8,768]{2,1,0:T(8,128)} %bitcast.1), calls=%async_computation.2 | async-start | bytes 393216 | tf_op jit(solution)/shard_map/all_to_all | solution.py:409
  104.5 6.8 %collective-permute-start = (f32[16,8,128]{2,1,0:T(8,128)S(1)}, f32[16,8,128]{2,1,0:T(8,128)S(1)}, u32[]{:S(2)}, u32[]{:S(2)}) collective-permute-start(f32[16,8,128]{2,1,0:T(8,128)S(1)} %bitcast.32), channel_id=1, source_target_pairs={{0,8},{8,16},{16,24},{24,32},{32,40},{40,48},{48,56},{56,0},{1,9},... | collective-permute-start | bytes 196616 | tf_op jit(solution)/shard_map/ppermute | solution.py:377
  106.8 5.6 %collective-permute-start.1 = (f32[16,8,128]{2,1,0:T(8,128)S(1)}, f32[16,8,128]{2,1,0:T(8,128)S(1)}, u32[]{:S(2)}, u32[]{:S(2)}) collective-permute-start(f32[16,8,128]{2,1,0:T(8,128)S(1)} %bitcast.30), channel_id=1, source_target_pairs={{0,56},{8,0},{16,8},{24,16},{32,24},{40,32},{48,40},{56,48},{1,57}... | collective-permute-start | bytes 196616 | tf_op jit(solution)/shard_map/ppermute | solution.py:378
  125.3 15.6 %all-to-all-start.5 = ((f32[8,4,8,128]{3,2,1,0:T(8,128)}), f32[8,4,8,128]{3,2,1,0:T(8,128)S(1)}, u32[]{:S(2)}, u32[]{:S(2)}) async-start(f32[8,4,8,128]{3,2,1,0:T(8,128)} %get-tuple-element.8.u0_ref), calls=%async_computation.5 | async-start | bytes 262144 | tf_op jit(solution)/shard_map/all_to_all | solution.py:421
  132.6 8.4 %collective-permute-start.2 = (f32[16,8,128]{2,1,0:T(8,128)S(1)}, f32[16,8,128]{2,1,0:T(8,128)S(1)}, u32[]{:S(2)}, u32[]{:S(2)}) collective-permute-start(f32[16,8,128]{2,1,0:T(8,128)S(1)} %bitcast.28), channel_id=1, source_target_pairs={{0,8},{8,16},{16,24},{24,32},{32,40},{40,48},{48,56},{56,0},{1,9},... | collective-permute-start | bytes 196616 | tf_op jit(solution)/shard_map/ppermute | solution.py:377
  134.6 6.6 %collective-permute-start.3 = (f32[16,8,128]{2,1,0:T(8,128)S(1)}, f32[16,8,128]{2,1,0:T(8,128)S(1)}, u32[]{:S(2)}, u32[]{:S(2)}) collective-permute-start(f32[16,8,128]{2,1,0:T(8,128)S(1)} %bitcast.27), channel_id=1, source_target_pairs={{0,56},{8,0},{16,8},{24,16},{32,24},{40,32},{48,40},{56,48},{1,57}... | collective-permute-start | bytes 196616 | tf_op jit(solution)/shard_map/ppermute | solution.py:378
  154.1 13.9 %all-to-all-start.7 = ((f32[8,4,8,128]{3,2,1,0:T(8,128)}), f32[8,4,8,128]{3,2,1,0:T(8,128)S(1)}, u32[]{:S(2)}, u32[]{:S(2)}) async-start(f32[8,4,8,128]{3,2,1,0:T(8,128)} %shard_map.72.u1_ref), calls=%async_computation.7 | async-start | bytes 262144 | tf_op jit(solution)/shard_map/all_to_all | solution.py:427
  160.9 7.7 %collective-permute-start.4 = (f32[16,8,128]{2,1,0:T(8,128)S(1)}, f32[16,8,128]{2,1,0:T(8,128)S(1)}, u32[]{:S(2)}, u32[]{:S(2)}) collective-permute-start(f32[16,8,128]{2,1,0:T(8,128)S(1)} %bitcast.31), channel_id=1, source_target_pairs={{0,8},{8,16},{16,24},{24,32},{32,40},{40,48},{48,56},{56,0},{1,9},... | collective-permute-start | bytes 196616 | tf_op jit(solution)/shard_map/ppermute | solution.py:377
  162.8 6.7 %collective-permute-start.5 = (f32[16,8,128]{2,1,0:T(8,128)S(1)}, f32[16,8,128]{2,1,0:T(8,128)S(1)}, u32[]{:S(2)}, u32[]{:S(2)}) collective-permute-start(f32[16,8,128]{2,1,0:T(8,128)S(1)} %bitcast.29), channel_id=1, source_target_pairs={{0,56},{8,0},{16,8},{24,16},{32,24},{40,32},{48,40},{56,48},{1,57}... | collective-permute-start | bytes 196616 | tf_op jit(solution)/shard_map/ppermute | solution.py:378
  182.4 12.1 %all-to-all-start.9 = ((f32[8,4,8,128]{3,2,1,0:T(8,128)}), f32[8,4,8,128]{3,2,1,0:T(8,128)S(1)}, u32[]{:S(2)}, u32[]{:S(2)}) async-start(f32[8,4,8,128]{3,2,1,0:T(8,128)} %shard_map.73.u2_ref), calls=%async_computation.9 | async-start | bytes 262144 | tf_op jit(solution)/shard_map/all_to_all | solution.py:432
  189.2 7.7 %collective-permute-start.6 = (f32[16,8,128]{2,1,0:T(8,128)S(1)}, f32[16,8,128]{2,1,0:T(8,128)S(1)}, u32[]{:S(2)}, u32[]{:S(2)}) collective-permute-start(f32[16,8,128]{2,1,0:T(8,128)S(1)} %bitcast.26), channel_id=1, source_target_pairs={{0,8},{8,16},{16,24},{24,32},{32,40},{40,48},{48,56},{56,0},{1,9},... | collective-permute-start | bytes 196616 | tf_op jit(solution)/shard_map/ppermute | solution.py:377
  209.0 17.6 %all-to-all-start.11 = ((f32[64,8,128]{2,1,0:T(8,128)}), f32[64,8,128]{2,1,0:T(8,128)S(1)}, u32[]{:S(2)}, u32[]{:S(2)}) async-start(f32[64,8,128]{2,1,0:T(8,128)} %shard_map.75), calls=%async_computation.11 | async-start | bytes 524288 | tf_op jit(solution)/shard_map/all_to_all | solution.py:441

commit v2 on v1

--- a/solution.py
+++ b/solution.py
@@ -44,41 +44,74 @@
     return lax.dot_general(a, b, (dims, ((), ())), precision=HIGH, preferred_element_type=F32)
 
 
-def front_kernel(panel_ref, obs_ref, x_ref, out_ref):
+def front_kernel(panel_ref, obs_ref, x_ref, own_ref, out_ref):
     flags = obs_ref[...].astype(F32)
     x = x_ref[...]
-    row = iota((32, 128), 0)
-    col = iota((32, 128), 1) % 64
+    row = iota((32, 64), 0)
+    col = iota((32, 64), 1)
     keep = (col < 32) | (col - 32 >= row)
     diag_at = iota((64, 128), 0) == iota((64, 128), 1) % 64
-    left = iota((64, 128), 1) < 64
-    packs, diags, lanes = [], [], []
-    masked = []
+    lane = iota((8, 128), 1)
+    sub = iota((8, 128), 0)
+    packs, masked = [], []
+    extra = jnp.zeros((8, 128), F32)
     for b in range(4):
         xb = x[:, b * TILE : (b + 1) * TILE]
         gram = dot(xb, xb, ((1,), (1,)))
+        moved = jnp.concatenate([gram[0:32, 32:64], gram[0:32, 0:32]], axis=1)
+        packs.append(jnp.where(keep, gram[32:64], moved))
         twice = jnp.concatenate([gram, gram], axis=1)
-        packs.append(jnp.where(keep, twice[32:64], pltpu.roll(twice[0:32], 32, axis=1)))
-        diags.append(jnp.sum(jnp.where(diag_at, twice, 0.0), axis=0, keepdims=True))
-        flag = flags[:, b : b + 1]
-        lanes.append(jnp.where(left, flag[0:64], flag[64:128]))
-        masked.append(panel_ref[:, b * TILE : (b + 1) * TILE] * flag)
+        diag = jnp.sum(jnp.where(diag_at, twice, 0.0), axis=0, keepdims=True)
+        extra = jnp.where((sub == b) & (lane % 64 < 32), diag, extra)
+        masked.append(panel_ref[:, b * TILE : (b + 1) * TILE] * flags[:, b : b + 1])
     rhs = dot(jnp.concatenate(masked, axis=1), x, ((1,), (1,)))
-    rhs = jnp.concatenate([rhs[0:64], rhs[64:128]], axis=1)
-    diag = lanes[0] * diags[0] + lanes[1] * diags[1] + lanes[2] * diags[2] + lanes[3] * diags[3]
+    pairs = [jnp.concatenate([packs[0], packs[1]], axis=1), jnp.concatenate([packs[2], packs[3]], axis=1)]
+    for y in range(8):
+        out_ref[y, 0:32, :] = pairs[0]
+        out_ref[y, 32:64, :] = pairs[1]
+        first, second = slice(16 * y, 16 * y + 8), slice(16 * y + 8, 16 * y + 16)
+        out_ref[y, 64:72, :] = jnp.concatenate([rhs[first], rhs[second]], axis=1)
+        tail = extra
+        for b in range(4):
+            tail = jnp.where(lane // 8 == 4 + b, flags[first, b : b + 1], tail)
+            tail = jnp.where(lane // 8 == 12 + b, flags[second, b : b + 1], tail)
+        out_ref[y, 72:80, :] = tail
+        for q in range(4):
+            out_ref[y, 80 + 8 * q : 88 + 8 * q, :] = own_ref[q]
+
+
+def middle_kernel(parts_ref, out_ref, x_ref):
+    lane = iota((8, 128), 1)
     sub = iota((8, 128), 0)
-    for j in range(64):
-        total = packs[0] * lanes[0][j : j + 1]
-        for b in range(1, 4):
-            total = total + packs[b] * lanes[b][j : j + 1]
-        out_ref[j, 0:32, :] = total
-        tail = jnp.where(sub == 0, diag[j : j + 1], jnp.where(sub == 1, rhs[j : j + 1], 0.0))
-        out_ref[j, 32:40, :] = tail
+    left = lane < 64
+    wide_left = iota((32, 128), 1) < 64
+    totals = [None] * 8
+    diag = jnp.zeros((8, 128), F32)
+    rhs = jnp.zeros((8, 128), F32)
+    for y in range(8):
+        extra = parts_ref[y, 72:80, :]
+        rhs = rhs + parts_ref[y, 64:72, :]
+        for pair in range(2):
+            both = parts_ref[y, 32 * pair : 32 * pair + 32, :]
+            other = pltpu.roll(both, 64, axis=1)
+            packs = (jnp.where(wide_left, both, other), jnp.where(wide_left, other, both))
+            for half in range(2):
+                b = 2 * pair + half
+                flag = jnp.where(left, extra[:, 32 + 8 * b : 33 + 8 * b], extra[:, 96 + 8 * b : 97 + 8 * b])
+                diag = diag + flag * extra[b : b + 1]
+                for z in range(8):
+                    term = packs[half] * flag[z : z + 1]
+                    totals[z] = term if totals[z] is None else totals[z] + term
+        for q in range(4):
+            x_ref[4 * y + q] = parts_ref[y, 80 + 8 * q : 88 + 8 * q, :]
+    for z in range(8):
+        out_ref[z, 0:32, :] = totals[z]
+        out_ref[z, 32:40, :] = jnp.where(sub == 0, diag[z : z + 1], jnp.where(sub == 1, rhs[z : z + 1], 0.0))
 
 
 def solve_kernel(parts_ref, out_ref):
     total = parts_ref[0]
-    for j in range(1, 64):
+    for j in range(1, 8):
         total = total + parts_ref[j]
     pack = total[0:32]
     diag = total[32:33]
@@ -117,8 +150,11 @@
 
 
 def normal_kernel(scale, gathered_ref, panel_ref, obs_ref, factors_ref, out_ref):
-    gathered = gathered_ref[...]
-    factors = jnp.concatenate([gathered[:, 0:64], gathered[:, 64:128]], axis=0)
+    pieces = []
+    for y in range(8):
+        pair = gathered_ref[8 * y : 8 * y + 8, :]
+        pieces += [pair[:, 0:64], pair[:, 64:128]]
+    factors = jnp.concatenate(pieces, axis=0)
     factors_ref[...] = factors
     flags = obs_ref[...].astype(F32)
     for b in range(4):
@@ -174,17 +210,14 @@
     return [errors[j] - later[j] for j in range(4)]
 
 
-def start_kernel(steps_all, sums_ref, x_ref, near_ref, weight_ref, meta_ref, out_ref, h_ref, context_ref, errors_ref):
+def start_kernel(
+    steps_all, sums_ref, x_ref, plane_ref, near_ref, weight_ref, meta_ref, out_ref, h_ref, context_ref, errors_ref
+):
     slab, y = meta_ref[LAGS], meta_ref[LAGS + 1]
-    fill_context(near_ref, context_ref)
-    base = 16 + 4 * y
+    read = fill_context(plane_ref, near_ref, context_ref, y)
     total = sums_ref[0]
     for j in range(1, 8):
         total = total + sums_ref[j]
-
-    def read(j):
-        return context_ref[base + j]
-
     back = ar_part(read, slab * 512, steps_all, meta_ref, weight_ref, errors_ref)
     for q in range(4):
         h = total[:, 512 + 64 * q : 576 + 64 * q]
@@ -195,14 +228,17 @@
             out_ref[j, q] = value
 
 
-def fill_context(near_refs, context_ref):
-    middle, before, after = near_refs
+def fill_context(plane_ref, near_ref, context_ref, y):
+    lower = y < 4
+    at = jnp.where(lower, 16, 0)
+    near_at = jnp.where(lower, 0, 32)
+    near_from = jnp.where(lower, 16, 0)
+    for j in range(32):
+        context_ref[at + j] = plane_ref[j]
     for j in range(16):
-        context_ref[j] = before[j]
-        if after is not None:
-            context_ref[48 + j] = after[j]
-    for j in range(32):
-        context_ref[16 + j] = middle[j]
+        context_ref[near_at + j] = near_ref[near_from + j]
+    base = at + 4 * y
+    return lambda j: context_ref[base + j]
 
 
 def data_part(h_ref, wide_ref, q):
@@ -210,16 +246,11 @@
 
 
 def image_kernel(
-    steps_all, middle_ref, before_ref, after_ref, wide_ref, h_ref, weight_ref, theta_ref, meta_ref,
+    steps_all, plane_ref, near_ref, wide_ref, h_ref, weight_ref, theta_ref, meta_ref,
     out_ref, context_ref, errors_ref,
 ):
     slab, y = meta_ref[LAGS], meta_ref[LAGS + 1]
-    fill_context((middle_ref, before_ref, after_ref), context_ref)
-    base = 16 + 4 * y
-
-    def read(j):
-        return context_ref[base + j]
-
+    read = fill_context(plane_ref, near_ref, context_ref, y)
     back = ar_part(read, slab * 512, steps_all, meta_ref, weight_ref, errors_ref)
     theta = theta_ref[...]
     for q in range(4):
@@ -284,16 +315,11 @@
 
 
 def moment_kernel(
-    steps_all, middle_ref, before_ref, wide_ref, h_ref, weight_ref, u0_ref, u1_ref, u2_ref, meta_ref,
+    steps_all, plane_ref, near_ref, wide_ref, h_ref, weight_ref, u0_ref, u1_ref, u2_ref, meta_ref,
     out_ref, context_ref,
 ):
     slab, y = meta_ref[LAGS], meta_ref[LAGS + 1]
-    fill_context((middle_ref, before_ref, None), context_ref)
-    base = 16 + 4 * y
-
-    def read(j):
-        return context_ref[base + j]
-
+    read = fill_context(plane_ref, near_ref, context_ref, y)
     errors = residuals(read, 4, slab * 512, steps_all, meta_ref, weight_ref)
     sums = [jnp.zeros((8, 128), F32)] * 7
     for q in range(4):
@@ -367,16 +393,14 @@
             out_ref[at] = x_ref[at] + step
 
 
-def ring(length, by):
-    return [(i, (i + by) % length) for i in range(length)]
-
-
-def planes(spread, both):
-    middle = lax.all_to_all(spread, "ty", 0, 0).reshape(32, 8, 128)
-    count = lax.axis_size("tz")
-    before = lax.ppermute(middle[16:32], "tz", ring(count, 1))
-    after = lax.ppermute(middle[0:16], "tz", ring(count, -1)) if both else None
-    return middle, before, after
+def neighbour(plane):
+    pairs = [(8 * z + y, 8 * ((z + (1 if y < 4 else -1)) % 8) + y) for z in range(8) for y in range(8)]
+    return lax.ppermute(plane, TM, pairs)
+
+
+def exchange(spread):
+    plane = lax.all_to_all(spread, "ty", 0, 0).reshape(32, 8, 128)
+    return plane, neighbour(plane), lax.all_to_all(spread, "series", 0, 0)
 
 
 def per_device(panel, observed, start_time, ar_weight, lags):
@@ -391,49 +415,47 @@
     weight = jnp.broadcast_to(own_weight.T[:, :, None], (LAGS, 8, 128))
     theta = RIDGE_TIME + AR * (1.0 + jnp.sum(ar_weight * ar_weight) / 64.0)
     theta = jnp.broadcast_to(theta, (8, 128))
-    context = pltpu.VMEM((64, 8, 128), F32)
+    own_x = lax.dynamic_slice_in_dim(start_time, 8 * series, 8, 0).reshape(8, 4, 128).transpose(1, 0, 2)
+    context = pltpu.VMEM((48, 8, 128), F32)
     errors = pltpu.VMEM((20, 8, 128), F32)
 
-    own_x = lax.dynamic_slice_in_dim(start_time, 8 * series, 8, 0).reshape(8, 4, 128).transpose(1, 0, 2)
-    near_x = planes(jnp.broadcast_to(own_x[None], (8, 4, 8, 128)), True)
-
-    parts = call(front_kernel, struct(64, 40, 128), (panel, observed, start_time))
-    parts = lax.all_to_all(parts, TM, 0, 0)
+    parts = call(front_kernel, struct(8, 112, 128), (panel, observed, start_time, own_x))
+    parts = lax.all_to_all(parts, "ty", 0, 0)
+    parts, plane = call(middle_kernel, (struct(8, 40, 128), struct(32, 8, 128)), (parts,))
+    near = neighbour(plane)
+    parts = lax.all_to_all(parts, "tz", 0, 0)
     solved = call(solve_kernel, struct(64, 1, 128), (parts,))
-    gathered = lax.all_to_all(solved, TM, 0, 0).reshape(64, 128)
+    gathered = lax.all_to_all(solved, ("ty", "tz"), 0, 0).reshape(64, 128)
     factors, normal = call(
         functools.partial(normal_kernel, 1.0 / cells_all),
         (struct(cells, 64), struct(64, 768)),
         (gathered, panel, observed),
     )
     sums = lax.all_to_all(normal.reshape(8, 8, 768), "series", 0, 0)
-
-    def begin(sums, x, middle, before, after, weight, meta, out, h, ctx, err):
-        start_kernel(steps_all, sums, x, (middle, before, after), weight, meta, out, h, ctx, err)
-
     u0, h = call(
-        begin,
+        functools.partial(start_kernel, steps_all),
         (struct(8, 4, 8, 128), struct(4, 8, 64)),
-        (sums, start_time, *near_x, weight, meta),
+        (sums, start_time, plane, near, weight, meta),
         (context, errors),
     )
-    middle, before, after = planes(u0, True)
-    wide0 = lax.all_to_all(u0, "series", 0, 0)
-    image = functools.partial(image_kernel, steps_all)
-    u1 = call(
-        image, struct(8, 4, 8, 128), (middle, before, after, wide0, h, weight, theta, meta), (context, errors)
-    )
-    middle, before, after = planes(u1, True)
-    wide1 = lax.all_to_all(u1, "series", 0, 0)
-    u2 = call(
-        image, struct(8, 4, 8, 128), (middle, before, after, wide1, h, weight, theta, meta), (context, errors)
-    )
-    middle, before, _ = planes(u2, False)
-    wide2 = lax.all_to_all(u2, "series", 0, 0)
+
+    def image(plane, near, wide):
+        return call(
+            functools.partial(image_kernel, steps_all),
+            struct(8, 4, 8, 128),
+            (plane, near, wide, h, weight, theta, meta),
+            (context, errors),
+        )
+
+    plane, near, wide0 = exchange(u0)
+    u1 = image(plane, near, wide0)
+    plane, near, wide1 = exchange(u1)
+    u2 = image(plane, near, wide1)
+    plane, near, wide2 = exchange(u2)
     moments = call(
         functools.partial(moment_kernel, steps_all),
         struct(8, 8, 128),
-        (middle, before, wide2, h, weight, u0, u1, u2, meta),
+        (plane, near, wide2, h, weight, u0, u1, u2, meta),
         (context,),
     )
     moments = lax.all_to_all(moments, "series", 0, 0)

time: 230 us -> 194 us (0.84)
  blocking collectives: 42.6 us -> 101 us
  starting transfers between devices: 85.5 us -> 34.8 us
  waiting for transfers between devices: 70.9 us -> 29 us
  Pallas kernels: 22.3 us -> 19.8 us
    all_to_all x3 -> x7, blocking collectives: 33.1 us -> 92.9 us  [the longest x3 32.4 us: exchange(): plane = lax.all_to_all(spread, 'ty', 0, 0).reshape(32, 8, 128)]
    all_to_all x6 -> x2, waiting for transfers between devices: 53.6 us -> 12 us  [the longest x1 7.93 us: per_device(): gathered = lax.all_to_all(solved, ('ty', 'tz'), 0, 0).reshape(64, 128)]
    all_to_all x6 -> x2, starting transfers between devices: 49.1 us -> 10.4 us  [the longest x1 5.83 us: exchange(): return (plane, neighbour(plane), lax.all_to_all(spread, 'series', 0, 0))]
    ppermute x7 -> x4, starting transfers between devices: 22.7 us -> 9.15 us  [neighbour(): return lax.ppermute(plane, TM, pairs)]
    ppermute x7 -> x4, waiting for transfers between devices: 5.33 us -> 0.01 us  [neighbour(): return lax.ppermute(plane, TM, pairs)]
    all_to_all x1, waiting for transfers between devices: 0.01 us -> 5.08 us  [per_device(): sums = lax.all_to_all(normal.reshape(8, 8, 768), 'series', 0, 0)]
    pallas_call x9 -> x10, Pallas kernels: 22.3 us -> 19.8 us  [call(): pl.pallas_call(kernel, out_shape=outs, in_specs=specs, out_specs=jax.tree...]
  transfers between devices with their start and end apart: 15 -> 8, of which waited for: 11 -> 4; matrix products, arithmetic and copies ran while one was open for 1% -> 1% of each run, Pallas kernels for 1% -> 1%
where the time goes in v2:
time: 194 us; the launch traced here: 191 us
  blocking collectives  101 us (52%)
  starting transfers between devices  34.8 us (18%)
  waiting for transfers between devices  29 us (15%)
  Pallas kernels  19.8 us (10%)
  local copies, waits for them, and re-layouts  4.87 us (3%)
    all_to_all x3, blocking collectives, exchange(): plane = lax.all_to_all(spread, 'ty', 0, 0).reshape(32, 8, 128)  32.4 us
    all_to_all x1, blocking collectives, per_device(): parts = lax.all_to_all(parts, 'ty', 0, 0)  21.2 us
    all_to_all x2, blocking collectives, exchange(): return (plane, neighbour(plane), lax.all_to_all(spread, 'series', 0, 0))  20.2 us
    pallas_call x10, Pallas kernels, call(): pl.pallas_call(kernel, out_shape=outs, in_specs=specs, out_specs=jax.tree...  19.8 us
    all_to_all x1, blocking collectives, per_device(): parts = lax.all_to_all(parts, 'tz', 0, 0)  19.1 us
    all_to_all x1, waiting for transfers between devices, per_device(): moments = lax.all_to_all(moments, TM, 0, 0)  11.9 us
    all_to_all x1, starting transfers between devices, per_device(): sums = lax.all_to_all(normal.reshape(8, 8, 768), 'series', 0, 0)  9.44 us
    ppermute x4, starting transfers between devices, neighbour(): return lax.ppermute(plane, TM, pairs)  9.15 us
  transfers between devices with their start and end apart: 8, of which 4 were waited for; matrix products, arithmetic and copies ran while one was open for 1% of the time, Pallas kernels for 1%

profile of v2, /device:TPU:1, one launch (start us, length us, event | category | flops | bytes accessed | tf_op | source)
XLA Modules:
  0.0 191.4 jit_solution(3145768657677499743)
XLA Ops:
  1.4 0.7 dynamic-slice_bitcast_fusion.own_ref
  2.2 0.9 copy-done
  3.1 0.9 copy-done.2
  4.6 21.2 %all_to_all.60.parts_ref = f32[8,112,128]{2,1,0:T(8,128)S(1)} all-to-all(f32[8,112,128]{2,1,0:T(8,128)S(1)} %shard_map.68), channel_id=1, replica_groups=mesh['series'=8,'tz'=8,'ty'=8] {'ty'}, dimensions={0} | all-to-all | bytes 917504 | tf_op jit(solution)/shard_map/all_to_all | solution.py:423
  26.4 19.1 %all_to_all.61.parts_ref = f32[8,40,128]{2,1,0:T(8,128)S(1)} all-to-all(f32[8,40,128]{2,1,0:T(8,128)S(1)} %get-tuple-element.8), channel_id=1, replica_groups=mesh['series'=8,'tz'=8,'ty'=8] {'tz'}, dimensions={0} | all-to-all | bytes 327680 | tf_op jit(solution)/shard_map/all_to_all | solution.py:426
  45.4 9.5 %shard_map.70 = f32[64,1,128]{2,1,0:T(1,128)} custom-call(f32[8,40,128]{2,1,0:T(8,128)S(1)} %all_to_all.61.parts_ref), custom_call_target="tpu_custom_call" | custom-call | tf_op jit(solution)/shard_map/pallas_call | solution.py:33
  54.9 4.6 %all-to-all-start.2 = ((f32[64,1,128]{2,1,0:T(1,128)}), f32[64,1,128]{2,1,0:T(1,128)S(1)}, u32[]{:S(2)}, u32[]{:S(2)}) async-start(f32[64,1,128]{2,1,0:T(1,128)} %shard_map.70), calls=%async_computation.2 | async-start | bytes 65536 | tf_op jit(solution)/shard_map/all_to_all | solution.py:428
  59.5 2.8 %collective-permute-start = (f32[32,8,128]{2,1,0:T(8,128)S(1)}, f32[32,8,128]{2,1,0:T(8,128)S(1)}, u32[]{:S(2)}, u32[]{:S(2)}) collective-permute-start(f32[32,8,128]{2,1,0:T(8,128)S(1)} %get-tuple-element.11.plane_ref), channel_id=1, source_target_pairs={{0,8},{1,9},{2,10},{3,11},{4,60},{5,61},{6,62},{7,63},{8,16},{9,17... | collective-permute-start | bytes 393224 | tf_op jit(solution)/shard_map/ppermute | solution.py:398
  62.3 7.9 %all-to-all-done.2 = f32[64,1,128]{2,1,0:T(1,128)S(1)} async-done(((f32[64,1,128]{2,1,0:T(1,128)}), f32[64,1,128]{2,1,0:T(1,128)S(1)}, u32[]{:S(2)}, u32[]{:S(2)}) %all-to-all-start.2) | async-done | bytes 32800 | tf_op jit(solution)/shard_map/all_to_all | solution.py:428
  70.2 1.4 shard_map.71
  71.6 9.4 %all-to-all-start.3 = ((f32[8,8,768]{2,1,0:T(8,128)}), f32[8,8,768]{2,1,0:T(8,128)S(1)}, u32[]{:S(2)}, u32[]{:S(2)}) async-start(f32[8,8,768]{2,1,0:T(8,128)} %bitcast.3), calls=%async_computation.3 | async-start | bytes 393216 | tf_op jit(solution)/shard_map/all_to_all | solution.py:434
  81.9 5.1 %all-to-all-done.3.sums_ref = f32[8,8,768]{2,1,0:T(8,128)S(1)} async-done(((f32[8,8,768]{2,1,0:T(8,128)}), f32[8,8,768]{2,1,0:T(8,128)S(1)}, u32[]{:S(2)}, u32[]{:S(2)}) %all-to-all-start.3) | async-done | bytes 196640 | tf_op jit(solution)/shard_map/all_to_all | solution.py:434
  87.1 1.9 shard_map.72
  88.9 11.0 %all_to_all.62 = f32[8,4,8,128]{3,2,1,0:T(8,128)S(1)} all-to-all(f32[8,4,8,128]{3,2,1,0:T(8,128)} %get-tuple-element.12.u0_ref), channel_id=1, replica_groups=mesh['series'=8,'tz'=8,'ty'=8] {'ty'}, dimensions={0} | all-to-all | bytes 262144 | tf_op jit(solution)/shard_map/all_to_all | solution.py:402
  100.0 2.2 %collective-permute-start.1 = (f32[32,8,128]{2,1,0:T(8,128)S(1)}, f32[32,8,128]{2,1,0:T(8,128)S(1)}, u32[]{:S(2)}, u32[]{:S(2)}) collective-permute-start(f32[32,8,128]{2,1,0:T(8,128)S(1)} %bitcast.15), channel_id=1, source_target_pairs={{0,8},{1,9},{2,10},{3,11},{4,60},{5,61},{6,62},{7,63},{8,16},{9,17... | collective-permute-start | bytes 393224 | tf_op jit(solution)/shard_map/ppermute | solution.py:398
  102.2 5.8 %all-to-all-start.5 = ((f32[8,4,8,128]{3,2,1,0:T(8,128)}), f32[8,4,8,128]{3,2,1,0:T(8,128)S(1)}, u32[]{:S(2)}, u32[]{:S(2)}) async-start(f32[8,4,8,128]{3,2,1,0:T(8,128)} %get-tuple-element.12.u0_ref), calls=%async_computation.5 | async-start | bytes 262144 | tf_op jit(solution)/shard_map/all_to_all | solution.py:403
  109.3 4.0 %all-to-all-done.5.wide_ref.wide0_ref = f32[8,4,8,128]{3,2,1,0:T(8,128)S(1)} async-done(((f32[8,4,8,128]{3,2,1,0:T(8,128)}), f32[8,4,8,128]{3,2,1,0:T(8,128)S(1)}, u32[]{:S(2)}, u32[]{:S(2)}) %all-to-all-start.5) | async-done | bytes 131104 | tf_op jit(solution)/shard_map/all_to_all | solution.py:403
  113.3 1.2 shard_map.73.u1_ref
  114.5 10.1 %all_to_all.63 = f32[8,4,8,128]{3,2,1,0:T(8,128)S(1)} all-to-all(f32[8,4,8,128]{3,2,1,0:T(8,128)S(1)} %shard_map.73.u1_ref), channel_id=1, replica_groups=mesh['series'=8,'tz'=8,'ty'=8] {'ty'}, dimensions={0} | all-to-all | bytes 262144 | tf_op jit(solution)/shard_map/all_to_all | solution.py:402
  124.7 2.2 %collective-permute-start.2 = (f32[32,8,128]{2,1,0:T(8,128)S(1)}, f32[32,8,128]{2,1,0:T(8,128)S(1)}, u32[]{:S(2)}, u32[]{:S(2)}) collective-permute-start(f32[32,8,128]{2,1,0:T(8,128)S(1)} %bitcast.17), channel_id=1, source_target_pairs={{0,8},{1,9},{2,10},{3,11},{4,60},{5,61},{6,62},{7,63},{8,16},{9,17... | collective-permute-start | bytes 393224 | tf_op jit(solution)/shard_map/ppermute | solution.py:398
  126.9 10.2 %all_to_all.64.wide_ref.wide1_ref = f32[8,4,8,128]{3,2,1,0:T(8,128)S(1)} all-to-all(f32[8,4,8,128]{3,2,1,0:T(8,128)S(1)} %shard_map.73.u1_ref), channel_id=1, replica_groups=mesh['series'=8,'tz'=8,'ty'=8] {'series'}, dimensions={0} | all-to-all | bytes 262144 | tf_op jit(solution)/shard_map/all_to_all | solution.py:403
  137.1 1.2 shard_map.74.u2_ref
  138.3 11.2 %all_to_all.65 = f32[8,4,8,128]{3,2,1,0:T(8,128)S(1)} all-to-all(f32[8,4,8,128]{3,2,1,0:T(8,128)S(1)} %shard_map.74.u2_ref), channel_id=1, replica_groups=mesh['series'=8,'tz'=8,'ty'=8] {'ty'}, dimensions={0} | all-to-all | bytes 262144 | tf_op jit(solution)/shard_map/all_to_all | solution.py:402
  149.5 1.9 collective-permute-start.3
  151.4 10.0 %all_to_all.66.wide_ref.wide2_ref = f32[8,4,8,128]{3,2,1,0:T(8,128)S(1)} all-to-all(f32[8,4,8,128]{3,2,1,0:T(8,128)S(1)} %shard_map.74.u2_ref), channel_id=1, replica_groups=mesh['series'=8,'tz'=8,'ty'=8] {'series'}, dimensions={0} | all-to-all | bytes 262144 | tf_op jit(solution)/shard_map/all_to_all | solution.py:403
  161.5 1.7 shard_map.75
  163.2 7.9 %all_to_all.67.parts_ref = f32[8,8,128]{2,1,0:T(8,128)S(1)} all-to-all(f32[8,8,128]{2,1,0:T(8,128)S(1)} %shard_map.75), channel_id=1, replica_groups=mesh['series'=8,'tz'=8,'ty'=8] {'series'}, dimensions={0} | all-to-all | bytes 65536 | tf_op jit(solution)/shard_map/all_to_all | solution.py:461
  171.1 0.8 shard_map.76
  171.9 5.8 %all-to-all-start.11 = ((f32[64,8,128]{2,1,0:T(8,128)}), f32[64,8,128]{2,1,0:T(8,128)S(1)}, u32[]{:S(2)}, u32[]{:S(2)}) async-start(f32[64,8,128]{2,1,0:T(8,128)} %shard_map.76), calls=%async_computation.11 | async-start | bytes 524288 | tf_op jit(solution)/shard_map/all_to_all | solution.py:463
  177.7 0.7 copy.13
  178.4 11.9 %all-to-all-done.11.parts_ref = f32[64,8,128]{2,1,0:T(8,128)S(1)} async-done(((f32[64,8,128]{2,1,0:T(8,128)}), f32[64,8,128]{2,1,0:T(8,128)S(1)}, u32[]{:S(2)}, u32[]{:S(2)}) %all-to-all-start.11) | async-done | bytes 262176 | tf_op jit(solution)/shard_map/all_to_all | solution.py:463
  190.3 1.1 shard_map.77
  (24 shorter events, 3.4 us)
Async XLA Ops:
  0.6 0.7 copy-start.5
  2.2 0.9 copy-start
  3.1 0.9 copy-start.2
  26.4 43.9 %copy-start.3 = (f32[128,512]{1,0:T(8,128)S(1)}, f32[128,512]{1,0:T(8,128)}, u32[]{:S(2)}) copy-start(f32[128,512]{1,0:T(8,128)} %panel_ref.3) | copy-start | bytes 786436
  54.9 15.3 %all-to-all-start.2 = ((f32[64,1,128]{2,1,0:T(1,128)}), f32[64,1,128]{2,1,0:T(1,128)S(1)}, u32[]{:S(2)}, u32[]{:S(2)}) async-start(f32[64,1,128]{2,1,0:T(1,128)} %shard_map.70), calls=%async_computation.2 | async-start | bytes 65536 | tf_op jit(solution)/shard_map/all_to_all | solution.py:428
  59.5 22.4 %collective-permute-start = (f32[32,8,128]{2,1,0:T(8,128)S(1)}, f32[32,8,128]{2,1,0:T(8,128)S(1)}, u32[]{:S(2)}, u32[]{:S(2)}) collective-permute-start(f32[32,8,128]{2,1,0:T(8,128)S(1)} %get-tuple-element.11.plane_ref), channel_id=1, source_target_pairs={{0,8},{1,9},{2,10},{3,11},{4,60},{5,61},{6,62},{7,63},{8,16},{9,17... | collective-permute-start | bytes 393224 | tf_op jit(solution)/shard_map/ppermute | solution.py:398
  71.6 10.2 %copy-start.4 = (f32[64,14]{0,1:T(8,128)S(1)}, f32[64,14]{0,1:T(8,128)}, u32[]{:S(2)}) copy-start(f32[64,14]{0,1:T(8,128)} %param.8) | copy-start | bytes 10756
  71.6 15.4 %copy-start.1 = (f32[64,512]{1,0:T(8,128)S(1)}, f32[64,512]{1,0:T(8,128)}, u32[]{:S(2)}) copy-start(f32[64,512]{1,0:T(8,128)} %x_ref.5) | copy-start | bytes 393220
  71.6 15.3 %all-to-all-start.3 = ((f32[8,8,768]{2,1,0:T(8,128)}), f32[8,8,768]{2,1,0:T(8,128)S(1)}, u32[]{:S(2)}, u32[]{:S(2)}) async-start(f32[8,8,768]{2,1,0:T(8,128)} %bitcast.3), calls=%async_computation.3 | async-start | bytes 393216 | tf_op jit(solution)/shard_map/all_to_all | solution.py:434
  81.1 0.7 copy-start.6
  100.0 13.4 %collective-permute-start.1 = (f32[32,8,128]{2,1,0:T(8,128)S(1)}, f32[32,8,128]{2,1,0:T(8,128)S(1)}, u32[]{:S(2)}, u32[]{:S(2)}) collective-permute-start(f32[32,8,128]{2,1,0:T(8,128)S(1)} %bitcast.15), channel_id=1, source_target_pairs={{0,8},{1,9},{2,10},{3,11},{4,60},{5,61},{6,62},{7,63},{8,16},{9,17... | collective-permute-start | bytes 393224 | tf_op jit(solution)/shard_map/ppermute | solution.py:398
  102.2 11.1 %all-to-all-start.5 = ((f32[8,4,8,128]{3,2,1,0:T(8,128)}), f32[8,4,8,128]{3,2,1,0:T(8,128)S(1)}, u32[]{:S(2)}, u32[]{:S(2)}) async-start(f32[8,4,8,128]{3,2,1,0:T(8,128)} %get-tuple-element.12.u0_ref), calls=%async_computation.5 | async-start | bytes 262144 | tf_op jit(solution)/shard_map/all_to_all | solution.py:403
  124.7 12.4 %collective-permute-start.2 = (f32[32,8,128]{2,1,0:T(8,128)S(1)}, f32[32,8,128]{2,1,0:T(8,128)S(1)}, u32[]{:S(2)}, u32[]{:S(2)}) collective-permute-start(f32[32,8,128]{2,1,0:T(8,128)S(1)} %bitcast.17), channel_id=1, source_target_pairs={{0,8},{1,9},{2,10},{3,11},{4,60},{5,61},{6,62},{7,63},{8,16},{9,17... | collective-permute-start | bytes 393224 | tf_op jit(solution)/shard_map/ppermute | solution.py:398
  149.5 11.9 %collective-permute-start.3 = (f32[32,8,128]{2,1,0:T(8,128)S(1)}, f32[32,8,128]{2,1,0:T(8,128)S(1)}, u32[]{:S(2)}, u32[]{:S(2)}) collective-permute-start(f32[32,8,128]{2,1,0:T(8,128)S(1)} %bitcast.13), channel_id=1, source_target_pairs={{0,8},{1,9},{2,10},{3,11},{4,60},{5,61},{6,62},{7,63},{8,16},{9,17... | collective-permute-start | bytes 393224 | tf_op jit(solution)/shard_map/ppermute | solution.py:398
  171.9 18.4 %all-to-all-start.11 = ((f32[64,8,128]{2,1,0:T(8,128)}), f32[64,8,128]{2,1,0:T(8,128)S(1)}, u32[]{:S(2)}, u32[]{:S(2)}) async-start(f32[64,8,128]{2,1,0:T(8,128)} %shard_map.76), calls=%async_computation.11 | async-start | bytes 524288 | tf_op jit(solution)/shard_map/all_to_all | solution.py:463

commit v3 on v2

--- a/solution.py
+++ b/solution.py
@@ -17,6 +17,7 @@
 TM = ("tz", "ty")
 F32 = jnp.float32
 VMEM = pl.BlockSpec(memory_space=pltpu.VMEM)
+HBM = pl.BlockSpec(memory_space=pltpu.HBM)
 SMEM = pl.BlockSpec(memory_space=pltpu.SMEM)
 
 
@@ -28,15 +29,15 @@
     return lax.broadcasted_iota(jnp.int32, shape, dim)
 
 
-def call(kernel, outs, ins, scratch=()):
-    specs = [SMEM if a.dtype == jnp.int32 and a.ndim == 1 else VMEM for a in ins]
+def call(kernel, outs, ins, scratch=(), place=VMEM, room=32):
+    specs = [SMEM if a.dtype == jnp.int32 and a.ndim == 1 else place for a in ins]
     return pl.pallas_call(
         kernel,
         out_shape=outs,
         in_specs=specs,
         out_specs=jax.tree.map(lambda _: VMEM, outs),
         scratch_shapes=list(scratch),
-        compiler_params=pltpu.CompilerParams(vmem_limit_bytes=32 * 1024 * 1024),
+        compiler_params=pltpu.CompilerParams(vmem_limit_bytes=room * 1024 * 1024),
     )(*ins)
 
 
@@ -44,8 +45,19 @@
     return lax.dot_general(a, b, (dims, ((), ())), precision=HIGH, preferred_element_type=F32)
 
 
-def front_kernel(panel_ref, obs_ref, x_ref, own_ref, out_ref):
+def columns_of(obs_ref):
     flags = obs_ref[...].astype(F32)
+    return jnp.concatenate([flags] * 32, axis=0).T
+
+
+def front_kernel(panel_hbm, obs_hbm, x_hbm, out_ref, panel_ref, obs_ref, x_ref, sems):
+    copies = [
+        pltpu.make_async_copy(source, target, sems.at[i])
+        for i, (source, target) in enumerate(((x_hbm, x_ref), (obs_hbm, obs_ref), (panel_hbm, panel_ref)))
+    ]
+    for copy in copies:
+        copy.start()
+    copies[0].wait()
     x = x_ref[...]
     row = iota((32, 64), 0)
     col = iota((32, 64), 1)
@@ -63,8 +75,14 @@
         twice = jnp.concatenate([gram, gram], axis=1)
         diag = jnp.sum(jnp.where(diag_at, twice, 0.0), axis=0, keepdims=True)
         extra = jnp.where((sub == b) & (lane % 64 < 32), diag, extra)
+    copies[1].wait()
+    flags = columns_of(obs_ref)
+    copies[2].wait()
+    for b in range(4):
         masked.append(panel_ref[:, b * TILE : (b + 1) * TILE] * flags[:, b : b + 1])
     rhs = dot(jnp.concatenate(masked, axis=1), x, ((1,), (1,)))
+    mine = pl.ds(pl.multiple_of(8 * lax.axis_index("series"), 8), 8)
+    own = [x_ref[mine, q * TILE : (q + 1) * TILE] for q in range(4)]
     pairs = [jnp.concatenate([packs[0], packs[1]], axis=1), jnp.concatenate([packs[2], packs[3]], axis=1)]
     for y in range(8):
         out_ref[y, 0:32, :] = pairs[0]
@@ -77,7 +95,7 @@
             tail = jnp.where(lane // 8 == 12 + b, flags[second, b : b + 1], tail)
         out_ref[y, 72:80, :] = tail
         for q in range(4):
-            out_ref[y, 80 + 8 * q : 88 + 8 * q, :] = own_ref[q]
+            out_ref[y, 80 + 8 * q : 88 + 8 * q, :] = own[q]
 
 
 def middle_kernel(parts_ref, out_ref, x_ref):
@@ -138,14 +156,22 @@
     def spread(value, k):
         return jnp.where(half, value[:, k : k + 1], value[:, 64 + k : 65 + k])
 
-    for k in range(64):
-        i, r = divmod(k, 8)
-        pivot_row = jnp.broadcast_to(blocks[i][r : r + 1], (8, 128))
-        inverse = 1.0 / spread(pivot_row, k)
-        factor = jnp.where(within == k, 1.0 - inverse, pivot_row * inverse)
-        side = side - spread(side, k) * factor
-        for m in range(i if r < 7 else i + 1, 8):
-            blocks[m] = blocks[m] - spread(blocks[m], k) * factor
+    for i in range(8):
+        columns = [[spread(blocks[m], 8 * i + j) for j in range(8)] for m in range(i, 8)]
+        ends = [spread(side, 8 * i + j) for j in range(8)]
+        for r in range(8):
+            inverse = 1.0 / jnp.broadcast_to(columns[0][r][r : r + 1], (8, 128))
+            pivot_row = jnp.broadcast_to(blocks[i][r : r + 1], (8, 128))
+            factor = jnp.where(within == 8 * i + r, 1.0 - inverse, pivot_row * inverse)
+            factors = [jnp.broadcast_to(columns[0][j][r : r + 1], (8, 128)) * inverse for j in range(r + 1, 8)]
+            for m in range(i if r < 7 else i + 1, 8):
+                own = columns[m - i]
+                blocks[m] = blocks[m] - own[r] * factor
+                for j in range(r + 1, 8):
+                    own[j] = own[j] - own[r] * factors[j - r - 1]
+            side = side - ends[r] * factor
+            for j in range(r + 1, 8):
+                ends[j] = ends[j] - ends[r] * factors[j - r - 1]
     out_ref[...] = jnp.broadcast_to(side[0:1][None], out_ref.shape)
 
 
@@ -156,7 +182,7 @@
         pieces += [pair[:, 0:64], pair[:, 64:128]]
     factors = jnp.concatenate(pieces, axis=0)
     factors_ref[...] = factors
-    flags = obs_ref[...].astype(F32)
+    flags = columns_of(obs_ref)
     for b in range(4):
         flag = flags[:, b : b + 1]
         out_ref[:, b * TILE : (b + 1) * TILE] = scale * dot(
@@ -192,8 +218,8 @@
     return sums
 
 
-def residuals(read, count, first_step, steps_all, meta_ref, weight_ref):
-    past = lagged(read, count, meta_ref, weight_ref, False)
+def residuals(read, count, first_step, steps_all, lags_ref, weight_ref):
+    past = lagged(read, count, lags_ref, weight_ref, False)
     lane = iota((8, 128), 1)
     out = []
     for j in range(count):
@@ -202,23 +228,28 @@
     return out
 
 
-def ar_part(read, first_step, steps_all, meta_ref, weight_ref, errors_ref):
-    errors = residuals(read, 20, first_step, steps_all, meta_ref, weight_ref)
+def ar_part(read, first_step, steps_all, lags_ref, weight_ref, errors_ref):
+    errors = residuals(read, 20, first_step, steps_all, lags_ref, weight_ref)
     for j in range(20):
         errors_ref[j] = errors[j]
-    later = lagged(lambda j: errors_ref[j], 4, meta_ref, weight_ref, True)
+    later = lagged(lambda j: errors_ref[j], 4, lags_ref, weight_ref, True)
     return [errors[j] - later[j] for j in range(4)]
 
 
+def place():
+    y = lax.axis_index("ty")
+    return lax.axis_index("tz") * 8 + y, y
+
+
 def start_kernel(
-    steps_all, sums_ref, x_ref, plane_ref, near_ref, weight_ref, meta_ref, out_ref, h_ref, context_ref, errors_ref
+    steps_all, sums_ref, x_ref, plane_ref, near_ref, weight_ref, lags_ref, out_ref, h_ref, context_ref, errors_ref
 ):
-    slab, y = meta_ref[LAGS], meta_ref[LAGS + 1]
+    slab, y = place()
     read = fill_context(plane_ref, near_ref, context_ref, y)
     total = sums_ref[0]
     for j in range(1, 8):
         total = total + sums_ref[j]
-    back = ar_part(read, slab * 512, steps_all, meta_ref, weight_ref, errors_ref)
+    back = ar_part(read, slab * 512, steps_all, lags_ref, weight_ref, errors_ref)
     for q in range(4):
         h = total[:, 512 + 64 * q : 576 + 64 * q]
         h_ref[q] = h
@@ -246,12 +277,12 @@
 
 
 def image_kernel(
-    steps_all, plane_ref, near_ref, wide_ref, h_ref, weight_ref, theta_ref, meta_ref,
+    steps_all, plane_ref, near_ref, wide_ref, h_ref, weight_ref, theta_ref, lags_ref,
     out_ref, context_ref, errors_ref,
 ):
-    slab, y = meta_ref[LAGS], meta_ref[LAGS + 1]
+    slab, y = place()
     read = fill_context(plane_ref, near_ref, context_ref, y)
-    back = ar_part(read, slab * 512, steps_all, meta_ref, weight_ref, errors_ref)
+    back = ar_part(read, slab * 512, steps_all, lags_ref, weight_ref, errors_ref)
     theta = theta_ref[...]
     for q in range(4):
         own = read(q)
@@ -315,12 +346,12 @@
 
 
 def moment_kernel(
-    steps_all, plane_ref, near_ref, wide_ref, h_ref, weight_ref, u0_ref, u1_ref, u2_ref, meta_ref,
+    steps_all, plane_ref, near_ref, wide_ref, h_ref, weight_ref, u0_ref, u1_ref, u2_ref, lags_ref,
     out_ref, context_ref,
 ):
-    slab, y = meta_ref[LAGS], meta_ref[LAGS + 1]
+    slab, y = place()
     read = fill_context(plane_ref, near_ref, context_ref, y)
-    errors = residuals(read, 4, slab * 512, steps_all, meta_ref, weight_ref)
+    errors = residuals(read, 4, slab * 512, steps_all, lags_ref, weight_ref)
     sums = [jnp.zeros((8, 128), F32)] * 7
     for q in range(4):
         u0, u1, u2 = u0_ref[0, q], u1_ref[0, q], u2_ref[0, q]
@@ -408,24 +439,35 @@
     steps_all = 64 * 512
     cells_all = cells * 8
     series = lax.axis_index("series")
-    y = lax.axis_index("ty")
-    slab = lax.axis_index("tz") * 8 + y
-    meta = jnp.concatenate([lags, jnp.stack([slab, y]).astype(jnp.int32)])
     own_weight = lax.dynamic_slice_in_dim(ar_weight, 8 * series, 8, 0)
     weight = jnp.broadcast_to(own_weight.T[:, :, None], (LAGS, 8, 128))
     theta = RIDGE_TIME + AR * (1.0 + jnp.sum(ar_weight * ar_weight) / 64.0)
     theta = jnp.broadcast_to(theta, (8, 128))
-    own_x = lax.dynamic_slice_in_dim(start_time, 8 * series, 8, 0).reshape(8, 4, 128).transpose(1, 0, 2)
+    observed = observed.T
     context = pltpu.VMEM((48, 8, 128), F32)
     errors = pltpu.VMEM((20, 8, 128), F32)
 
-    parts = call(front_kernel, struct(8, 112, 128), (panel, observed, start_time, own_x))
+    parts = call(
+        front_kernel,
+        struct(8, 112, 128),
+        (panel, observed, start_time),
+        (
+            pltpu.VMEM(panel.shape, F32),
+            pltpu.VMEM(observed.shape, jnp.int32),
+            pltpu.VMEM(start_time.shape, F32),
+            pltpu.SemaphoreType.DMA((3,)),
+        ),
+        HBM,
+        60,
+    )
     parts = lax.all_to_all(parts, "ty", 0, 0)
     parts, plane = call(middle_kernel, (struct(8, 40, 128), struct(32, 8, 128)), (parts,))
-    near = neighbour(plane)
     parts = lax.all_to_all(parts, "tz", 0, 0)
     solved = call(solve_kernel, struct(64, 1, 128), (parts,))
+    solved, plane = lax.optimization_barrier((solved, plane))
+    near = neighbour(plane)
     gathered = lax.all_to_all(solved, ("ty", "tz"), 0, 0).reshape(64, 128)
+    gathered, near = lax.optimization_barrier((gathered, near))
     factors, normal = call(
         functools.partial(normal_kernel, 1.0 / cells_all),
         (struct(cells, 64), struct(64, 768)),
@@ -435,7 +477,7 @@
     u0, h = call(
         functools.partial(start_kernel, steps_all),
         (struct(8, 4, 8, 128), struct(4, 8, 64)),
-        (sums, start_time, plane, near, weight, meta),
+        (sums, start_time, plane, near, weight, lags),
         (context, errors),
     )
 
@@ -443,7 +485,7 @@
         return call(
             functools.partial(image_kernel, steps_all),
             struct(8, 4, 8, 128),
-            (plane, near, wide, h, weight, theta, meta),
+            (plane, near, wide, h, weight, theta, lags),
             (context, errors),
         )
 
@@ -455,7 +497,7 @@
     moments = call(
         functools.partial(moment_kernel, steps_all),
         struct(8, 8, 128),
-        (plane, near, wide2, h, weight, u0, u1, u2, meta),
+        (plane, near, wide2, h, weight, u0, u1, u2, lags),
         (context,),
     )
     moments = lax.all_to_all(moments, "series", 0, 0)

time: 194 us -> 188 us (0.969)
  blocking collectives: 101 us -> 118 us
  waiting for transfers between devices: 29 us -> 21.1 us
  starting transfers between devices: 34.8 us -> 29 us
  Pallas kernels: 19.8 us -> 14.3 us
  local copies, waits for them, and re-layouts: 4.87 us -> 1.56 us
    all_to_all x0 -> x1, blocking collectives: none -> 16.5 us  [per_device(): gathered = lax.all_to_all(solved, ('ty', 'tz'), 0, 0).reshape(64, 128)]
    all_to_all x1 -> x0, waiting for transfers between devices: 7.93 us -> none  [per_device(): gathered = lax.all_to_all(solved, ('ty', 'tz'), 0, 0).reshape(64, 128)]
    pallas_call x10, Pallas kernels: 19.8 us -> 14.3 us  [call(): pl.pallas_call(kernel, out_shape=outs, in_specs=specs, out_specs=jax.tree...]
    all_to_all x1 -> x0, starting transfers between devices: 4.59 us -> none  [per_device(): gathered = lax.all_to_all(solved, ('ty', 'tz'), 0, 0).reshape(64, 128)]
    unnamed x16 -> x11, local copies, waits for them, and re-layouts: 4.01 us -> 1.41 us
  transfers between devices with their start and end apart: 8 -> 7, of which waited for: 4 -> 3; matrix products, arithmetic and copies ran while one was open for 1% -> 1% of each run, Pallas kernels for 1% -> 0%
where the time goes in v3:
time: 188 us; the launch traced here: 186 us
  blocking collectives  118 us (63%)
  starting transfers between devices  29 us (15%)
  waiting for transfers between devices  21.1 us (11%)
  Pallas kernels  14.3 us (8%)
    all_to_all x3, blocking collectives, exchange(): plane = lax.all_to_all(spread, 'ty', 0, 0).reshape(32, 8, 128)  32.4 us
    all_to_all x1, blocking collectives, per_device(): parts = lax.all_to_all(parts, 'ty', 0, 0)  20.3 us
    all_to_all x2, blocking collectives, exchange(): return (plane, neighbour(plane), lax.all_to_all(spread, 'series', 0, 0))  20.2 us
    all_to_all x1, blocking collectives, per_device(): parts = lax.all_to_all(parts, 'tz', 0, 0)  20.2 us
    all_to_all x1, blocking collectives, per_device(): gathered = lax.all_to_all(solved, ('ty', 'tz'), 0, 0).reshape(64, 128)  16.5 us
    pallas_call x10, Pallas kernels, call(): pl.pallas_call(kernel, out_shape=outs, in_specs=specs, out_specs=jax.tree...  14.3 us
    all_to_all x1, waiting for transfers between devices, per_device(): moments = lax.all_to_all(moments, TM, 0, 0)  11.9 us
    all_to_all x1, starting transfers between devices, per_device(): sums = lax.all_to_all(normal.reshape(8, 8, 768), 'series', 0, 0)  8.96 us
  transfers between devices with their start and end apart: 7, of which 3 were waited for; matrix products, arithmetic and copies ran while one was open for 1% of the time, Pallas kernels for 0%

profile of v3, /device:TPU:1, one launch (start us, length us, event | category | flops | bytes accessed | tf_op | source)
XLA Modules:
  0.0 185.5 jit_solution(12150491535305934020)
XLA Ops:
  0.6 2.8 %shard_map.68 = f32[8,112,128]{2,1,0:T(8,128)} custom-call(f32[128,512]{1,0:T(8,128)} %panel_ref.1, s32[4,128]{1,0:T(4,128)} %bitcast.15, f32[64,512]{1,0:T(8,128)} %x_ref.3), custom_call_target="tpu_custom_call" | custom-call | tf_op jit(solution)/shard_map/pallas_call | solution.py:34
  3.4 20.3 %all_to_all.60.parts_ref = f32[8,112,128]{2,1,0:T(8,128)S(1)} all-to-all(f32[8,112,128]{2,1,0:T(8,128)} %shard_map.68), channel_id=1, replica_groups=mesh['series'=8,'tz'=8,'ty'=8] {'ty'}, dimensions={0} | all-to-all | bytes 917504 | tf_op jit(solution)/shard_map/all_to_all | solution.py:463
  23.7 0.5 shard_map.69
  24.2 20.2 %all_to_all.61.parts_ref = f32[8,40,128]{2,1,0:T(8,128)S(1)} all-to-all(f32[8,40,128]{2,1,0:T(8,128)S(1)} %get-tuple-element.12), channel_id=1, replica_groups=mesh['series'=8,'tz'=8,'ty'=8] {'tz'}, dimensions={0} | all-to-all | bytes 327680 | tf_op jit(solution)/shard_map/all_to_all | solution.py:465
  44.4 1.7 shard_map.70
  46.1 2.1 %collective-permute-start = (f32[32,8,128]{2,1,0:T(8,128)S(1)}, f32[32,8,128]{2,1,0:T(8,128)S(1)}, u32[]{:S(2)}, u32[]{:S(2)}) collective-permute-start(f32[32,8,128]{2,1,0:T(8,128)S(1)} %get-tuple-element.15.plane_ref), channel_id=1, source_target_pairs={{0,8},{1,9},{2,10},{3,11},{4,60},{5,61},{6,62},{7,63},{8,16},{9,17... | collective-permute-start | bytes 393224 | tf_op jit(solution)/shard_map/ppermute | solution.py:429
  48.3 16.5 %all_to_all.62 = f32[64,1,128]{2,1,0:T(1,128)S(1)} all-to-all(f32[64,1,128]{2,1,0:T(1,128)S(1)} %shard_map.70), channel_id=1, replica_groups=mesh['series'=8,'tz'=8,'ty'=8] {'ty','tz'}, dimensions={0} | all-to-all | bytes 65536 | tf_op jit(solution)/shard_map/all_to_all | solution.py:469
  64.7 1.5 shard_map.71
  66.2 9.0 %all-to-all-start.3 = ((f32[8,8,768]{2,1,0:T(8,128)}), f32[8,8,768]{2,1,0:T(8,128)S(1)}, u32[]{:S(2)}, u32[]{:S(2)}) async-start(f32[8,8,768]{2,1,0:T(8,128)} %bitcast.2), calls=%async_computation.3 | async-start | bytes 393216 | tf_op jit(solution)/shard_map/all_to_all | solution.py:476
  75.2 0.7 copy-done.4
  76.0 5.1 %all-to-all-done.3.sums_ref = f32[8,8,768]{2,1,0:T(8,128)S(1)} async-done(((f32[8,8,768]{2,1,0:T(8,128)}), f32[8,8,768]{2,1,0:T(8,128)S(1)}, u32[]{:S(2)}, u32[]{:S(2)}) %all-to-all-start.3) | async-done | bytes 196640 | tf_op jit(solution)/shard_map/all_to_all | solution.py:476
  81.2 1.9 %shard_map.72 = (f32[8,4,8,128]{3,2,1,0:T(8,128)}, f32[4,8,64]{2,1,0:T(8,128)S(1)}) custom-call(f32[8,8,768]{2,1,0:T(8,128)S(1)} %all-to-all-done.3.sums_ref, f32[64,512]{1,0:T(8,128)S(1)} %copy-done, f32[32,8,128]{2,1,0:T(8,128)S(1)} %get-tuple-element.15.plane_ref, f32[32,8,128]{2,1,0:T(8,128)S(1)} %collective-permute-done.near_ref, ...), custom_call_target="tpu_custom_call" | custom-call | tf_op jit(solution)/shard_map/pallas_call | solution.py:34
  83.0 11.0 %all_to_all.63 = f32[8,4,8,128]{3,2,1,0:T(8,128)S(1)} all-to-all(f32[8,4,8,128]{3,2,1,0:T(8,128)} %get-tuple-element.20.u0_ref), channel_id=1, replica_groups=mesh['series'=8,'tz'=8,'ty'=8] {'ty'}, dimensions={0} | all-to-all | bytes 262144 | tf_op jit(solution)/shard_map/all_to_all | solution.py:433
  94.1 2.2 %collective-permute-start.1 = (f32[32,8,128]{2,1,0:T(8,128)S(1)}, f32[32,8,128]{2,1,0:T(8,128)S(1)}, u32[]{:S(2)}, u32[]{:S(2)}) collective-permute-start(f32[32,8,128]{2,1,0:T(8,128)S(1)} %bitcast.10), channel_id=1, source_target_pairs={{0,8},{1,9},{2,10},{3,11},{4,60},{5,61},{6,62},{7,63},{8,16},{9,17... | collective-permute-start | bytes 393224 | tf_op jit(solution)/shard_map/ppermute | solution.py:429
  96.3 5.8 %all-to-all-start.5 = ((f32[8,4,8,128]{3,2,1,0:T(8,128)}), f32[8,4,8,128]{3,2,1,0:T(8,128)S(1)}, u32[]{:S(2)}, u32[]{:S(2)}) async-start(f32[8,4,8,128]{3,2,1,0:T(8,128)} %get-tuple-element.20.u0_ref), calls=%async_computation.5 | async-start | bytes 262144 | tf_op jit(solution)/shard_map/all_to_all | solution.py:434
  102.1 0.6 multiply_reduce_fusion
  103.4 4.0 %all-to-all-done.5.wide_ref.wide0_ref = f32[8,4,8,128]{3,2,1,0:T(8,128)S(1)} async-done(((f32[8,4,8,128]{3,2,1,0:T(8,128)}), f32[8,4,8,128]{3,2,1,0:T(8,128)S(1)}, u32[]{:S(2)}, u32[]{:S(2)}) %all-to-all-start.5) | async-done | bytes 131104 | tf_op jit(solution)/shard_map/all_to_all | solution.py:434
  107.4 1.2 shard_map.73.u1_ref
  108.6 10.1 %all_to_all.64 = f32[8,4,8,128]{3,2,1,0:T(8,128)S(1)} all-to-all(f32[8,4,8,128]{3,2,1,0:T(8,128)S(1)} %shard_map.73.u1_ref), channel_id=1, replica_groups=mesh['series'=8,'tz'=8,'ty'=8] {'ty'}, dimensions={0} | all-to-all | bytes 262144 | tf_op jit(solution)/shard_map/all_to_all | solution.py:433
  118.8 2.2 %collective-permute-start.2 = (f32[32,8,128]{2,1,0:T(8,128)S(1)}, f32[32,8,128]{2,1,0:T(8,128)S(1)}, u32[]{:S(2)}, u32[]{:S(2)}) collective-permute-start(f32[32,8,128]{2,1,0:T(8,128)S(1)} %bitcast.12), channel_id=1, source_target_pairs={{0,8},{1,9},{2,10},{3,11},{4,60},{5,61},{6,62},{7,63},{8,16},{9,17... | collective-permute-start | bytes 393224 | tf_op jit(solution)/shard_map/ppermute | solution.py:429
  121.0 10.2 %all_to_all.65.wide_ref.wide1_ref = f32[8,4,8,128]{3,2,1,0:T(8,128)S(1)} all-to-all(f32[8,4,8,128]{3,2,1,0:T(8,128)S(1)} %shard_map.73.u1_ref), channel_id=1, replica_groups=mesh['series'=8,'tz'=8,'ty'=8] {'series'}, dimensions={0} | all-to-all | bytes 262144 | tf_op jit(solution)/shard_map/all_to_all | solution.py:434
  131.2 1.2 shard_map.74.u2_ref
  132.4 11.2 %all_to_all.66 = f32[8,4,8,128]{3,2,1,0:T(8,128)S(1)} all-to-all(f32[8,4,8,128]{3,2,1,0:T(8,128)S(1)} %shard_map.74.u2_ref), channel_id=1, replica_groups=mesh['series'=8,'tz'=8,'ty'=8] {'ty'}, dimensions={0} | all-to-all | bytes 262144 | tf_op jit(solution)/shard_map/all_to_all | solution.py:433
  143.6 1.9 %collective-permute-start.3 = (f32[32,8,128]{2,1,0:T(8,128)S(1)}, f32[32,8,128]{2,1,0:T(8,128)S(1)}, u32[]{:S(2)}, u32[]{:S(2)}) collective-permute-start(f32[32,8,128]{2,1,0:T(8,128)S(1)} %bitcast.8), channel_id=1, source_target_pairs={{0,8},{1,9},{2,10},{3,11},{4,60},{5,61},{6,62},{7,63},{8,16},{9,17... | collective-permute-start | bytes 393224 | tf_op jit(solution)/shard_map/ppermute | solution.py:429
  145.6 10.0 %all_to_all.67.wide_ref.wide2_ref = f32[8,4,8,128]{3,2,1,0:T(8,128)S(1)} all-to-all(f32[8,4,8,128]{3,2,1,0:T(8,128)S(1)} %shard_map.74.u2_ref), channel_id=1, replica_groups=mesh['series'=8,'tz'=8,'ty'=8] {'series'}, dimensions={0} | all-to-all | bytes 262144 | tf_op jit(solution)/shard_map/all_to_all | solution.py:434
  155.6 1.7 shard_map.75
  157.3 7.9 %all_to_all.68.parts_ref = f32[8,8,128]{2,1,0:T(8,128)S(1)} all-to-all(f32[8,8,128]{2,1,0:T(8,128)S(1)} %shard_map.75), channel_id=1, replica_groups=mesh['series'=8,'tz'=8,'ty'=8] {'series'}, dimensions={0} | all-to-all | bytes 65536 | tf_op jit(solution)/shard_map/all_to_all | solution.py:503
  165.3 0.8 shard_map.76
  166.1 5.8 %all-to-all-start.11 = ((f32[64,8,128]{2,1,0:T(8,128)}), f32[64,8,128]{2,1,0:T(8,128)S(1)}, u32[]{:S(2)}, u32[]{:S(2)}) async-start(f32[64,8,128]{2,1,0:T(8,128)} %shard_map.76), calls=%async_computation.11 | async-start | bytes 524288 | tf_op jit(solution)/shard_map/all_to_all | solution.py:505
  171.8 0.7 copy.9
  172.5 11.9 %all-to-all-done.11.parts_ref = f32[64,8,128]{2,1,0:T(8,128)S(1)} async-done(((f32[64,8,128]{2,1,0:T(8,128)}), f32[64,8,128]{2,1,0:T(8,128)S(1)}, u32[]{:S(2)}, u32[]{:S(2)}) %all-to-all-start.11) | async-done | bytes 262176 | tf_op jit(solution)/shard_map/all_to_all | solution.py:505
  184.5 1.0 shard_map.77
  (16 shorter events, 0.2 us)
Async XLA Ops:
  24.2 40.5 %copy-start.1 = (f32[128,512]{1,0:T(8,128)S(1)}, f32[128,512]{1,0:T(8,128)}, u32[]{:S(2)}) copy-start(f32[128,512]{1,0:T(8,128)} %panel_ref.1) | copy-start | bytes 786436
  46.1 18.6 %collective-permute-start = (f32[32,8,128]{2,1,0:T(8,128)S(1)}, f32[32,8,128]{2,1,0:T(8,128)S(1)}, u32[]{:S(2)}, u32[]{:S(2)}) collective-permute-start(f32[32,8,128]{2,1,0:T(8,128)S(1)} %get-tuple-element.15.plane_ref), channel_id=1, source_target_pairs={{0,8},{1,9},{2,10},{3,11},{4,60},{5,61},{6,62},{7,63},{8,16},{9,17... | collective-permute-start | bytes 393224 | tf_op jit(solution)/shard_map/ppermute | solution.py:429
  48.2 16.5 %copy-start.2 = (s32[128,4]{0,1:T(4,128)S(1)}, s32[128,4]{0,1:T(4,128)}, u32[]{:S(2)}) copy-start(s32[128,4]{0,1:T(4,128)} %param.6) | copy-start | bytes 6148
  66.2 14.9 %copy-start = (f32[64,512]{1,0:T(8,128)S(1)}, f32[64,512]{1,0:T(8,128)}, u32[]{:S(2)}) copy-start(f32[64,512]{1,0:T(8,128)} %x_ref.3) | copy-start | bytes 393220
  66.2 14.9 %all-to-all-start.3 = ((f32[8,8,768]{2,1,0:T(8,128)}), f32[8,8,768]{2,1,0:T(8,128)S(1)}, u32[]{:S(2)}, u32[]{:S(2)}) async-start(f32[8,8,768]{2,1,0:T(8,128)} %bitcast.2), calls=%async_computation.3 | async-start | bytes 393216 | tf_op jit(solution)/shard_map/all_to_all | solution.py:476
  75.2 0.7 copy-start.4
  76.0 5.2 %copy-start.3 = (s32[14]{0:T(128)S(1)}, s32[14]{0:T(128)}, u32[]{:S(2)}) copy-start(s32[14]{0:T(128)} %lags_ref.7) | copy-start | bytes 172
  94.1 13.3 %collective-permute-start.1 = (f32[32,8,128]{2,1,0:T(8,128)S(1)}, f32[32,8,128]{2,1,0:T(8,128)S(1)}, u32[]{:S(2)}, u32[]{:S(2)}) collective-permute-start(f32[32,8,128]{2,1,0:T(8,128)S(1)} %bitcast.10), channel_id=1, source_target_pairs={{0,8},{1,9},{2,10},{3,11},{4,60},{5,61},{6,62},{7,63},{8,16},{9,17... | collective-permute-start | bytes 393224 | tf_op jit(solution)/shard_map/ppermute | solution.py:429
  96.3 11.1 %all-to-all-start.5 = ((f32[8,4,8,128]{3,2,1,0:T(8,128)}), f32[8,4,8,128]{3,2,1,0:T(8,128)S(1)}, u32[]{:S(2)}, u32[]{:S(2)}) async-start(f32[8,4,8,128]{3,2,1,0:T(8,128)} %get-tuple-element.20.u0_ref), calls=%async_computation.5 | async-start | bytes 262144 | tf_op jit(solution)/shard_map/all_to_all | solution.py:434
  118.8 12.5 %collective-permute-start.2 = (f32[32,8,128]{2,1,0:T(8,128)S(1)}, f32[32,8,128]{2,1,0:T(8,128)S(1)}, u32[]{:S(2)}, u32[]{:S(2)}) collective-permute-start(f32[32,8,128]{2,1,0:T(8,128)S(1)} %bitcast.12), channel_id=1, source_target_pairs={{0,8},{1,9},{2,10},{3,11},{4,60},{5,61},{6,62},{7,63},{8,16},{9,17... | collective-permute-start | bytes 393224 | tf_op jit(solution)/shard_map/ppermute | solution.py:429
  143.6 11.9 %collective-permute-start.3 = (f32[32,8,128]{2,1,0:T(8,128)S(1)}, f32[32,8,128]{2,1,0:T(8,128)S(1)}, u32[]{:S(2)}, u32[]{:S(2)}) collective-permute-start(f32[32,8,128]{2,1,0:T(8,128)S(1)} %bitcast.8), channel_id=1, source_target_pairs={{0,8},{1,9},{2,10},{3,11},{4,60},{5,61},{6,62},{7,63},{8,16},{9,17... | collective-permute-start | bytes 393224 | tf_op jit(solution)/shard_map/ppermute | solution.py:429
  166.1 18.4 %all-to-all-start.11 = ((f32[64,8,128]{2,1,0:T(8,128)}), f32[64,8,128]{2,1,0:T(8,128)S(1)}, u32[]{:S(2)}, u32[]{:S(2)}) async-start(f32[64,8,128]{2,1,0:T(8,128)} %shard_map.76), calls=%async_computation.11 | async-start | bytes 524288 | tf_op jit(solution)/shard_map/all_to_all | solution.py:505

commit v4 on v3

--- a/solution.py
+++ b/solution.py
@@ -242,7 +242,8 @@
 
 
 def start_kernel(
-    steps_all, sums_ref, x_ref, plane_ref, near_ref, weight_ref, lags_ref, out_ref, h_ref, context_ref, errors_ref
+    steps_all, sums_ref, x_ref, plane_ref, near_ref, weight_ref, lags_ref,
+    out_ref, own_ref, h_ref, context_ref, errors_ref,
 ):
     slab, y = place()
     read = fill_context(plane_ref, near_ref, context_ref, y)
@@ -255,6 +256,7 @@
         h_ref[q] = h
         image = dot(h, x_ref[:, q * 128 : (q + 1) * 128], ((1,), (0,))) + RIDGE_TIME * read(q) + AR * back[q]
         value = total[:, q * 128 : (q + 1) * 128] - image
+        own_ref[q] = value
         for j in range(8):
             out_ref[j, q] = value
 
@@ -278,7 +280,7 @@
 
 def image_kernel(
     steps_all, plane_ref, near_ref, wide_ref, h_ref, weight_ref, theta_ref, lags_ref,
-    out_ref, context_ref, errors_ref,
+    out_ref, own_ref, context_ref, errors_ref,
 ):
     slab, y = place()
     read = fill_context(plane_ref, near_ref, context_ref, y)
@@ -287,6 +289,7 @@
     for q in range(4):
         own = read(q)
         value = data_part(h_ref, wide_ref, q) + (RIDGE_TIME - theta) * own + AR * back[q]
+        own_ref[q] = value
         for j in range(8):
             out_ref[j, q] = value
 
@@ -345,54 +348,73 @@
     return values[0]
 
 
-def moment_kernel(
-    steps_all, plane_ref, near_ref, wide_ref, h_ref, weight_ref, u0_ref, u1_ref, u2_ref, lags_ref,
-    out_ref, context_ref,
-):
-    slab, y = place()
-    read = fill_context(plane_ref, near_ref, context_ref, y)
-    errors = residuals(read, 4, slab * 512, steps_all, lags_ref, weight_ref)
+def fold_rows(value):
+    pair = (value, jnp.zeros_like(value))
+    for by in (4, 2, 1):
+        pair = pair_add(pair, (pltpu.roll(pair[0], by, axis=0), pltpu.roll(pair[1], by, axis=0)))
+    return pair
+
+
+def product_kernel(wide_ref, h_ref, u0_ref, u1_ref, u2_ref, near_ref, out_ref):
     sums = [jnp.zeros((8, 128), F32)] * 7
     for q in range(4):
-        u0, u1, u2 = u0_ref[0, q], u1_ref[0, q], u2_ref[0, q]
+        u0, u1, u2 = u0_ref[q], u1_ref[q], u2_ref[q]
         image = data_part(h_ref, wide_ref, q) + RIDGE_TIME * u2
-        terms = [u0 * u0, u0 * u1, u0 * u2, u1 * u1, u1 * u2, u2 * u2, u2 * image + AR * (errors[q] * errors[q])]
+        terms = [u0 * u0, u0 * u1, u0 * u2, u1 * u1, u1 * u2, u2 * u2, u2 * image]
         sums = [a + b for a, b in zip(sums, terms)]
-    zero = jnp.zeros((8, 128), F32)
     sub = iota((8, 128), 0)
-    packed = (zero, zero)
+    high = low = jnp.zeros((8, 128), F32)
     for i in range(7):
-        pair = (sums[i], zero)
-        for by in (4, 2, 1):
-            pair = pair_add(pair, (pltpu.roll(pair[0], by, axis=0), pltpu.roll(pair[1], by, axis=0)))
-        packed = (jnp.where(sub == i, pair[0], packed[0]), jnp.where(sub == i, pair[1], packed[1]))
+        pair = fold_rows(sums[i])
+        high = jnp.where(sub == i, pair[0], high)
+        low = jnp.where(sub == i, pair[1], low)
+    for y in range(8):
+        for q in range(4):
+            out_ref[y, q] = u2_ref[q]
+            out_ref[y, 4 + q] = near_ref[q]
+        out_ref[y, 8] = high
+        out_ref[y, 9] = low
+
+
+def moment_kernel(steps_all, parts_ref, weight_ref, lags_ref, out_ref, context_ref):
+    for y in range(8):
+        for q in range(4):
+            context_ref[16 + 4 * y + q] = parts_ref[y, q]
+            if y >= 4:
+                context_ref[4 * (y - 4) + q] = parts_ref[y, 4 + q]
+    first = lax.axis_index("tz") * 4096
+    square = jnp.zeros((8, 128), F32)
+    for part in range(2):
+        errors = residuals(
+            lambda j: context_ref[16 + 16 * part + j], 16, first + 2048 * part, steps_all, lags_ref, weight_ref
+        )
+        for error in errors:
+            square = square + error * error
+    pair = fold_rows(AR * square)
+    last = iota((8, 128), 0) == 6
+    packed = pair_tree([(parts_ref[y, 8], parts_ref[y, 9]) for y in range(8)])
+    packed = pair_add(packed, (jnp.where(last, pair[0], 0.0), jnp.where(last, pair[1], 0.0)))
     for by in (64, 32, 16, 8, 4, 2, 1):
         packed = pair_add(packed, (pltpu.roll(packed[0], by, axis=1), pltpu.roll(packed[1], by, axis=1)))
-    value = jnp.where(iota((8, 128), 1) < 64, packed[0], packed[1])
+    lane = iota((8, 128), 1)
+    value = jnp.where(lane < 64, packed[0], packed[1])
+    value = jnp.sum(jnp.where(iota((8, 128), 0) == lane % 64 // 8, value, 0.0), axis=0, keepdims=True)
     out_ref[...] = jnp.broadcast_to(value[None], out_ref.shape)
 
 
-def sum_pairs(parts_ref, count):
+def finish_kernel(parts_ref, theta_ref, x_ref, wide0_ref, wide1_ref, wide2_ref, out_ref):
     half = iota((8, 128), 1) < 64
     pairs = []
-    for j in range(count):
-        part = parts_ref[j]
+    for j in range(8):
+        part = parts_ref[8 * j : 8 * j + 8, :]
         other = pltpu.roll(part, 64, axis=1)
         pairs.append((jnp.where(half, part, other), jnp.where(half, other, part)))
-    return pair_tree(pairs)
-
-
-def join_kernel(parts_ref, out_ref):
-    high, low = sum_pairs(parts_ref, 8)
-    value = jnp.where(iota((8, 128), 1) < 64, high, low)
-    out_ref[...] = jnp.broadcast_to(value[None], out_ref.shape)
-
-
-def finish_kernel(parts_ref, theta_ref, x_ref, wide0_ref, wide1_ref, wide2_ref, out_ref):
-    high, low = sum_pairs(parts_ref, 64)
+    total = pair_tree(pairs)
+    for by in (4, 2, 1):
+        total = pair_add(total, (pltpu.roll(total[0], by, axis=0), pltpu.roll(total[1], by, axis=0)))
 
     def moment(i):
-        return tuple(jnp.broadcast_to(a[i : i + 1], (8, 128)) for a in (high, low))
+        return tuple(jnp.broadcast_to(a[:, 8 * i : 8 * i + 1], (8, 128)) for a in total)
 
     g00, g01, g02, g11, g12, g22, m22 = [moment(i) for i in range(7)]
     theta = (theta_ref[...], jnp.zeros((8, 128), F32))
@@ -474,9 +496,9 @@
         (gathered, panel, observed),
     )
     sums = lax.all_to_all(normal.reshape(8, 8, 768), "series", 0, 0)
-    u0, h = call(
+    u0, own0, h = call(
         functools.partial(start_kernel, steps_all),
-        (struct(8, 4, 8, 128), struct(4, 8, 64)),
+        (struct(8, 4, 8, 128), struct(4, 8, 128), struct(4, 8, 64)),
         (sums, start_time, plane, near, weight, lags),
         (context, errors),
     )
@@ -484,25 +506,23 @@
     def image(plane, near, wide):
         return call(
             functools.partial(image_kernel, steps_all),
-            struct(8, 4, 8, 128),
+            (struct(8, 4, 8, 128), struct(4, 8, 128)),
             (plane, near, wide, h, weight, theta, lags),
             (context, errors),
         )
 
     plane, near, wide0 = exchange(u0)
-    u1 = image(plane, near, wide0)
+    u1, own1 = image(plane, near, wide0)
     plane, near, wide1 = exchange(u1)
-    u2 = image(plane, near, wide1)
-    plane, near, wide2 = exchange(u2)
+    u2, own2 = image(plane, near, wide1)
+    near = lax.ppermute(own2, "tz", [(z, (z + 1) % 8) for z in range(8)])
+    wide2 = lax.all_to_all(u2, "series", 0, 0)
+    parts = call(product_kernel, struct(8, 10, 8, 128), (wide2, h, own0, own1, own2, near))
+    parts = lax.all_to_all(parts, "ty", 0, 0)
     moments = call(
-        functools.partial(moment_kernel, steps_all),
-        struct(8, 8, 128),
-        (plane, near, wide2, h, weight, u0, u1, u2, lags),
-        (context,),
+        functools.partial(moment_kernel, steps_all), struct(64, 1, 128), (parts, weight, lags), (context,)
     )
-    moments = lax.all_to_all(moments, "series", 0, 0)
-    moments = call(join_kernel, struct(64, 8, 128), (moments,))
-    moments = lax.all_to_all(moments, TM, 0, 0)
+    moments = lax.all_to_all(moments, ("series", "tz"), 0, 0).reshape(64, 128)
     result = call(finish_kernel, struct(64, 512), (moments, theta, start_time, wide0, wide1, wide2))
     return (factors, result)
 

time: 188 us -> 180 us (0.957)
  blocking collectives: 118 us -> 103 us
  starting transfers between devices: 29 us -> 36.6 us
    all_to_all x1 -> x2, blocking collectives: 20.3 us -> 34.7 us  [per_device(): parts = lax.all_to_all(parts, 'ty', 0, 0)]
    all_to_all x3 -> x2, blocking collectives: 32.4 us -> 21.2 us  [exchange(): plane = lax.all_to_all(spread, 'ty', 0, 0).reshape(32, 8, 128)]
    all_to_all x2 -> x1, blocking collectives: 20.2 us -> 10.2 us  [exchange(): return (plane, neighbour(plane), lax.all_to_all(spread, 'series', 0, 0))]
    all_to_all x1 -> x0, blocking collectives: 7.94 us -> none  [per_device(): moments = lax.all_to_all(moments, 'series', 0, 0)]
    all_to_all x1 -> x2, starting transfers between devices: 5.75 us -> 13 us  [the longest x1 8.91 us: per_device(): moments = lax.all_to_all(moments, ('series', 'tz'), 0, 0).reshape(64, 128)]
    ppermute x0 -> x1, waiting for transfers between devices: none -> 3.53 us  [per_device(): near = lax.ppermute(own2, 'tz', [(z, (z + 1) % 8) for z in range(8)])]
    all_to_all x1 -> x2, waiting for transfers between devices: 11.9 us -> 8.43 us  [the longest x1 8.43 us: per_device(): moments = lax.all_to_all(moments, ('series', 'tz'), 0, 0).reshape(64, 128)]
    ppermute x0 -> x1, starting transfers between devices: none -> 2.22 us  [per_device(): near = lax.ppermute(own2, 'tz', [(z, (z + 1) % 8) for z in range(8)])]
  transfers between devices with their start and end apart: 7 -> 8, of which waited for: 3 -> 4; matrix products, arithmetic and copies ran while one was open for 1% -> 1% of each run, Pallas kernels for 0% -> 0%
where the time goes in v4:
time: 180 us; the launch traced here: 179 us
  blocking collectives  103 us (57%)
  starting transfers between devices  36.6 us (20%)
  waiting for transfers between devices  21.1 us (12%)
  Pallas kernels  15 us (8%)
    all_to_all x2, blocking collectives, per_device(): parts = lax.all_to_all(parts, 'ty', 0, 0)  34.7 us
    all_to_all x2, blocking collectives, exchange(): plane = lax.all_to_all(spread, 'ty', 0, 0).reshape(32, 8, 128)  21.2 us
    all_to_all x1, blocking collectives, per_device(): parts = lax.all_to_all(parts, 'tz', 0, 0)  20.2 us
    all_to_all x1, blocking collectives, per_device(): gathered = lax.all_to_all(solved, ('ty', 'tz'), 0, 0).reshape(64, 128)  16.5 us
    pallas_call x10, Pallas kernels, call(): pl.pallas_call(kernel, out_shape=outs, in_specs=specs, out_specs=jax.tree...  15 us
    all_to_all x1, blocking collectives, exchange(): return (plane, neighbour(plane), lax.all_to_all(spread, 'series', 0, 0))  10.2 us
    all_to_all x1, starting transfers between devices, per_device(): sums = lax.all_to_all(normal.reshape(8, 8, 768), 'series', 0, 0)  8.97 us
    all_to_all x1, starting transfers between devices, per_device(): moments = lax.all_to_all(moments, ('series', 'tz'), 0, 0).reshape(64, 128)  8.91 us
  transfers between devices with their start and end apart: 8, of which 4 were waited for; matrix products, arithmetic and copies ran while one was open for 1% of the time, Pallas kernels for 0%

profile of v4, /device:TPU:1, one launch (start us, length us, event | category | flops | bytes accessed | tf_op | source)
XLA Modules:
  0.0 179.0 jit_solution(16064215827665526439)
XLA Ops:
  0.6 2.8 %shard_map.68 = f32[8,112,128]{2,1,0:T(8,128)} custom-call(f32[128,512]{1,0:T(8,128)} %panel_ref.1, s32[4,128]{1,0:T(4,128)} %bitcast.14, f32[64,512]{1,0:T(8,128)} %x_ref.3), custom_call_target="tpu_custom_call" | custom-call | tf_op jit(solution)/shard_map/pallas_call | solution.py:34
  3.4 20.3 %all_to_all.55.parts_ref = f32[8,112,128]{2,1,0:T(8,128)S(1)} all-to-all(f32[8,112,128]{2,1,0:T(8,128)} %shard_map.68), channel_id=1, replica_groups=mesh['series'=8,'tz'=8,'ty'=8] {'ty'}, dimensions={0} | all-to-all | bytes 917504 | tf_op jit(solution)/shard_map/all_to_all | solution.py:485
  23.7 0.5 shard_map.69
  24.2 20.2 %all_to_all.56.parts_ref = f32[8,40,128]{2,1,0:T(8,128)S(1)} all-to-all(f32[8,40,128]{2,1,0:T(8,128)S(1)} %get-tuple-element.17), channel_id=1, replica_groups=mesh['series'=8,'tz'=8,'ty'=8] {'tz'}, dimensions={0} | all-to-all | bytes 327680 | tf_op jit(solution)/shard_map/all_to_all | solution.py:487
  44.4 1.7 shard_map.70
  46.2 2.1 %collective-permute-start = (f32[32,8,128]{2,1,0:T(8,128)S(1)}, f32[32,8,128]{2,1,0:T(8,128)S(1)}, u32[]{:S(2)}, u32[]{:S(2)}) collective-permute-start(f32[32,8,128]{2,1,0:T(8,128)S(1)} %get-tuple-element.20.plane_ref), channel_id=1, source_target_pairs={{0,8},{1,9},{2,10},{3,11},{4,60},{5,61},{6,62},{7,63},{8,16},{9,17... | collective-permute-start | bytes 393224 | tf_op jit(solution)/shard_map/ppermute | solution.py:451
  48.3 16.5 %all_to_all.57 = f32[64,1,128]{2,1,0:T(1,128)S(1)} all-to-all(f32[64,1,128]{2,1,0:T(1,128)S(1)} %shard_map.70), channel_id=1, replica_groups=mesh['series'=8,'tz'=8,'ty'=8] {'ty','tz'}, dimensions={0} | all-to-all | bytes 65536 | tf_op jit(solution)/shard_map/all_to_all | solution.py:491
  64.7 1.5 shard_map.71
  66.2 9.0 %all-to-all-start.3 = ((f32[8,8,768]{2,1,0:T(8,128)}), f32[8,8,768]{2,1,0:T(8,128)S(1)}, u32[]{:S(2)}, u32[]{:S(2)}) async-start(f32[8,8,768]{2,1,0:T(8,128)} %bitcast.2), calls=%async_computation.3 | async-start | bytes 393216 | tf_op jit(solution)/shard_map/all_to_all | solution.py:498
  75.2 0.7 copy-done.4
  76.0 5.1 %all-to-all-done.3.sums_ref = f32[8,8,768]{2,1,0:T(8,128)S(1)} async-done(((f32[8,8,768]{2,1,0:T(8,128)}), f32[8,8,768]{2,1,0:T(8,128)S(1)}, u32[]{:S(2)}, u32[]{:S(2)}) %all-to-all-start.3) | async-done | bytes 196640 | tf_op jit(solution)/shard_map/all_to_all | solution.py:498
  81.2 1.9 %shard_map.72 = (f32[8,4,8,128]{3,2,1,0:T(8,128)}, f32[4,8,128]{2,1,0:T(8,128)S(1)}, f32[4,8,64]{2,1,0:T(8,128)S(1)}) custom-call(f32[8,8,768]{2,1,0:T(8,128)S(1)} %all-to-all-done.3.sums_ref, f32[64,512]{1,0:T(8,128)S(1)} %copy-done, f32[32,8,128]{2,1,0:T(8,128)S(1)} %get-tuple-element.20.plane_ref, f32[32,8,128]{2,1,0:T(8,128)S(1)} %collective-permute-done.near_ref, ...), custom_call_target="tpu_custom_call" | custom-call | tf_op jit(solution)/shard_map/pallas_call | solution.py:34
  83.0 11.0 %all_to_all.58 = f32[8,4,8,128]{3,2,1,0:T(8,128)S(1)} all-to-all(f32[8,4,8,128]{3,2,1,0:T(8,128)} %get-tuple-element.25), channel_id=1, replica_groups=mesh['series'=8,'tz'=8,'ty'=8] {'ty'}, dimensions={0} | all-to-all | bytes 262144 | tf_op jit(solution)/shard_map/all_to_all | solution.py:455
  94.1 2.2 %collective-permute-start.1 = (f32[32,8,128]{2,1,0:T(8,128)S(1)}, f32[32,8,128]{2,1,0:T(8,128)S(1)}, u32[]{:S(2)}, u32[]{:S(2)}) collective-permute-start(f32[32,8,128]{2,1,0:T(8,128)S(1)} %bitcast.8), channel_id=1, source_target_pairs={{0,8},{1,9},{2,10},{3,11},{4,60},{5,61},{6,62},{7,63},{8,16},{9,17... | collective-permute-start | bytes 393224 | tf_op jit(solution)/shard_map/ppermute | solution.py:451
  96.3 5.8 %all-to-all-start.5 = ((f32[8,4,8,128]{3,2,1,0:T(8,128)}), f32[8,4,8,128]{3,2,1,0:T(8,128)S(1)}, u32[]{:S(2)}, u32[]{:S(2)}) async-start(f32[8,4,8,128]{3,2,1,0:T(8,128)} %get-tuple-element.25), calls=%async_computation.5 | async-start | bytes 262144 | tf_op jit(solution)/shard_map/all_to_all | solution.py:456
  102.1 0.6 multiply_reduce_fusion
  103.4 4.0 %all-to-all-done.5.wide_ref.wide0_ref = f32[8,4,8,128]{3,2,1,0:T(8,128)S(1)} async-done(((f32[8,4,8,128]{3,2,1,0:T(8,128)}), f32[8,4,8,128]{3,2,1,0:T(8,128)S(1)}, u32[]{:S(2)}, u32[]{:S(2)}) %all-to-all-start.5) | async-done | bytes 131104 | tf_op jit(solution)/shard_map/all_to_all | solution.py:456
  107.4 1.2 shard_map.73
  108.6 10.1 %all_to_all.59 = f32[8,4,8,128]{3,2,1,0:T(8,128)S(1)} all-to-all(f32[8,4,8,128]{3,2,1,0:T(8,128)S(1)} %get-tuple-element.27), channel_id=1, replica_groups=mesh['series'=8,'tz'=8,'ty'=8] {'ty'}, dimensions={0} | all-to-all | bytes 262144 | tf_op jit(solution)/shard_map/all_to_all | solution.py:455
  118.8 2.2 %collective-permute-start.2 = (f32[32,8,128]{2,1,0:T(8,128)S(1)}, f32[32,8,128]{2,1,0:T(8,128)S(1)}, u32[]{:S(2)}, u32[]{:S(2)}) collective-permute-start(f32[32,8,128]{2,1,0:T(8,128)S(1)} %bitcast.10), channel_id=1, source_target_pairs={{0,8},{1,9},{2,10},{3,11},{4,60},{5,61},{6,62},{7,63},{8,16},{9,17... | collective-permute-start | bytes 393224 | tf_op jit(solution)/shard_map/ppermute | solution.py:451
  121.0 10.2 %all_to_all.60.wide_ref.wide1_ref = f32[8,4,8,128]{3,2,1,0:T(8,128)S(1)} all-to-all(f32[8,4,8,128]{3,2,1,0:T(8,128)S(1)} %get-tuple-element.27), channel_id=1, replica_groups=mesh['series'=8,'tz'=8,'ty'=8] {'series'}, dimensions={0} | all-to-all | bytes 262144 | tf_op jit(solution)/shard_map/all_to_all | solution.py:456
  131.2 1.9 %shard_map.74 = (f32[8,4,8,128]{3,2,1,0:T(8,128)}, f32[4,8,128]{2,1,0:T(8,128)S(1)}) custom-call(f32[32,8,128]{2,1,0:T(8,128)S(1)} %bitcast.11, f32[32,8,128]{2,1,0:T(8,128)S(1)} %collective-permute-done.2.near_ref, f32[8,4,8,128]{3,2,1,0:T(8,128)S(1)} %all_to_all.60.wide_ref.wide1_ref, f32[4,8,64]{2,1,0:T(8,128)S(1)} %get-tuple-element.26.h_ref, ...), custom_call_target="tpu_custom_call" | custom-call | tf_op jit(solution)/shard_map/pallas_call | solution.py:34
  133.1 4.1 %all-to-all-start.8 = ((f32[8,4,8,128]{3,2,1,0:T(8,128)}), f32[8,4,8,128]{3,2,1,0:T(8,128)S(1)}, u32[]{:S(2)}, u32[]{:S(2)}) async-start(f32[8,4,8,128]{3,2,1,0:T(8,128)} %get-tuple-element.28), calls=%async_computation.8 | async-start | bytes 262144 | tf_op jit(solution)/shard_map/all_to_all | solution.py:519
  137.2 2.2 %collective-permute-start.3 = (f32[4,8,128]{2,1,0:T(8,128)S(1)}, f32[4,8,128]{2,1,0:T(8,128)S(1)}, u32[]{:S(2)}, u32[]{:S(2)}) collective-permute-start(f32[4,8,128]{2,1,0:T(8,128)S(1)} %get-tuple-element.31.u2_ref), channel_id=1, source_target_pairs={{0,8},{8,16},{16,24},{24,32},{32,40},{40,48},{48,56},{56,0},{1,9},... | collective-permute-start | bytes 49160 | tf_op jit(solution)/shard_map/ppermute | solution.py:518
  139.4 3.5 %collective-permute-done.3.near_ref = f32[4,8,128]{2,1,0:T(8,128)S(1)} collective-permute-done((f32[4,8,128]{2,1,0:T(8,128)S(1)}, f32[4,8,128]{2,1,0:T(8,128)S(1)}, u32[]{:S(2)}, u32[]{:S(2)}) %collective-permute-start.3) | collective-permute-done | bytes 16416 | tf_op jit(solution)/shard_map/ppermute | solution.py:518
  143.0 0.3 shard_map.75
  143.2 14.4 %all_to_all.61.parts_ref = f32[8,10,8,128]{3,2,1,0:T(8,128)S(1)} all-to-all(f32[8,10,8,128]{3,2,1,0:T(8,128)S(1)} %shard_map.75), channel_id=1, replica_groups=mesh['series'=8,'tz'=8,'ty'=8] {'ty'}, dimensions={0} | all-to-all | bytes 655360 | tf_op jit(solution)/shard_map/all_to_all | solution.py:521
  157.6 2.4 %shard_map.76 = f32[64,1,128]{2,1,0:T(1,128)} custom-call(f32[8,10,8,128]{3,2,1,0:T(8,128)S(1)} %all_to_all.61.parts_ref, f32[14,8,128]{2,1,0:T(8,128)S(1)} %broadcast_in_dim.4.weight_ref, s32[14]{0:T(128)S(1)} %copy-done.3), custom_call_target="tpu_custom_call" | custom-call | tf_op jit(solution)/shard_map/pallas_call | solution.py:34
  160.0 8.9 %all-to-all-start.10 = ((f32[64,1,128]{2,1,0:T(1,128)}), f32[64,1,128]{2,1,0:T(1,128)S(1)}, u32[]{:S(2)}, u32[]{:S(2)}) async-start(f32[64,1,128]{2,1,0:T(1,128)} %shard_map.76), calls=%async_computation.10 | async-start | bytes 65536 | tf_op jit(solution)/shard_map/all_to_all | solution.py:525
  168.9 0.7 copy.10
  169.6 8.4 %all-to-all-done.10 = f32[64,1,128]{2,1,0:T(1,128)S(1)} async-done(((f32[64,1,128]{2,1,0:T(1,128)}), f32[64,1,128]{2,1,0:T(1,128)S(1)}, u32[]{:S(2)}, u32[]{:S(2)}) %all-to-all-start.10) | async-done | bytes 32800 | tf_op jit(solution)/shard_map/all_to_all | solution.py:525
  178.0 1.0 shard_map.77
  (16 shorter events, 0.2 us)
Async XLA Ops:
  24.2 40.5 %copy-start.1 = (f32[128,512]{1,0:T(8,128)S(1)}, f32[128,512]{1,0:T(8,128)}, u32[]{:S(2)}) copy-start(f32[128,512]{1,0:T(8,128)} %panel_ref.1) | copy-start | bytes 786436
  46.2 18.6 %collective-permute-start = (f32[32,8,128]{2,1,0:T(8,128)S(1)}, f32[32,8,128]{2,1,0:T(8,128)S(1)}, u32[]{:S(2)}, u32[]{:S(2)}) collective-permute-start(f32[32,8,128]{2,1,0:T(8,128)S(1)} %get-tuple-element.20.plane_ref), channel_id=1, source_target_pairs={{0,8},{1,9},{2,10},{3,11},{4,60},{5,61},{6,62},{7,63},{8,16},{9,17... | collective-permute-start | bytes 393224 | tf_op jit(solution)/shard_map/ppermute | solution.py:451
  48.3 16.5 %copy-start.2 = (s32[128,4]{0,1:T(4,128)S(1)}, s32[128,4]{0,1:T(4,128)}, u32[]{:S(2)}) copy-start(s32[128,4]{0,1:T(4,128)} %param.6) | copy-start | bytes 6148
  66.2 14.9 %copy-start = (f32[64,512]{1,0:T(8,128)S(1)}, f32[64,512]{1,0:T(8,128)}, u32[]{:S(2)}) copy-start(f32[64,512]{1,0:T(8,128)} %x_ref.3) | copy-start | bytes 393220
  66.2 14.9 %all-to-all-start.3 = ((f32[8,8,768]{2,1,0:T(8,128)}), f32[8,8,768]{2,1,0:T(8,128)S(1)}, u32[]{:S(2)}, u32[]{:S(2)}) async-start(f32[8,8,768]{2,1,0:T(8,128)} %bitcast.2), calls=%async_computation.3 | async-start | bytes 393216 | tf_op jit(solution)/shard_map/all_to_all | solution.py:498
  75.2 0.7 copy-start.4
  76.0 5.2 %copy-start.3 = (s32[14]{0:T(128)S(1)}, s32[14]{0:T(128)}, u32[]{:S(2)}) copy-start(s32[14]{0:T(128)} %lags_ref.7) | copy-start | bytes 172
  94.1 13.3 %collective-permute-start.1 = (f32[32,8,128]{2,1,0:T(8,128)S(1)}, f32[32,8,128]{2,1,0:T(8,128)S(1)}, u32[]{:S(2)}, u32[]{:S(2)}) collective-permute-start(f32[32,8,128]{2,1,0:T(8,128)S(1)} %bitcast.8), channel_id=1, source_target_pairs={{0,8},{1,9},{2,10},{3,11},{4,60},{5,61},{6,62},{7,63},{8,16},{9,17... | collective-permute-start | bytes 393224 | tf_op jit(solution)/shard_map/ppermute | solution.py:451
  96.3 11.1 %all-to-all-start.5 = ((f32[8,4,8,128]{3,2,1,0:T(8,128)}), f32[8,4,8,128]{3,2,1,0:T(8,128)S(1)}, u32[]{:S(2)}, u32[]{:S(2)}) async-start(f32[8,4,8,128]{3,2,1,0:T(8,128)} %get-tuple-element.25), calls=%async_computation.5 | async-start | bytes 262144 | tf_op jit(solution)/shard_map/all_to_all | solution.py:456
  118.8 12.4 %collective-permute-start.2 = (f32[32,8,128]{2,1,0:T(8,128)S(1)}, f32[32,8,128]{2,1,0:T(8,128)S(1)}, u32[]{:S(2)}, u32[]{:S(2)}) collective-permute-start(f32[32,8,128]{2,1,0:T(8,128)S(1)} %bitcast.10), channel_id=1, source_target_pairs={{0,8},{1,9},{2,10},{3,11},{4,60},{5,61},{6,62},{7,63},{8,16},{9,17... | collective-permute-start | bytes 393224 | tf_op jit(solution)/shard_map/ppermute | solution.py:451
  133.1 9.9 %all-to-all-start.8 = ((f32[8,4,8,128]{3,2,1,0:T(8,128)}), f32[8,4,8,128]{3,2,1,0:T(8,128)S(1)}, u32[]{:S(2)}, u32[]{:S(2)}) async-start(f32[8,4,8,128]{3,2,1,0:T(8,128)} %get-tuple-element.28), calls=%async_computation.8 | async-start | bytes 262144 | tf_op jit(solution)/shard_map/all_to_all | solution.py:519
  137.2 5.8 %collective-permute-start.3 = (f32[4,8,128]{2,1,0:T(8,128)S(1)}, f32[4,8,128]{2,1,0:T(8,128)S(1)}, u32[]{:S(2)}, u32[]{:S(2)}) collective-permute-start(f32[4,8,128]{2,1,0:T(8,128)S(1)} %get-tuple-element.31.u2_ref), channel_id=1, source_target_pairs={{0,8},{8,16},{16,24},{24,32},{32,40},{40,48},{48,56},{56,0},{1,9},... | collective-permute-start | bytes 49160 | tf_op jit(solution)/shard_map/ppermute | solution.py:518
  160.0 18.0 %all-to-all-start.10 = ((f32[64,1,128]{2,1,0:T(1,128)}), f32[64,1,128]{2,1,0:T(1,128)S(1)}, u32[]{:S(2)}, u32[]{:S(2)}) async-start(f32[64,1,128]{2,1,0:T(1,128)} %shard_map.76), calls=%async_computation.10 | async-start | bytes 65536 | tf_op jit(solution)/shard_map/all_to_all | solution.py:525

commit v5 on v4

--- a/solution.py
+++ b/solution.py
@@ -183,14 +183,10 @@
     factors = jnp.concatenate(pieces, axis=0)
     factors_ref[...] = factors
     flags = columns_of(obs_ref)
-    for b in range(4):
-        flag = flags[:, b : b + 1]
-        out_ref[:, b * TILE : (b + 1) * TILE] = scale * dot(
-            factors, panel_ref[:, b * TILE : (b + 1) * TILE] * flag, ((0,), (0,))
-        )
-    for pair in range(2):
-        halves = [dot(factors * flags[:, b : b + 1], factors, ((0,), (0,))) for b in (2 * pair, 2 * pair + 1)]
-        out_ref[:, 512 + 128 * pair : 640 + 128 * pair] = scale * jnp.concatenate(halves, axis=1)
+    right = [panel_ref[:, b * TILE : (b + 1) * TILE] * flags[:, b : b + 1] for b in range(4)]
+    for b in (0, 2):
+        right.append(jnp.concatenate([factors * flags[:, b : b + 1], factors * flags[:, b + 1 : b + 2]], axis=1))
+    out_ref[...] = scale * dot(factors, jnp.concatenate(right, axis=1), ((0,), (0,)))
 
 
 def lagged(read, count, lags_ref, weight_ref, ahead):
@@ -241,20 +237,26 @@
     return lax.axis_index("tz") * 8 + y, y
 
 
-def start_kernel(
-    steps_all, sums_ref, x_ref, plane_ref, near_ref, weight_ref, lags_ref,
-    out_ref, own_ref, h_ref, context_ref, errors_ref,
+def drift_kernel(
+    steps_all, plane_ref, near_ref, weight_ref, all_ref, lags_ref, out_ref, theta_ref, context_ref, errors_ref
 ):
     slab, y = place()
     read = fill_context(plane_ref, near_ref, context_ref, y)
+    back = ar_part(read, slab * 512, steps_all, lags_ref, weight_ref, errors_ref)
+    for q in range(4):
+        out_ref[q] = RIDGE_TIME * read(q) + AR * back[q]
+    squares = all_ref[...] * all_ref[...]
+    theta_ref[...] = jnp.full((8, 128), RIDGE_TIME + AR) + (AR / 64.0) * jnp.sum(squares)
+
+
+def start_kernel(sums_ref, x_ref, drift_ref, out_ref, own_ref, h_ref):
     total = sums_ref[0]
     for j in range(1, 8):
         total = total + sums_ref[j]
-    back = ar_part(read, slab * 512, steps_all, lags_ref, weight_ref, errors_ref)
     for q in range(4):
         h = total[:, 512 + 64 * q : 576 + 64 * q]
         h_ref[q] = h
-        image = dot(h, x_ref[:, q * 128 : (q + 1) * 128], ((1,), (0,))) + RIDGE_TIME * read(q) + AR * back[q]
+        image = dot(h, x_ref[:, q * 128 : (q + 1) * 128], ((1,), (0,))) + drift_ref[q]
         value = total[:, q * 128 : (q + 1) * 128] - image
         own_ref[q] = value
         for j in range(8):
@@ -346,6 +348,15 @@
             for i in range(0, len(values), 2)
         ]
     return values[0]
+
+
+def lane_sum(pair):
+    high, low = pair
+    large = 6144.0 * jnp.max(jnp.abs(high), axis=1, keepdims=True)
+    lead = (high + large) - large
+    rest = (high - lead) + low
+    total = [jnp.broadcast_to(jnp.sum(a, axis=1, keepdims=True), (8, 128)) for a in (lead, rest)]
+    return two_sum(*total)
 
 
 def fold_rows(value):
@@ -394,8 +405,7 @@
     last = iota((8, 128), 0) == 6
     packed = pair_tree([(parts_ref[y, 8], parts_ref[y, 9]) for y in range(8)])
     packed = pair_add(packed, (jnp.where(last, pair[0], 0.0), jnp.where(last, pair[1], 0.0)))
-    for by in (64, 32, 16, 8, 4, 2, 1):
-        packed = pair_add(packed, (pltpu.roll(packed[0], by, axis=1), pltpu.roll(packed[1], by, axis=1)))
+    packed = lane_sum(packed)
     lane = iota((8, 128), 1)
     value = jnp.where(lane < 64, packed[0], packed[1])
     value = jnp.sum(jnp.where(iota((8, 128), 0) == lane % 64 // 8, value, 0.0), axis=0, keepdims=True)
@@ -463,8 +473,6 @@
     series = lax.axis_index("series")
     own_weight = lax.dynamic_slice_in_dim(ar_weight, 8 * series, 8, 0)
     weight = jnp.broadcast_to(own_weight.T[:, :, None], (LAGS, 8, 128))
-    theta = RIDGE_TIME + AR * (1.0 + jnp.sum(ar_weight * ar_weight) / 64.0)
-    theta = jnp.broadcast_to(theta, (8, 128))
     observed = observed.T
     context = pltpu.VMEM((48, 8, 128), F32)
     errors = pltpu.VMEM((20, 8, 128), F32)
@@ -490,17 +498,23 @@
     near = neighbour(plane)
     gathered = lax.all_to_all(solved, ("ty", "tz"), 0, 0).reshape(64, 128)
     gathered, near = lax.optimization_barrier((gathered, near))
+    gathered, near = lax.optimization_barrier((gathered, near))
     factors, normal = call(
         functools.partial(normal_kernel, 1.0 / cells_all),
         (struct(cells, 64), struct(64, 768)),
         (gathered, panel, observed),
     )
     sums = lax.all_to_all(normal.reshape(8, 8, 768), "series", 0, 0)
+    drift, theta = call(
+        functools.partial(drift_kernel, steps_all),
+        (struct(4, 8, 128), struct(8, 128)),
+        (plane, near, weight, ar_weight, lags),
+        (context, errors),
+    )
     u0, own0, h = call(
-        functools.partial(start_kernel, steps_all),
+        start_kernel,
         (struct(8, 4, 8, 128), struct(4, 8, 128), struct(4, 8, 64)),
-        (sums, start_time, plane, near, weight, lags),
-        (context, errors),
+        (sums, start_time, drift),
     )
 
     def image(plane, near, wide):

time: 180 us -> 176 us (0.978)
  blocking collectives: 103 us -> 112 us
  waiting for transfers between devices: 21.1 us -> 15.1 us
  starting transfers between devices: 36.6 us -> 30.6 us
    all_to_all x1 -> x2, blocking collectives: 10.2 us -> 20.4 us  [exchange(): return (plane, neighbour(plane), lax.all_to_all(spread, 'series', 0, 0))]
    all_to_all x1 -> x0, starting transfers between devices: 5.83 us -> none  [exchange(): return (plane, neighbour(plane), lax.all_to_all(spread, 'series', 0, 0))]
    all_to_all x1 -> x0, waiting for transfers between devices: 4.04 us -> none  [exchange(): return (plane, neighbour(plane), lax.all_to_all(spread, 'series', 0, 0))]
    all_to_all x1, waiting for transfers between devices: 5.12 us -> 3.15 us  [per_device(): sums = lax.all_to_all(normal.reshape(8, 8, 768), 'series', 0, 0)]
    pallas_call x10 -> x11, Pallas kernels: 15 us -> 14.1 us  [call(): pl.pallas_call(kernel, out_shape=outs, in_specs=specs, out_specs=jax.tree...]
  transfers between devices with their start and end apart: 8 -> 7, of which waited for: 4 -> 3; matrix products, arithmetic and copies ran while one was open for 1% -> 1% of each run, Pallas kernels for 0% -> 1%
where the time goes in v5:
time: 176 us; the launch traced here: 175 us
  blocking collectives  112 us (64%)
  starting transfers between devices  30.6 us (17%)
  waiting for transfers between devices  15.1 us (9%)
  Pallas kernels  14.1 us (8%)
  local copies, waits for them, and re-layouts  2.23 us (1%)
    all_to_all x2, blocking collectives, per_device(): parts = lax.all_to_all(parts, 'ty', 0, 0)  34.7 us
    all_to_all x2, blocking collectives, exchange(): return (plane, neighbour(plane), lax.all_to_all(spread, 'series', 0, 0))  20.4 us
    all_to_all x2, blocking collectives, exchange(): plane = lax.all_to_all(spread, 'ty', 0, 0).reshape(32, 8, 128)  20.3 us
    all_to_all x1, blocking collectives, per_device(): parts = lax.all_to_all(parts, 'tz', 0, 0)  20.2 us
    all_to_all x1, blocking collectives, per_device(): gathered = lax.all_to_all(solved, ('ty', 'tz'), 0, 0).reshape(64, 128)  16.5 us
    pallas_call x11, Pallas kernels, call(): pl.pallas_call(kernel, out_shape=outs, in_specs=specs, out_specs=jax.tree...  14.1 us
    all_to_all x1, starting transfers between devices, per_device(): moments = lax.all_to_all(moments, ('series', 'tz'), 0, 0).reshape(64, 128)  8.91 us
    all_to_all x1, starting transfers between devices, per_device(): sums = lax.all_to_all(normal.reshape(8, 8, 768), 'series', 0, 0)  8.83 us
  transfers between devices with their start and end apart: 7, of which 3 were waited for; matrix products, arithmetic and copies ran while one was open for 1% of the time, Pallas kernels for 1%

profile of v5, /device:TPU:1, one launch (start us, length us, event | category | flops | bytes accessed | tf_op | source)
XLA Modules:
  0.0 174.8 jit_solution(6985915424281989713)
XLA Ops:
  0.6 2.8 %shard_map.68 = f32[8,112,128]{2,1,0:T(8,128)} custom-call(f32[128,512]{1,0:T(8,128)} %panel_ref.1, s32[4,128]{1,0:T(4,128)} %bitcast.14, f32[64,512]{1,0:T(8,128)} %x_ref.3), custom_call_target="tpu_custom_call" | custom-call | tf_op jit(solution)/shard_map/pallas_call | solution.py:34
  3.4 20.3 %all_to_all.55.parts_ref = f32[8,112,128]{2,1,0:T(8,128)S(1)} all-to-all(f32[8,112,128]{2,1,0:T(8,128)} %shard_map.68), channel_id=1, replica_groups=mesh['series'=8,'tz'=8,'ty'=8] {'ty'}, dimensions={0} | all-to-all | bytes 917504 | tf_op jit(solution)/shard_map/all_to_all | solution.py:493
  23.7 0.5 shard_map.69
  24.3 20.2 %all_to_all.56.parts_ref = f32[8,40,128]{2,1,0:T(8,128)S(1)} all-to-all(f32[8,40,128]{2,1,0:T(8,128)S(1)} %get-tuple-element.19), channel_id=1, replica_groups=mesh['series'=8,'tz'=8,'ty'=8] {'tz'}, dimensions={0} | all-to-all | bytes 327680 | tf_op jit(solution)/shard_map/all_to_all | solution.py:495
  44.4 1.7 shard_map.70
  46.2 2.1 %collective-permute-start = (f32[32,8,128]{2,1,0:T(8,128)S(1)}, f32[32,8,128]{2,1,0:T(8,128)S(1)}, u32[]{:S(2)}, u32[]{:S(2)}) collective-permute-start(f32[32,8,128]{2,1,0:T(8,128)S(1)} %get-tuple-element.22.plane_ref), channel_id=1, source_target_pairs={{0,8},{1,9},{2,10},{3,11},{4,60},{5,61},{6,62},{7,63},{8,16},{9,17... | collective-permute-start | bytes 393224 | tf_op jit(solution)/shard_map/ppermute | solution.py:461
  48.3 16.5 %all_to_all.57 = f32[64,1,128]{2,1,0:T(1,128)S(1)} all-to-all(f32[64,1,128]{2,1,0:T(1,128)S(1)} %shard_map.70), channel_id=1, replica_groups=mesh['series'=8,'tz'=8,'ty'=8] {'ty','tz'}, dimensions={0} | all-to-all | bytes 65536 | tf_op jit(solution)/shard_map/all_to_all | solution.py:499
  64.8 1.2 shard_map.71
  66.0 8.8 %all-to-all-start.3 = ((f32[8,8,768]{2,1,0:T(8,128)}), f32[8,8,768]{2,1,0:T(8,128)S(1)}, u32[]{:S(2)}, u32[]{:S(2)}) async-start(f32[8,8,768]{2,1,0:T(8,128)} %bitcast.2), calls=%async_computation.3 | async-start | bytes 393216 | tf_op jit(solution)/shard_map/all_to_all | solution.py:507
  74.8 0.7 copy-done.4
  75.8 0.6 copy-done.3
  76.4 1.2 shard_map.72
  77.6 3.2 %all-to-all-done.3.sums_ref = f32[8,8,768]{2,1,0:T(8,128)S(1)} async-done(((f32[8,8,768]{2,1,0:T(8,128)}), f32[8,8,768]{2,1,0:T(8,128)S(1)}, u32[]{:S(2)}, u32[]{:S(2)}) %all-to-all-start.3) | async-done | bytes 196640 | tf_op jit(solution)/shard_map/all_to_all | solution.py:507
  80.7 0.3 shard_map.73
  81.0 10.1 %all_to_all.58 = f32[8,4,8,128]{3,2,1,0:T(8,128)S(1)} all-to-all(f32[8,4,8,128]{3,2,1,0:T(8,128)S(1)} %get-tuple-element.28), channel_id=1, replica_groups=mesh['series'=8,'tz'=8,'ty'=8] {'ty'}, dimensions={0} | all-to-all | bytes 262144 | tf_op jit(solution)/shard_map/all_to_all | solution.py:465
  91.2 2.2 %collective-permute-start.1 = (f32[32,8,128]{2,1,0:T(8,128)S(1)}, f32[32,8,128]{2,1,0:T(8,128)S(1)}, u32[]{:S(2)}, u32[]{:S(2)}) collective-permute-start(f32[32,8,128]{2,1,0:T(8,128)S(1)} %bitcast.8), channel_id=1, source_target_pairs={{0,8},{1,9},{2,10},{3,11},{4,60},{5,61},{6,62},{7,63},{8,16},{9,17... | collective-permute-start | bytes 393224 | tf_op jit(solution)/shard_map/ppermute | solution.py:461
  93.4 10.2 %all_to_all.59.wide_ref.wide0_ref = f32[8,4,8,128]{3,2,1,0:T(8,128)S(1)} all-to-all(f32[8,4,8,128]{3,2,1,0:T(8,128)S(1)} %get-tuple-element.28), channel_id=1, replica_groups=mesh['series'=8,'tz'=8,'ty'=8] {'series'}, dimensions={0} | all-to-all | bytes 262144 | tf_op jit(solution)/shard_map/all_to_all | solution.py:466
  103.6 1.2 shard_map.74
  104.8 10.1 %all_to_all.60 = f32[8,4,8,128]{3,2,1,0:T(8,128)S(1)} all-to-all(f32[8,4,8,128]{3,2,1,0:T(8,128)S(1)} %get-tuple-element.31), channel_id=1, replica_groups=mesh['series'=8,'tz'=8,'ty'=8] {'ty'}, dimensions={0} | all-to-all | bytes 262144 | tf_op jit(solution)/shard_map/all_to_all | solution.py:465
  114.9 2.2 %collective-permute-start.2 = (f32[32,8,128]{2,1,0:T(8,128)S(1)}, f32[32,8,128]{2,1,0:T(8,128)S(1)}, u32[]{:S(2)}, u32[]{:S(2)}) collective-permute-start(f32[32,8,128]{2,1,0:T(8,128)S(1)} %bitcast.10), channel_id=1, source_target_pairs={{0,8},{1,9},{2,10},{3,11},{4,60},{5,61},{6,62},{7,63},{8,16},{9,17... | collective-permute-start | bytes 393224 | tf_op jit(solution)/shard_map/ppermute | solution.py:461
  117.2 10.2 %all_to_all.61.wide_ref.wide1_ref = f32[8,4,8,128]{3,2,1,0:T(8,128)S(1)} all-to-all(f32[8,4,8,128]{3,2,1,0:T(8,128)S(1)} %get-tuple-element.31), channel_id=1, replica_groups=mesh['series'=8,'tz'=8,'ty'=8] {'series'}, dimensions={0} | all-to-all | bytes 262144 | tf_op jit(solution)/shard_map/all_to_all | solution.py:466
  127.4 1.9 %shard_map.75 = (f32[8,4,8,128]{3,2,1,0:T(8,128)}, f32[4,8,128]{2,1,0:T(8,128)S(1)}) custom-call(f32[32,8,128]{2,1,0:T(8,128)S(1)} %bitcast.11, f32[32,8,128]{2,1,0:T(8,128)S(1)} %collective-permute-done.2.near_ref, f32[8,4,8,128]{3,2,1,0:T(8,128)S(1)} %all_to_all.61.wide_ref.wide1_ref, f32[4,8,64]{2,1,0:T(8,128)S(1)} %get-tuple-element.29.h_ref, ...), custom_call_target="tpu_custom_call" | custom-call | tf_op jit(solution)/shard_map/pallas_call | solution.py:34
  129.2 4.1 %all-to-all-start.8 = ((f32[8,4,8,128]{3,2,1,0:T(8,128)}), f32[8,4,8,128]{3,2,1,0:T(8,128)S(1)}, u32[]{:S(2)}, u32[]{:S(2)}) async-start(f32[8,4,8,128]{3,2,1,0:T(8,128)} %get-tuple-element.32), calls=%async_computation.8 | async-start | bytes 262144 | tf_op jit(solution)/shard_map/all_to_all | solution.py:533
  133.4 2.2 %collective-permute-start.3 = (f32[4,8,128]{2,1,0:T(8,128)S(1)}, f32[4,8,128]{2,1,0:T(8,128)S(1)}, u32[]{:S(2)}, u32[]{:S(2)}) collective-permute-start(f32[4,8,128]{2,1,0:T(8,128)S(1)} %get-tuple-element.35.u2_ref), channel_id=1, source_target_pairs={{0,8},{8,16},{16,24},{24,32},{32,40},{40,48},{48,56},{56,0},{1,9},... | collective-permute-start | bytes 49160 | tf_op jit(solution)/shard_map/ppermute | solution.py:532
  135.6 3.5 %collective-permute-done.3.near_ref = f32[4,8,128]{2,1,0:T(8,128)S(1)} collective-permute-done((f32[4,8,128]{2,1,0:T(8,128)S(1)}, f32[4,8,128]{2,1,0:T(8,128)S(1)}, u32[]{:S(2)}, u32[]{:S(2)}) %collective-permute-start.3) | collective-permute-done | bytes 16416 | tf_op jit(solution)/shard_map/ppermute | solution.py:532
  139.2 0.3 shard_map.76
  139.4 14.4 %all_to_all.62.parts_ref = f32[8,10,8,128]{3,2,1,0:T(8,128)S(1)} all-to-all(f32[8,10,8,128]{3,2,1,0:T(8,128)S(1)} %shard_map.76), channel_id=1, replica_groups=mesh['series'=8,'tz'=8,'ty'=8] {'ty'}, dimensions={0} | all-to-all | bytes 655360 | tf_op jit(solution)/shard_map/all_to_all | solution.py:535
  153.8 2.0 %shard_map.77 = f32[64,1,128]{2,1,0:T(1,128)} custom-call(f32[8,10,8,128]{3,2,1,0:T(8,128)S(1)} %all_to_all.62.parts_ref, f32[14,8,128]{2,1,0:T(8,128)S(1)} %broadcast_in_dim.2.weight_ref, s32[14]{0:T(128)S(1)} %copy-done.3), custom_call_target="tpu_custom_call" | custom-call | tf_op jit(solution)/shard_map/pallas_call | solution.py:34
  155.7 8.9 %all-to-all-start.10 = ((f32[64,1,128]{2,1,0:T(1,128)}), f32[64,1,128]{2,1,0:T(1,128)S(1)}, u32[]{:S(2)}, u32[]{:S(2)}) async-start(f32[64,1,128]{2,1,0:T(1,128)} %shard_map.77), calls=%async_computation.10 | async-start | bytes 65536 | tf_op jit(solution)/shard_map/all_to_all | solution.py:539
  164.7 0.7 copy.12
  165.4 8.4 %all-to-all-done.10 = f32[64,1,128]{2,1,0:T(1,128)S(1)} async-done(((f32[64,1,128]{2,1,0:T(1,128)}), f32[64,1,128]{2,1,0:T(1,128)S(1)}, u32[]{:S(2)}, u32[]{:S(2)}) %all-to-all-start.10) | async-done | bytes 32800 | tf_op jit(solution)/shard_map/all_to_all | solution.py:539
  173.8 1.0 shard_map.78
  (15 shorter events, 0.3 us)
Async XLA Ops:
  24.2 40.5 %copy-start.1 = (f32[128,512]{1,0:T(8,128)S(1)}, f32[128,512]{1,0:T(8,128)}, u32[]{:S(2)}) copy-start(f32[128,512]{1,0:T(8,128)} %panel_ref.1) | copy-start | bytes 786436
  46.2 18.6 %collective-permute-start = (f32[32,8,128]{2,1,0:T(8,128)S(1)}, f32[32,8,128]{2,1,0:T(8,128)S(1)}, u32[]{:S(2)}, u32[]{:S(2)}) collective-permute-start(f32[32,8,128]{2,1,0:T(8,128)S(1)} %get-tuple-element.22.plane_ref), channel_id=1, source_target_pairs={{0,8},{1,9},{2,10},{3,11},{4,60},{5,61},{6,62},{7,63},{8,16},{9,17... | collective-permute-start | bytes 393224 | tf_op jit(solution)/shard_map/ppermute | solution.py:461
  48.3 16.5 %copy-start.2 = (s32[128,4]{0,1:T(4,128)S(1)}, s32[128,4]{0,1:T(4,128)}, u32[]{:S(2)}) copy-start(s32[128,4]{0,1:T(4,128)} %param.6) | copy-start | bytes 6148
  66.0 14.7 %all-to-all-start.3 = ((f32[8,8,768]{2,1,0:T(8,128)}), f32[8,8,768]{2,1,0:T(8,128)S(1)}, u32[]{:S(2)}, u32[]{:S(2)}) async-start(f32[8,8,768]{2,1,0:T(8,128)} %bitcast.2), calls=%async_computation.3 | async-start | bytes 393216 | tf_op jit(solution)/shard_map/all_to_all | solution.py:507
  74.8 0.7 copy-start.4
  75.7 0.7 copy-start.3
  76.4 4.4 %copy-start = (f32[64,512]{1,0:T(8,128)S(1)}, f32[64,512]{1,0:T(8,128)}, u32[]{:S(2)}) copy-start(f32[64,512]{1,0:T(8,128)} %x_ref.3) | copy-start | bytes 393220
  91.2 12.4 %collective-permute-start.1 = (f32[32,8,128]{2,1,0:T(8,128)S(1)}, f32[32,8,128]{2,1,0:T(8,128)S(1)}, u32[]{:S(2)}, u32[]{:S(2)}) collective-permute-start(f32[32,8,128]{2,1,0:T(8,128)S(1)} %bitcast.8), channel_id=1, source_target_pairs={{0,8},{1,9},{2,10},{3,11},{4,60},{5,61},{6,62},{7,63},{8,16},{9,17... | collective-permute-start | bytes 393224 | tf_op jit(solution)/shard_map/ppermute | solution.py:461
  114.9 12.5 %collective-permute-start.2 = (f32[32,8,128]{2,1,0:T(8,128)S(1)}, f32[32,8,128]{2,1,0:T(8,128)S(1)}, u32[]{:S(2)}, u32[]{:S(2)}) collective-permute-start(f32[32,8,128]{2,1,0:T(8,128)S(1)} %bitcast.10), channel_id=1, source_target_pairs={{0,8},{1,9},{2,10},{3,11},{4,60},{5,61},{6,62},{7,63},{8,16},{9,17... | collective-permute-start | bytes 393224 | tf_op jit(solution)/shard_map/ppermute | solution.py:461
  129.2 9.9 %all-to-all-start.8 = ((f32[8,4,8,128]{3,2,1,0:T(8,128)}), f32[8,4,8,128]{3,2,1,0:T(8,128)S(1)}, u32[]{:S(2)}, u32[]{:S(2)}) async-start(f32[8,4,8,128]{3,2,1,0:T(8,128)} %get-tuple-element.32), calls=%async_computation.8 | async-start | bytes 262144 | tf_op jit(solution)/shard_map/all_to_all | solution.py:533
  133.4 5.8 %collective-permute-start.3 = (f32[4,8,128]{2,1,0:T(8,128)S(1)}, f32[4,8,128]{2,1,0:T(8,128)S(1)}, u32[]{:S(2)}, u32[]{:S(2)}) collective-permute-start(f32[4,8,128]{2,1,0:T(8,128)S(1)} %get-tuple-element.35.u2_ref), channel_id=1, source_target_pairs={{0,8},{8,16},{16,24},{24,32},{32,40},{40,48},{48,56},{56,0},{1,9},... | collective-permute-start | bytes 49160 | tf_op jit(solution)/shard_map/ppermute | solution.py:532
  155.7 18.0 %all-to-all-start.10 = ((f32[64,1,128]{2,1,0:T(1,128)}), f32[64,1,128]{2,1,0:T(1,128)S(1)}, u32[]{:S(2)}, u32[]{:S(2)}) async-start(f32[64,1,128]{2,1,0:T(1,128)} %shard_map.77), calls=%async_computation.10 | async-start | bytes 65536 | tf_op jit(solution)/shard_map/all_to_all | solution.py:539

commit v6 on v5

--- a/solution.py
+++ b/solution.py
@@ -186,7 +186,14 @@
     right = [panel_ref[:, b * TILE : (b + 1) * TILE] * flags[:, b : b + 1] for b in range(4)]
     for b in (0, 2):
         right.append(jnp.concatenate([factors * flags[:, b : b + 1], factors * flags[:, b + 1 : b + 2]], axis=1))
-    out_ref[...] = scale * dot(factors, jnp.concatenate(right, axis=1), ((0,), (0,)))
+    right.append(factors)
+    product = scale * dot(factors, jnp.concatenate(right, axis=1), ((0,), (0,)))
+    out_ref[:, 0:768] = product[:, 0:768]
+    gram = product[:, 768:832]
+    norm = jnp.sum(gram * gram)
+    trace = jnp.sum(jnp.where(iota((64, 64), 0) == iota((64, 64), 1), gram, 0.0))
+    some = jnp.full((64, 128), trace)
+    out_ref[:, 768:896] = jnp.where(some > 0.0, norm / jnp.where(some > 0.0, some, 1.0), 0.0)
 
 
 def lagged(read, count, lags_ref, weight_ref, ahead):
@@ -249,10 +256,11 @@
     theta_ref[...] = jnp.full((8, 128), RIDGE_TIME + AR) + (AR / 64.0) * jnp.sum(squares)
 
 
-def start_kernel(sums_ref, x_ref, drift_ref, out_ref, own_ref, h_ref):
+def start_kernel(sums_ref, x_ref, drift_ref, theta_ref, out_ref, own_ref, h_ref, first_ref):
     total = sums_ref[0]
     for j in range(1, 8):
         total = total + sums_ref[j]
+    first_ref[...] = theta_ref[...] + total[:, 768:896]
     for q in range(4):
         h = total[:, 512 + 64 * q : 576 + 64 * q]
         h_ref[q] = h
@@ -412,7 +420,7 @@
     out_ref[...] = jnp.broadcast_to(value[None], out_ref.shape)
 
 
-def finish_kernel(parts_ref, theta_ref, x_ref, wide0_ref, wide1_ref, wide2_ref, out_ref):
+def finish_kernel(parts_ref, first_ref, theta_ref, x_ref, wide0_ref, wide1_ref, wide2_ref, out_ref):
     half = iota((8, 128), 1) < 64
     pairs = []
     for j in range(8):
@@ -428,9 +436,10 @@
 
     g00, g01, g02, g11, g12, g22, m22 = [moment(i) for i in range(7)]
     theta = (theta_ref[...], jnp.zeros((8, 128), F32))
-    m00 = pair_add(g01, pair_mul(theta, g00))
-    m01 = pair_add(g11, pair_mul(theta, g01))
-    m02 = pair_add(g12, pair_mul(theta, g02))
+    first = (first_ref[...], jnp.zeros((8, 128), F32))
+    m00 = pair_add(g01, pair_mul(first, g00))
+    m01 = pair_add(g11, pair_mul(first, g01))
+    m02 = pair_add(g12, pair_mul(first, g02))
     m11 = pair_add(g12, pair_mul(theta, g11))
     m12 = pair_add(g22, pair_mul(theta, g12))
     l10 = pair_div(m01, m00)
@@ -501,34 +510,34 @@
     gathered, near = lax.optimization_barrier((gathered, near))
     factors, normal = call(
         functools.partial(normal_kernel, 1.0 / cells_all),
-        (struct(cells, 64), struct(64, 768)),
+        (struct(cells, 64), struct(64, 896)),
         (gathered, panel, observed),
     )
-    sums = lax.all_to_all(normal.reshape(8, 8, 768), "series", 0, 0)
+    sums = lax.all_to_all(normal.reshape(8, 8, 896), "series", 0, 0)
     drift, theta = call(
         functools.partial(drift_kernel, steps_all),
         (struct(4, 8, 128), struct(8, 128)),
         (plane, near, weight, ar_weight, lags),
         (context, errors),
     )
-    u0, own0, h = call(
+    u0, own0, h, first = call(
         start_kernel,
-        (struct(8, 4, 8, 128), struct(4, 8, 128), struct(4, 8, 64)),
-        (sums, start_time, drift),
+        (struct(8, 4, 8, 128), struct(4, 8, 128), struct(4, 8, 64), struct(8, 128)),
+        (sums, start_time, drift, theta),
     )
 
-    def image(plane, near, wide):
+    def image(plane, near, wide, shift):
         return call(
             functools.partial(image_kernel, steps_all),
             (struct(8, 4, 8, 128), struct(4, 8, 128)),
-            (plane, near, wide, h, weight, theta, lags),
+            (plane, near, wide, h, weight, shift, lags),
             (context, errors),
         )
 
     plane, near, wide0 = exchange(u0)
-    u1, own1 = image(plane, near, wide0)
+    u1, own1 = image(plane, near, wide0, first)
     plane, near, wide1 = exchange(u1)
-    u2, own2 = image(plane, near, wide1)
+    u2, own2 = image(plane, near, wide1, theta)
     near = lax.ppermute(own2, "tz", [(z, (z + 1) % 8) for z in range(8)])
     wide2 = lax.all_to_all(u2, "series", 0, 0)
     parts = call(product_kernel, struct(8, 10, 8, 128), (wide2, h, own0, own1, own2, near))
@@ -537,7 +546,7 @@
         functools.partial(moment_kernel, steps_all), struct(64, 1, 128), (parts, weight, lags), (context,)
     )
     moments = lax.all_to_all(moments, ("series", "tz"), 0, 0).reshape(64, 128)
-    result = call(finish_kernel, struct(64, 512), (moments, theta, start_time, wide0, wide1, wide2))
+    result = call(finish_kernel, struct(64, 512), (moments, first, theta, start_time, wide0, wide1, wide2))
     return (factors, result)
 
 

time: 176 us -> 176 us (level)
  no operation moved by 1% of the time
where the time goes in v6:
time: 176 us; the launch traced here: 175 us
  blocking collectives  112 us (64%)
  starting transfers between devices  30.6 us (17%)
  waiting for transfers between devices  15.4 us (9%)
  Pallas kernels  14.2 us (8%)
  local copies, waits for them, and re-layouts  2.23 us (1%)
    all_to_all x2, blocking collectives, per_device(): parts = lax.all_to_all(parts, 'ty', 0, 0)  34.7 us
    all_to_all x2, blocking collectives, exchange(): return (plane, neighbour(plane), lax.all_to_all(spread, 'series', 0, 0))  20.5 us
    all_to_all x2, blocking collectives, exchange(): plane = lax.all_to_all(spread, 'ty', 0, 0).reshape(32, 8, 128)  20.3 us
    all_to_all x1, blocking collectives, per_device(): parts = lax.all_to_all(parts, 'tz', 0, 0)  20.2 us
    all_to_all x1, blocking collectives, per_device(): gathered = lax.all_to_all(solved, ('ty', 'tz'), 0, 0).reshape(64, 128)  16.5 us
    pallas_call x11, Pallas kernels, call(): pl.pallas_call(kernel, out_shape=outs, in_specs=specs, out_specs=jax.tree...  14.2 us
    all_to_all x1, starting transfers between devices, per_device(): moments = lax.all_to_all(moments, ('series', 'tz'), 0, 0).reshape(64, 128)  8.91 us
    all_to_all x1, starting transfers between devices, per_device(): sums = lax.all_to_all(normal.reshape(8, 8, 896), 'series', 0, 0)  8.83 us
  transfers between devices with their start and end apart: 7, of which 3 were waited for; matrix products, arithmetic and copies ran while one was open for 1% of the time, Pallas kernels for 1%

profile of v6, /device:TPU:1, one launch (start us, length us, event | category | flops | bytes accessed | tf_op | source)
XLA Modules:
  0.0 175.3 jit_solution(3534598411503355039)
XLA Ops:
  0.6 2.8 %shard_map.68 = f32[8,112,128]{2,1,0:T(8,128)} custom-call(f32[128,512]{1,0:T(8,128)} %panel_ref.1, s32[4,128]{1,0:T(4,128)} %bitcast.14, f32[64,512]{1,0:T(8,128)} %x_ref.3), custom_call_target="tpu_custom_call" | custom-call | tf_op jit(solution)/shard_map/pallas_call | solution.py:34
  3.4 20.3 %all_to_all.55.parts_ref = f32[8,112,128]{2,1,0:T(8,128)S(1)} all-to-all(f32[8,112,128]{2,1,0:T(8,128)} %shard_map.68), channel_id=1, replica_groups=mesh['series'=8,'tz'=8,'ty'=8] {'ty'}, dimensions={0} | all-to-all | bytes 917504 | tf_op jit(solution)/shard_map/all_to_all | solution.py:502
  23.7 0.5 shard_map.69
  24.2 20.2 %all_to_all.56.parts_ref = f32[8,40,128]{2,1,0:T(8,128)S(1)} all-to-all(f32[8,40,128]{2,1,0:T(8,128)S(1)} %get-tuple-element.20), channel_id=1, replica_groups=mesh['series'=8,'tz'=8,'ty'=8] {'tz'}, dimensions={0} | all-to-all | bytes 327680 | tf_op jit(solution)/shard_map/all_to_all | solution.py:504
  44.4 1.7 shard_map.70
  46.2 2.1 %collective-permute-start = (f32[32,8,128]{2,1,0:T(8,128)S(1)}, f32[32,8,128]{2,1,0:T(8,128)S(1)}, u32[]{:S(2)}, u32[]{:S(2)}) collective-permute-start(f32[32,8,128]{2,1,0:T(8,128)S(1)} %get-tuple-element.23.plane_ref), channel_id=1, source_target_pairs={{0,8},{1,9},{2,10},{3,11},{4,60},{5,61},{6,62},{7,63},{8,16},{9,17... | collective-permute-start | bytes 393224 | tf_op jit(solution)/shard_map/ppermute | solution.py:470
  48.3 16.5 %all_to_all.57 = f32[64,1,128]{2,1,0:T(1,128)S(1)} all-to-all(f32[64,1,128]{2,1,0:T(1,128)S(1)} %shard_map.70), channel_id=1, replica_groups=mesh['series'=8,'tz'=8,'ty'=8] {'ty','tz'}, dimensions={0} | all-to-all | bytes 65536 | tf_op jit(solution)/shard_map/all_to_all | solution.py:508
  64.8 1.4 shard_map.71
  66.1 8.8 %all-to-all-start.3 = ((f32[8,8,896]{2,1,0:T(8,128)}), f32[8,8,896]{2,1,0:T(8,128)S(1)}, u32[]{:S(2)}, u32[]{:S(2)}) async-start(f32[8,8,896]{2,1,0:T(8,128)} %bitcast.2), calls=%async_computation.3 | async-start | bytes 458752 | tf_op jit(solution)/shard_map/all_to_all | solution.py:516
  74.9 0.7 copy-done.4
  75.9 0.6 copy-done.3
  76.5 1.2 shard_map.72
  77.7 3.5 %all-to-all-done.3.sums_ref = f32[8,8,896]{2,1,0:T(8,128)S(1)} async-done(((f32[8,8,896]{2,1,0:T(8,128)}), f32[8,8,896]{2,1,0:T(8,128)S(1)}, u32[]{:S(2)}, u32[]{:S(2)}) %all-to-all-start.3) | async-done | bytes 229408 | tf_op jit(solution)/shard_map/all_to_all | solution.py:516
  81.1 0.3 shard_map.73
  81.4 10.1 %all_to_all.58 = f32[8,4,8,128]{3,2,1,0:T(8,128)S(1)} all-to-all(f32[8,4,8,128]{3,2,1,0:T(8,128)S(1)} %get-tuple-element.30), channel_id=1, replica_groups=mesh['series'=8,'tz'=8,'ty'=8] {'ty'}, dimensions={0} | all-to-all | bytes 262144 | tf_op jit(solution)/shard_map/all_to_all | solution.py:474
  91.6 2.2 %collective-permute-start.1 = (f32[32,8,128]{2,1,0:T(8,128)S(1)}, f32[32,8,128]{2,1,0:T(8,128)S(1)}, u32[]{:S(2)}, u32[]{:S(2)}) collective-permute-start(f32[32,8,128]{2,1,0:T(8,128)S(1)} %bitcast.8), channel_id=1, source_target_pairs={{0,8},{1,9},{2,10},{3,11},{4,60},{5,61},{6,62},{7,63},{8,16},{9,17... | collective-permute-start | bytes 393224 | tf_op jit(solution)/shard_map/ppermute | solution.py:470
  93.8 10.2 %all_to_all.59.wide_ref.wide0_ref = f32[8,4,8,128]{3,2,1,0:T(8,128)S(1)} all-to-all(f32[8,4,8,128]{3,2,1,0:T(8,128)S(1)} %get-tuple-element.30), channel_id=1, replica_groups=mesh['series'=8,'tz'=8,'ty'=8] {'series'}, dimensions={0} | all-to-all | bytes 262144 | tf_op jit(solution)/shard_map/all_to_all | solution.py:475
  104.0 1.2 shard_map.74
  105.2 10.1 %all_to_all.60 = f32[8,4,8,128]{3,2,1,0:T(8,128)S(1)} all-to-all(f32[8,4,8,128]{3,2,1,0:T(8,128)S(1)} %get-tuple-element.33), channel_id=1, replica_groups=mesh['series'=8,'tz'=8,'ty'=8] {'ty'}, dimensions={0} | all-to-all | bytes 262144 | tf_op jit(solution)/shard_map/all_to_all | solution.py:474
  115.4 2.2 %collective-permute-start.2 = (f32[32,8,128]{2,1,0:T(8,128)S(1)}, f32[32,8,128]{2,1,0:T(8,128)S(1)}, u32[]{:S(2)}, u32[]{:S(2)}) collective-permute-start(f32[32,8,128]{2,1,0:T(8,128)S(1)} %bitcast.10), channel_id=1, source_target_pairs={{0,8},{1,9},{2,10},{3,11},{4,60},{5,61},{6,62},{7,63},{8,16},{9,17... | collective-permute-start | bytes 393224 | tf_op jit(solution)/shard_map/ppermute | solution.py:470
  117.6 10.2 %all_to_all.61.wide_ref.wide1_ref = f32[8,4,8,128]{3,2,1,0:T(8,128)S(1)} all-to-all(f32[8,4,8,128]{3,2,1,0:T(8,128)S(1)} %get-tuple-element.33), channel_id=1, replica_groups=mesh['series'=8,'tz'=8,'ty'=8] {'series'}, dimensions={0} | all-to-all | bytes 262144 | tf_op jit(solution)/shard_map/all_to_all | solution.py:475
  127.8 1.9 %shard_map.75 = (f32[8,4,8,128]{3,2,1,0:T(8,128)}, f32[4,8,128]{2,1,0:T(8,128)S(1)}) custom-call(f32[32,8,128]{2,1,0:T(8,128)S(1)} %bitcast.11, f32[32,8,128]{2,1,0:T(8,128)S(1)} %collective-permute-done.2.near_ref, f32[8,4,8,128]{3,2,1,0:T(8,128)S(1)} %all_to_all.61.wide_ref.wide1_ref, f32[4,8,64]{2,1,0:T(8,128)S(1)} %get-tuple-element.31.h_ref, ...), custom_call_target="tpu_custom_call" | custom-call | tf_op jit(solution)/shard_map/pallas_call | solution.py:34
  129.7 4.1 %all-to-all-start.8 = ((f32[8,4,8,128]{3,2,1,0:T(8,128)}), f32[8,4,8,128]{3,2,1,0:T(8,128)S(1)}, u32[]{:S(2)}, u32[]{:S(2)}) async-start(f32[8,4,8,128]{3,2,1,0:T(8,128)} %get-tuple-element.34), calls=%async_computation.8 | async-start | bytes 262144 | tf_op jit(solution)/shard_map/all_to_all | solution.py:542
  133.8 2.2 %collective-permute-start.3 = (f32[4,8,128]{2,1,0:T(8,128)S(1)}, f32[4,8,128]{2,1,0:T(8,128)S(1)}, u32[]{:S(2)}, u32[]{:S(2)}) collective-permute-start(f32[4,8,128]{2,1,0:T(8,128)S(1)} %get-tuple-element.37.u2_ref), channel_id=1, source_target_pairs={{0,8},{8,16},{16,24},{24,32},{32,40},{40,48},{48,56},{56,0},{1,9},... | collective-permute-start | bytes 49160 | tf_op jit(solution)/shard_map/ppermute | solution.py:541
  136.1 3.5 %collective-permute-done.3.near_ref = f32[4,8,128]{2,1,0:T(8,128)S(1)} collective-permute-done((f32[4,8,128]{2,1,0:T(8,128)S(1)}, f32[4,8,128]{2,1,0:T(8,128)S(1)}, u32[]{:S(2)}, u32[]{:S(2)}) %collective-permute-start.3) | collective-permute-done | bytes 16416 | tf_op jit(solution)/shard_map/ppermute | solution.py:541
  139.6 0.3 shard_map.76
  139.8 14.4 %all_to_all.62.parts_ref = f32[8,10,8,128]{3,2,1,0:T(8,128)S(1)} all-to-all(f32[8,10,8,128]{3,2,1,0:T(8,128)S(1)} %shard_map.76), channel_id=1, replica_groups=mesh['series'=8,'tz'=8,'ty'=8] {'ty'}, dimensions={0} | all-to-all | bytes 655360 | tf_op jit(solution)/shard_map/all_to_all | solution.py:544
  154.2 2.0 %shard_map.77 = f32[64,1,128]{2,1,0:T(1,128)} custom-call(f32[8,10,8,128]{3,2,1,0:T(8,128)S(1)} %all_to_all.62.parts_ref, f32[14,8,128]{2,1,0:T(8,128)S(1)} %broadcast_in_dim.2.weight_ref, s32[14]{0:T(128)S(1)} %copy-done.3), custom_call_target="tpu_custom_call" | custom-call | tf_op jit(solution)/shard_map/pallas_call | solution.py:34
  156.2 8.9 %all-to-all-start.10 = ((f32[64,1,128]{2,1,0:T(1,128)}), f32[64,1,128]{2,1,0:T(1,128)S(1)}, u32[]{:S(2)}, u32[]{:S(2)}) async-start(f32[64,1,128]{2,1,0:T(1,128)} %shard_map.77), calls=%async_computation.10 | async-start | bytes 65536 | tf_op jit(solution)/shard_map/all_to_all | solution.py:548
  165.1 0.7 copy.12
  165.8 8.4 %all-to-all-done.10 = f32[64,1,128]{2,1,0:T(1,128)S(1)} async-done(((f32[64,1,128]{2,1,0:T(1,128)}), f32[64,1,128]{2,1,0:T(1,128)S(1)}, u32[]{:S(2)}, u32[]{:S(2)}) %all-to-all-start.10) | async-done | bytes 32800 | tf_op jit(solution)/shard_map/all_to_all | solution.py:548
  174.2 1.0 shard_map.78
  (15 shorter events, 0.3 us)
Async XLA Ops:
  24.2 40.5 %copy-start.1 = (f32[128,512]{1,0:T(8,128)S(1)}, f32[128,512]{1,0:T(8,128)}, u32[]{:S(2)}) copy-start(f32[128,512]{1,0:T(8,128)} %panel_ref.1) | copy-start | bytes 786436
  46.2 18.6 %collective-permute-start = (f32[32,8,128]{2,1,0:T(8,128)S(1)}, f32[32,8,128]{2,1,0:T(8,128)S(1)}, u32[]{:S(2)}, u32[]{:S(2)}) collective-permute-start(f32[32,8,128]{2,1,0:T(8,128)S(1)} %get-tuple-element.23.plane_ref), channel_id=1, source_target_pairs={{0,8},{1,9},{2,10},{3,11},{4,60},{5,61},{6,62},{7,63},{8,16},{9,17... | collective-permute-start | bytes 393224 | tf_op jit(solution)/shard_map/ppermute | solution.py:470
  48.3 16.5 %copy-start.2 = (s32[128,4]{0,1:T(4,128)S(1)}, s32[128,4]{0,1:T(4,128)}, u32[]{:S(2)}) copy-start(s32[128,4]{0,1:T(4,128)} %param.6) | copy-start | bytes 6148
  66.1 15.0 %all-to-all-start.3 = ((f32[8,8,896]{2,1,0:T(8,128)}), f32[8,8,896]{2,1,0:T(8,128)S(1)}, u32[]{:S(2)}, u32[]{:S(2)}) async-start(f32[8,8,896]{2,1,0:T(8,128)} %bitcast.2), calls=%async_computation.3 | async-start | bytes 458752 | tf_op jit(solution)/shard_map/all_to_all | solution.py:516
  74.9 0.7 copy-start.4
  75.8 0.7 copy-start.3
  76.5 4.7 %copy-start = (f32[64,512]{1,0:T(8,128)S(1)}, f32[64,512]{1,0:T(8,128)}, u32[]{:S(2)}) copy-start(f32[64,512]{1,0:T(8,128)} %x_ref.3) | copy-start | bytes 393220
  91.6 12.5 %collective-permute-start.1 = (f32[32,8,128]{2,1,0:T(8,128)S(1)}, f32[32,8,128]{2,1,0:T(8,128)S(1)}, u32[]{:S(2)}, u32[]{:S(2)}) collective-permute-start(f32[32,8,128]{2,1,0:T(8,128)S(1)} %bitcast.8), channel_id=1, source_target_pairs={{0,8},{1,9},{2,10},{3,11},{4,60},{5,61},{6,62},{7,63},{8,16},{9,17... | collective-permute-start | bytes 393224 | tf_op jit(solution)/shard_map/ppermute | solution.py:470
  115.4 12.4 %collective-permute-start.2 = (f32[32,8,128]{2,1,0:T(8,128)S(1)}, f32[32,8,128]{2,1,0:T(8,128)S(1)}, u32[]{:S(2)}, u32[]{:S(2)}) collective-permute-start(f32[32,8,128]{2,1,0:T(8,128)S(1)} %bitcast.10), channel_id=1, source_target_pairs={{0,8},{1,9},{2,10},{3,11},{4,60},{5,61},{6,62},{7,63},{8,16},{9,17... | collective-permute-start | bytes 393224 | tf_op jit(solution)/shard_map/ppermute | solution.py:470
  129.7 9.9 %all-to-all-start.8 = ((f32[8,4,8,128]{3,2,1,0:T(8,128)}), f32[8,4,8,128]{3,2,1,0:T(8,128)S(1)}, u32[]{:S(2)}, u32[]{:S(2)}) async-start(f32[8,4,8,128]{3,2,1,0:T(8,128)} %get-tuple-element.34), calls=%async_computation.8 | async-start | bytes 262144 | tf_op jit(solution)/shard_map/all_to_all | solution.py:542
  133.8 5.8 %collective-permute-start.3 = (f32[4,8,128]{2,1,0:T(8,128)S(1)}, f32[4,8,128]{2,1,0:T(8,128)S(1)}, u32[]{:S(2)}, u32[]{:S(2)}) collective-permute-start(f32[4,8,128]{2,1,0:T(8,128)S(1)} %get-tuple-element.37.u2_ref), channel_id=1, source_target_pairs={{0,8},{8,16},{16,24},{24,32},{32,40},{40,48},{48,56},{56,0},{1,9},... | collective-permute-start | bytes 49160 | tf_op jit(solution)/shard_map/ppermute | solution.py:541
  156.2 18.0 %all-to-all-start.10 = ((f32[64,1,128]{2,1,0:T(1,128)}), f32[64,1,128]{2,1,0:T(1,128)S(1)}, u32[]{:S(2)}, u32[]{:S(2)}) async-start(f32[64,1,128]{2,1,0:T(1,128)} %shard_map.77), calls=%async_computation.10 | async-start | bytes 65536 | tf_op jit(solution)/shard_map/all_to_all | solution.py:548

commit v7 on v6

--- a/solution.py
+++ b/solution.py
@@ -196,9 +196,9 @@
     out_ref[:, 768:896] = jnp.where(some > 0.0, norm / jnp.where(some > 0.0, some, 1.0), 0.0)
 
 
-def lagged(read, count, lags_ref, weight_ref, ahead):
+def lagged(read, chunks, lags_ref, weight_ref, ahead):
     lane = iota((8, 128), 1)
-    sums = [None] * count
+    sums = {}
     for index in range(LAGS):
         lag = lags_ref[index]
         if ahead:
@@ -212,30 +212,31 @@
         weight = weight_ref[index]
         own = lane < cut
         turn = jnp.where(cut == 128, 0, cut)
-        low = pltpu.roll(read(start), turn, axis=1)
-        for j in range(count):
-            high = pltpu.roll(read(start + j + 1), turn, axis=1)
-            term = weight * jnp.where(own, low, high)
-            sums[j] = term if sums[j] is None else sums[j] + term
-            low = high
+        for first, last in chunks:
+            low = pltpu.roll(read(start + first), turn, axis=1)
+            for j in range(first, last):
+                high = pltpu.roll(read(start + j + 1), turn, axis=1)
+                term = weight * jnp.where(own, low, high)
+                sums[j] = sums[j] + term if j in sums else term
+                low = high
     return sums
 
 
-def residuals(read, count, first_step, steps_all, lags_ref, weight_ref):
-    past = lagged(read, count, lags_ref, weight_ref, False)
+def residuals(read, chunks, first_step, steps_all, lags_ref, weight_ref):
+    past = lagged(read, chunks, lags_ref, weight_ref, False)
     lane = iota((8, 128), 1)
-    out = []
-    for j in range(count):
+    out = {}
+    for j, value in past.items():
         step = first_step + 128 * j + lane
-        out.append(jnp.where((step >= LONGEST) & (step < steps_all), read(j) - past[j], 0.0))
+        out[j] = jnp.where((step >= LONGEST) & (step < steps_all), read(j) - value, 0.0)
     return out
 
 
 def ar_part(read, first_step, steps_all, lags_ref, weight_ref, errors_ref):
-    errors = residuals(read, 20, first_step, steps_all, lags_ref, weight_ref)
-    for j in range(20):
-        errors_ref[j] = errors[j]
-    later = lagged(lambda j: errors_ref[j], 4, lags_ref, weight_ref, True)
+    errors = residuals(read, ((0, 8), (15, 20)), first_step, steps_all, lags_ref, weight_ref)
+    for j, value in errors.items():
+        errors_ref[j] = value
+    later = lagged(lambda j: errors_ref[j], ((0, 4),), lags_ref, weight_ref, True)
     return [errors[j] - later[j] for j in range(4)]
 
 
@@ -387,12 +388,13 @@
         pair = fold_rows(sums[i])
         high = jnp.where(sub == i, pair[0], high)
         low = jnp.where(sub == i, pair[1], low)
+    high, low = pair_add((high, low), (pltpu.roll(high, 64, axis=1), pltpu.roll(low, 64, axis=1)))
+    value = jnp.where(iota((8, 128), 1) < 64, high, low)
     for y in range(8):
         for q in range(4):
             out_ref[y, q] = u2_ref[q]
             out_ref[y, 4 + q] = near_ref[q]
-        out_ref[y, 8] = high
-        out_ref[y, 9] = low
+        out_ref[y, 8] = value
 
 
 def moment_kernel(steps_all, parts_ref, weight_ref, lags_ref, out_ref, context_ref):
@@ -405,13 +407,17 @@
     square = jnp.zeros((8, 128), F32)
     for part in range(2):
         errors = residuals(
-            lambda j: context_ref[16 + 16 * part + j], 16, first + 2048 * part, steps_all, lags_ref, weight_ref
+            lambda j: context_ref[16 + 16 * part + j], ((0, 16),), first + 2048 * part, steps_all, lags_ref, weight_ref
         )
-        for error in errors:
+        for error in errors.values():
             square = square + error * error
     pair = fold_rows(AR * square)
     last = iota((8, 128), 0) == 6
-    packed = pair_tree([(parts_ref[y, 8], parts_ref[y, 9]) for y in range(8)])
+    half = iota((8, 128), 1) < 64
+    packed = pair_tree([
+        (jnp.where(half, value, 0.0), jnp.where(half, pltpu.roll(value, 64, axis=1), 0.0))
+        for value in (parts_ref[y, 8] for y in range(8))
+    ])
     packed = pair_add(packed, (jnp.where(last, pair[0], 0.0), jnp.where(last, pair[1], 0.0)))
     packed = lane_sum(packed)
     lane = iota((8, 128), 1)
@@ -507,7 +513,6 @@
     near = neighbour(plane)
     gathered = lax.all_to_all(solved, ("ty", "tz"), 0, 0).reshape(64, 128)
     gathered, near = lax.optimization_barrier((gathered, near))
-    gathered, near = lax.optimization_barrier((gathered, near))
     factors, normal = call(
         functools.partial(normal_kernel, 1.0 / cells_all),
         (struct(cells, 64), struct(64, 896)),
@@ -540,7 +545,7 @@
     u2, own2 = image(plane, near, wide1, theta)
     near = lax.ppermute(own2, "tz", [(z, (z + 1) % 8) for z in range(8)])
     wide2 = lax.all_to_all(u2, "series", 0, 0)
-    parts = call(product_kernel, struct(8, 10, 8, 128), (wide2, h, own0, own1, own2, near))
+    parts = call(product_kernel, struct(8, 9, 8, 128), (wide2, h, own0, own1, own2, near))
     parts = lax.all_to_all(parts, "ty", 0, 0)
     moments = call(
         functools.partial(moment_kernel, steps_all), struct(64, 1, 128), (parts, weight, lags), (context,)

time: 176 us -> 175 us (level)
  no operation moved by 1% of the time
where the time goes in v7:
time: 175 us; the launch traced here: 174 us
  blocking collectives  112 us (64%)
  starting transfers between devices  30.5 us (17%)
  waiting for transfers between devices  15.5 us (9%)
  Pallas kernels  14 us (8%)
  local copies, waits for them, and re-layouts  2.23 us (1%)
    all_to_all x2, blocking collectives, per_device(): parts = lax.all_to_all(parts, 'ty', 0, 0)  34.1 us
    all_to_all x2, blocking collectives, exchange(): return (plane, neighbour(plane), lax.all_to_all(spread, 'series', 0, 0))  20.5 us
    all_to_all x2, blocking collectives, exchange(): plane = lax.all_to_all(spread, 'ty', 0, 0).reshape(32, 8, 128)  20.3 us
    all_to_all x1, blocking collectives, per_device(): parts = lax.all_to_all(parts, 'tz', 0, 0)  20.2 us
    all_to_all x1, blocking collectives, per_device(): gathered = lax.all_to_all(solved, ('ty', 'tz'), 0, 0).reshape(64, 128)  16.5 us
    pallas_call x11, Pallas kernels, call(): pl.pallas_call(kernel, out_shape=outs, in_specs=specs, out_specs=jax.tree...  14 us
    all_to_all x1, starting transfers between devices, per_device(): sums = lax.all_to_all(normal.reshape(8, 8, 896), 'series', 0, 0)  8.83 us
    all_to_all x1, starting transfers between devices, per_device(): moments = lax.all_to_all(moments, ('series', 'tz'), 0, 0).reshape(64, 128)  8.78 us
  transfers between devices with their start and end apart: 7, of which 3 were waited for; matrix products, arithmetic and copies ran while one was open for 1% of the time, Pallas kernels for 1%

profile of v7, /device:TPU:1, one launch (start us, length us, event | category | flops | bytes accessed | tf_op | source)
XLA Modules:
  0.0 174.4 jit_solution(5616613797285154372)
XLA Ops:
  0.6 2.8 %shard_map.68 = f32[8,112,128]{2,1,0:T(8,128)} custom-call(f32[128,512]{1,0:T(8,128)} %panel_ref.1, s32[4,128]{1,0:T(4,128)} %bitcast.14, f32[64,512]{1,0:T(8,128)} %x_ref.3), custom_call_target="tpu_custom_call" | custom-call | tf_op jit(solution)/shard_map/pallas_call | solution.py:34
  3.4 20.3 %all_to_all.55.parts_ref = f32[8,112,128]{2,1,0:T(8,128)S(1)} all-to-all(f32[8,112,128]{2,1,0:T(8,128)} %shard_map.68), channel_id=1, replica_groups=mesh['series'=8,'tz'=8,'ty'=8] {'ty'}, dimensions={0} | all-to-all | bytes 917504 | tf_op jit(solution)/shard_map/all_to_all | solution.py:508
  23.7 0.5 shard_map.69
  24.2 20.2 %all_to_all.56.parts_ref = f32[8,40,128]{2,1,0:T(8,128)S(1)} all-to-all(f32[8,40,128]{2,1,0:T(8,128)S(1)} %get-tuple-element.20), channel_id=1, replica_groups=mesh['series'=8,'tz'=8,'ty'=8] {'tz'}, dimensions={0} | all-to-all | bytes 327680 | tf_op jit(solution)/shard_map/all_to_all | solution.py:510
  44.4 1.7 shard_map.70
  46.2 2.1 %collective-permute-start = (f32[32,8,128]{2,1,0:T(8,128)S(1)}, f32[32,8,128]{2,1,0:T(8,128)S(1)}, u32[]{:S(2)}, u32[]{:S(2)}) collective-permute-start(f32[32,8,128]{2,1,0:T(8,128)S(1)} %get-tuple-element.23.plane_ref), channel_id=1, source_target_pairs={{0,8},{1,9},{2,10},{3,11},{4,60},{5,61},{6,62},{7,63},{8,16},{9,17... | collective-permute-start | bytes 393224 | tf_op jit(solution)/shard_map/ppermute | solution.py:476
  48.3 16.5 %all_to_all.57 = f32[64,1,128]{2,1,0:T(1,128)S(1)} all-to-all(f32[64,1,128]{2,1,0:T(1,128)S(1)} %shard_map.70), channel_id=1, replica_groups=mesh['series'=8,'tz'=8,'ty'=8] {'ty','tz'}, dimensions={0} | all-to-all | bytes 65536 | tf_op jit(solution)/shard_map/all_to_all | solution.py:514
  64.8 1.4 shard_map.71
  66.1 8.8 %all-to-all-start.3 = ((f32[8,8,896]{2,1,0:T(8,128)}), f32[8,8,896]{2,1,0:T(8,128)S(1)}, u32[]{:S(2)}, u32[]{:S(2)}) async-start(f32[8,8,896]{2,1,0:T(8,128)} %bitcast.2), calls=%async_computation.3 | async-start | bytes 458752 | tf_op jit(solution)/shard_map/all_to_all | solution.py:521
  74.9 0.7 copy-done.4
  75.9 0.6 copy-done.3
  76.5 1.1 shard_map.72
  77.6 3.6 %all-to-all-done.3.sums_ref = f32[8,8,896]{2,1,0:T(8,128)S(1)} async-done(((f32[8,8,896]{2,1,0:T(8,128)}), f32[8,8,896]{2,1,0:T(8,128)S(1)}, u32[]{:S(2)}, u32[]{:S(2)}) %all-to-all-start.3) | async-done | bytes 229408 | tf_op jit(solution)/shard_map/all_to_all | solution.py:521
  81.1 0.3 shard_map.73
  81.4 10.1 %all_to_all.58 = f32[8,4,8,128]{3,2,1,0:T(8,128)S(1)} all-to-all(f32[8,4,8,128]{3,2,1,0:T(8,128)S(1)} %get-tuple-element.30), channel_id=1, replica_groups=mesh['series'=8,'tz'=8,'ty'=8] {'ty'}, dimensions={0} | all-to-all | bytes 262144 | tf_op jit(solution)/shard_map/all_to_all | solution.py:480
  91.6 2.2 %collective-permute-start.1 = (f32[32,8,128]{2,1,0:T(8,128)S(1)}, f32[32,8,128]{2,1,0:T(8,128)S(1)}, u32[]{:S(2)}, u32[]{:S(2)}) collective-permute-start(f32[32,8,128]{2,1,0:T(8,128)S(1)} %bitcast.8), channel_id=1, source_target_pairs={{0,8},{1,9},{2,10},{3,11},{4,60},{5,61},{6,62},{7,63},{8,16},{9,17... | collective-permute-start | bytes 393224 | tf_op jit(solution)/shard_map/ppermute | solution.py:476
  93.8 10.2 %all_to_all.59.wide_ref.wide0_ref = f32[8,4,8,128]{3,2,1,0:T(8,128)S(1)} all-to-all(f32[8,4,8,128]{3,2,1,0:T(8,128)S(1)} %get-tuple-element.30), channel_id=1, replica_groups=mesh['series'=8,'tz'=8,'ty'=8] {'series'}, dimensions={0} | all-to-all | bytes 262144 | tf_op jit(solution)/shard_map/all_to_all | solution.py:481
  104.0 1.1 shard_map.74
  105.1 10.1 %all_to_all.60 = f32[8,4,8,128]{3,2,1,0:T(8,128)S(1)} all-to-all(f32[8,4,8,128]{3,2,1,0:T(8,128)S(1)} %get-tuple-element.33), channel_id=1, replica_groups=mesh['series'=8,'tz'=8,'ty'=8] {'ty'}, dimensions={0} | all-to-all | bytes 262144 | tf_op jit(solution)/shard_map/all_to_all | solution.py:480
  115.3 2.2 %collective-permute-start.2 = (f32[32,8,128]{2,1,0:T(8,128)S(1)}, f32[32,8,128]{2,1,0:T(8,128)S(1)}, u32[]{:S(2)}, u32[]{:S(2)}) collective-permute-start(f32[32,8,128]{2,1,0:T(8,128)S(1)} %bitcast.10), channel_id=1, source_target_pairs={{0,8},{1,9},{2,10},{3,11},{4,60},{5,61},{6,62},{7,63},{8,16},{9,17... | collective-permute-start | bytes 393224 | tf_op jit(solution)/shard_map/ppermute | solution.py:476
  117.5 10.2 %all_to_all.61.wide_ref.wide1_ref = f32[8,4,8,128]{3,2,1,0:T(8,128)S(1)} all-to-all(f32[8,4,8,128]{3,2,1,0:T(8,128)S(1)} %get-tuple-element.33), channel_id=1, replica_groups=mesh['series'=8,'tz'=8,'ty'=8] {'series'}, dimensions={0} | all-to-all | bytes 262144 | tf_op jit(solution)/shard_map/all_to_all | solution.py:481
  127.7 1.8 %shard_map.75 = (f32[8,4,8,128]{3,2,1,0:T(8,128)}, f32[4,8,128]{2,1,0:T(8,128)S(1)}) custom-call(f32[32,8,128]{2,1,0:T(8,128)S(1)} %bitcast.11, f32[32,8,128]{2,1,0:T(8,128)S(1)} %collective-permute-done.2.near_ref, f32[8,4,8,128]{3,2,1,0:T(8,128)S(1)} %all_to_all.61.wide_ref.wide1_ref, f32[4,8,64]{2,1,0:T(8,128)S(1)} %get-tuple-element.31.h_ref, ...), custom_call_target="tpu_custom_call" | custom-call | tf_op jit(solution)/shard_map/pallas_call | solution.py:34
  129.5 4.1 %all-to-all-start.8 = ((f32[8,4,8,128]{3,2,1,0:T(8,128)}), f32[8,4,8,128]{3,2,1,0:T(8,128)S(1)}, u32[]{:S(2)}, u32[]{:S(2)}) async-start(f32[8,4,8,128]{3,2,1,0:T(8,128)} %get-tuple-element.34), calls=%async_computation.8 | async-start | bytes 262144 | tf_op jit(solution)/shard_map/all_to_all | solution.py:547
  133.6 2.2 %collective-permute-start.3 = (f32[4,8,128]{2,1,0:T(8,128)S(1)}, f32[4,8,128]{2,1,0:T(8,128)S(1)}, u32[]{:S(2)}, u32[]{:S(2)}) collective-permute-start(f32[4,8,128]{2,1,0:T(8,128)S(1)} %get-tuple-element.37.u2_ref), channel_id=1, source_target_pairs={{0,8},{8,16},{16,24},{24,32},{32,40},{40,48},{48,56},{56,0},{1,9},... | collective-permute-start | bytes 49160 | tf_op jit(solution)/shard_map/ppermute | solution.py:546
  135.9 3.5 %collective-permute-done.3.near_ref = f32[4,8,128]{2,1,0:T(8,128)S(1)} collective-permute-done((f32[4,8,128]{2,1,0:T(8,128)S(1)}, f32[4,8,128]{2,1,0:T(8,128)S(1)}, u32[]{:S(2)}, u32[]{:S(2)}) %collective-permute-start.3) | collective-permute-done | bytes 16416 | tf_op jit(solution)/shard_map/ppermute | solution.py:546
  139.4 0.3 shard_map.76
  139.7 13.8 %all_to_all.62.parts_ref = f32[8,9,8,128]{3,2,1,0:T(8,128)S(1)} all-to-all(f32[8,9,8,128]{3,2,1,0:T(8,128)S(1)} %shard_map.76), channel_id=1, replica_groups=mesh['series'=8,'tz'=8,'ty'=8] {'ty'}, dimensions={0} | all-to-all | bytes 589824 | tf_op jit(solution)/shard_map/all_to_all | solution.py:549
  153.5 2.0 %shard_map.77 = f32[64,1,128]{2,1,0:T(1,128)} custom-call(f32[8,9,8,128]{3,2,1,0:T(8,128)S(1)} %all_to_all.62.parts_ref, f32[14,8,128]{2,1,0:T(8,128)S(1)} %broadcast_in_dim.2.weight_ref, s32[14]{0:T(128)S(1)} %copy-done.3), custom_call_target="tpu_custom_call" | custom-call | tf_op jit(solution)/shard_map/pallas_call | solution.py:34
  155.5 8.8 %all-to-all-start.10 = ((f32[64,1,128]{2,1,0:T(1,128)}), f32[64,1,128]{2,1,0:T(1,128)S(1)}, u32[]{:S(2)}, u32[]{:S(2)}) async-start(f32[64,1,128]{2,1,0:T(1,128)} %shard_map.77), calls=%async_computation.10 | async-start | bytes 65536 | tf_op jit(solution)/shard_map/all_to_all | solution.py:553
  164.3 0.7 copy.12
  165.0 8.4 %all-to-all-done.10 = f32[64,1,128]{2,1,0:T(1,128)S(1)} async-done(((f32[64,1,128]{2,1,0:T(1,128)}), f32[64,1,128]{2,1,0:T(1,128)S(1)}, u32[]{:S(2)}, u32[]{:S(2)}) %all-to-all-start.10) | async-done | bytes 32800 | tf_op jit(solution)/shard_map/all_to_all | solution.py:553
  173.4 1.0 shard_map.78
  (15 shorter events, 0.3 us)
Async XLA Ops:
  24.2 40.5 %copy-start.1 = (f32[128,512]{1,0:T(8,128)S(1)}, f32[128,512]{1,0:T(8,128)}, u32[]{:S(2)}) copy-start(f32[128,512]{1,0:T(8,128)} %panel_ref.1) | copy-start | bytes 786436
  46.2 18.6 %collective-permute-start = (f32[32,8,128]{2,1,0:T(8,128)S(1)}, f32[32,8,128]{2,1,0:T(8,128)S(1)}, u32[]{:S(2)}, u32[]{:S(2)}) collective-permute-start(f32[32,8,128]{2,1,0:T(8,128)S(1)} %get-tuple-element.23.plane_ref), channel_id=1, source_target_pairs={{0,8},{1,9},{2,10},{3,11},{4,60},{5,61},{6,62},{7,63},{8,16},{9,17... | collective-permute-start | bytes 393224 | tf_op jit(solution)/shard_map/ppermute | solution.py:476
  48.3 16.5 %copy-start.2 = (s32[128,4]{0,1:T(4,128)S(1)}, s32[128,4]{0,1:T(4,128)}, u32[]{:S(2)}) copy-start(s32[128,4]{0,1:T(4,128)} %param.6) | copy-start | bytes 6148
  66.1 15.0 %all-to-all-start.3 = ((f32[8,8,896]{2,1,0:T(8,128)}), f32[8,8,896]{2,1,0:T(8,128)S(1)}, u32[]{:S(2)}, u32[]{:S(2)}) async-start(f32[8,8,896]{2,1,0:T(8,128)} %bitcast.2), calls=%async_computation.3 | async-start | bytes 458752 | tf_op jit(solution)/shard_map/all_to_all | solution.py:521
  74.9 0.7 copy-start.4
  75.8 0.7 copy-start.3
  76.5 4.7 %copy-start = (f32[64,512]{1,0:T(8,128)S(1)}, f32[64,512]{1,0:T(8,128)}, u32[]{:S(2)}) copy-start(f32[64,512]{1,0:T(8,128)} %x_ref.3) | copy-start | bytes 393220
  91.6 12.5 %collective-permute-start.1 = (f32[32,8,128]{2,1,0:T(8,128)S(1)}, f32[32,8,128]{2,1,0:T(8,128)S(1)}, u32[]{:S(2)}, u32[]{:S(2)}) collective-permute-start(f32[32,8,128]{2,1,0:T(8,128)S(1)} %bitcast.8), channel_id=1, source_target_pairs={{0,8},{1,9},{2,10},{3,11},{4,60},{5,61},{6,62},{7,63},{8,16},{9,17... | collective-permute-start | bytes 393224 | tf_op jit(solution)/shard_map/ppermute | solution.py:476
  115.3 12.4 %collective-permute-start.2 = (f32[32,8,128]{2,1,0:T(8,128)S(1)}, f32[32,8,128]{2,1,0:T(8,128)S(1)}, u32[]{:S(2)}, u32[]{:S(2)}) collective-permute-start(f32[32,8,128]{2,1,0:T(8,128)S(1)} %bitcast.10), channel_id=1, source_target_pairs={{0,8},{1,9},{2,10},{3,11},{4,60},{5,61},{6,62},{7,63},{8,16},{9,17... | collective-permute-start | bytes 393224 | tf_op jit(solution)/shard_map/ppermute | solution.py:476
  129.5 9.9 %all-to-all-start.8 = ((f32[8,4,8,128]{3,2,1,0:T(8,128)}), f32[8,4,8,128]{3,2,1,0:T(8,128)S(1)}, u32[]{:S(2)}, u32[]{:S(2)}) async-start(f32[8,4,8,128]{3,2,1,0:T(8,128)} %get-tuple-element.34), calls=%async_computation.8 | async-start | bytes 262144 | tf_op jit(solution)/shard_map/all_to_all | solution.py:547
  133.6 5.8 %collective-permute-start.3 = (f32[4,8,128]{2,1,0:T(8,128)S(1)}, f32[4,8,128]{2,1,0:T(8,128)S(1)}, u32[]{:S(2)}, u32[]{:S(2)}) collective-permute-start(f32[4,8,128]{2,1,0:T(8,128)S(1)} %get-tuple-element.37.u2_ref), channel_id=1, source_target_pairs={{0,8},{8,16},{16,24},{24,32},{32,40},{40,48},{48,56},{56,0},{1,9},... | collective-permute-start | bytes 49160 | tf_op jit(solution)/shard_map/ppermute | solution.py:546
  155.5 17.9 %all-to-all-start.10 = ((f32[64,1,128]{2,1,0:T(1,128)}), f32[64,1,128]{2,1,0:T(1,128)S(1)}, u32[]{:S(2)}, u32[]{:S(2)}) async-start(f32[64,1,128]{2,1,0:T(1,128)} %shard_map.77), calls=%async_computation.10 | async-start | bytes 65536 | tf_op jit(solution)/shard_map/all_to_all | solution.py:553

commit v8 on v7

--- a/solution.py
+++ b/solution.py
@@ -18,7 +18,6 @@
 F32 = jnp.float32
 VMEM = pl.BlockSpec(memory_space=pltpu.VMEM)
 HBM = pl.BlockSpec(memory_space=pltpu.HBM)
-SMEM = pl.BlockSpec(memory_space=pltpu.SMEM)
 
 
 def struct(*shape):
@@ -30,11 +29,10 @@
 
 
 def call(kernel, outs, ins, scratch=(), place=VMEM, room=32):
-    specs = [SMEM if a.dtype == jnp.int32 and a.ndim == 1 else place for a in ins]
     return pl.pallas_call(
         kernel,
         out_shape=outs,
-        in_specs=specs,
+        in_specs=[place] * len(ins),
         out_specs=jax.tree.map(lambda _: VMEM, outs),
         scratch_shapes=list(scratch),
         compiler_params=pltpu.CompilerParams(vmem_limit_bytes=room * 1024 * 1024),
@@ -181,13 +179,14 @@
         pair = gathered_ref[8 * y : 8 * y + 8, :]
         pieces += [pair[:, 0:64], pair[:, 64:128]]
     factors = jnp.concatenate(pieces, axis=0)
-    factors_ref[...] = factors
+    turned = factors.T
+    factors_ref[...] = turned
     flags = columns_of(obs_ref)
     right = [panel_ref[:, b * TILE : (b + 1) * TILE] * flags[:, b : b + 1] for b in range(4)]
     for b in (0, 2):
         right.append(jnp.concatenate([factors * flags[:, b : b + 1], factors * flags[:, b + 1 : b + 2]], axis=1))
     right.append(factors)
-    product = scale * dot(factors, jnp.concatenate(right, axis=1), ((0,), (0,)))
+    product = scale * dot(turned, jnp.concatenate(right, axis=1), ((1,), (0,)))
     out_ref[:, 0:768] = product[:, 0:768]
     gram = product[:, 768:832]
     norm = jnp.sum(gram * gram)
@@ -196,11 +195,15 @@
     out_ref[:, 768:896] = jnp.where(some > 0.0, norm / jnp.where(some > 0.0, some, 1.0), 0.0)
 
 
-def lagged(read, chunks, lags_ref, weight_ref, ahead):
+def scalars(lags_ref):
+    return [jnp.max(lags_ref[index : index + 1, :]) for index in range(LAGS)]
+
+
+def lagged(read, chunks, lags, weight_ref, ahead):
     lane = iota((8, 128), 1)
     sums = {}
     for index in range(LAGS):
-        lag = lags_ref[index]
+        lag = lags[index]
         if ahead:
             start = lag // 128
             shift = lag % 128
@@ -222,8 +225,8 @@
     return sums
 
 
-def residuals(read, chunks, first_step, steps_all, lags_ref, weight_ref):
-    past = lagged(read, chunks, lags_ref, weight_ref, False)
+def residuals(read, chunks, first_step, steps_all, lags, weight_ref):
+    past = lagged(read, chunks, lags, weight_ref, False)
     lane = iota((8, 128), 1)
     out = {}
     for j, value in past.items():
@@ -232,11 +235,11 @@
     return out
 
 
-def ar_part(read, first_step, steps_all, lags_ref, weight_ref, errors_ref):
-    errors = residuals(read, ((0, 8), (15, 20)), first_step, steps_all, lags_ref, weight_ref)
+def ar_part(read, first_step, steps_all, lags, weight_ref, errors_ref):
+    errors = residuals(read, ((0, 8), (15, 20)), first_step, steps_all, lags, weight_ref)
     for j, value in errors.items():
         errors_ref[j] = value
-    later = lagged(lambda j: errors_ref[j], ((0, 4),), lags_ref, weight_ref, True)
+    later = lagged(lambda j: errors_ref[j], ((0, 4),), lags, weight_ref, True)
     return [errors[j] - later[j] for j in range(4)]
 
 
@@ -248,9 +251,10 @@
 def drift_kernel(
     steps_all, plane_ref, near_ref, weight_ref, all_ref, lags_ref, out_ref, theta_ref, context_ref, errors_ref
 ):
+    lags = scalars(lags_ref)
     slab, y = place()
     read = fill_context(plane_ref, near_ref, context_ref, y)
-    back = ar_part(read, slab * 512, steps_all, lags_ref, weight_ref, errors_ref)
+    back = ar_part(read, slab * 512, steps_all, lags, weight_ref, errors_ref)
     for q in range(4):
         out_ref[q] = RIDGE_TIME * read(q) + AR * back[q]
     squares = all_ref[...] * all_ref[...]
@@ -293,9 +297,10 @@
     steps_all, plane_ref, near_ref, wide_ref, h_ref, weight_ref, theta_ref, lags_ref,
     out_ref, own_ref, context_ref, errors_ref,
 ):
+    lags = scalars(lags_ref)
     slab, y = place()
     read = fill_context(plane_ref, near_ref, context_ref, y)
-    back = ar_part(read, slab * 512, steps_all, lags_ref, weight_ref, errors_ref)
+    back = ar_part(read, slab * 512, steps_all, lags, weight_ref, errors_ref)
     theta = theta_ref[...]
     for q in range(4):
         own = read(q)
@@ -397,27 +402,45 @@
         out_ref[y, 8] = value
 
 
-def moment_kernel(steps_all, parts_ref, weight_ref, lags_ref, out_ref, context_ref):
-    for y in range(8):
-        for q in range(4):
-            context_ref[16 + 4 * y + q] = parts_ref[y, q]
-            if y >= 4:
-                context_ref[4 * (y - 4) + q] = parts_ref[y, 4 + q]
-    first = lax.axis_index("tz") * 4096
-    square = jnp.zeros((8, 128), F32)
-    for part in range(2):
-        errors = residuals(
-            lambda j: context_ref[16 + 16 * part + j], ((0, 16),), first + 2048 * part, steps_all, lags_ref, weight_ref
-        )
-        for error in errors.values():
-            square = square + error * error
-    pair = fold_rows(AR * square)
-    last = iota((8, 128), 0) == 6
+def moment_kernel(steps_all, parts_ref, weight_ref, lags_ref, out_ref, stack_ref):
+    starts = [512 - lag for lag in scalars(lags_ref)[: LAGS - 1]]
+    lane = iota((128, 128), 1)
+    none = jnp.zeros((64, 128), F32)
+
+    def moved(runs, main, halo):
+        return pltpu.roll(jnp.where(lane >= 128 - 8 * runs, halo, main), 8 * runs, axis=1)
+
+    far = []
+    for j in range(2):
+        main = jnp.concatenate([parts_ref[s // 2, 2 * (s % 2) + j] for s in range(16)], axis=0).T
+        halo = [parts_ref[4 + s // 2, 4 + 2 * (s % 2) + j] for s in range(8)]
+        halo = jnp.concatenate([none] + halo, axis=0).T
+        at = 128 * j
+        stack_ref[512 + at : 640 + at, :] = main
+        stack_ref[256 + at : 384 + at, :] = moved(1, main, halo)
+        stack_ref[at : 128 + at, :] = moved(2, main, halo)
+        far.append(moved(8, main, halo))
+        if j == 0:
+            end = moved(7, main, halo)[0:32]
+    far = jnp.concatenate([far[0][32:128], far[1], end], axis=0)
     half = iota((8, 128), 1) < 64
     packed = pair_tree([
         (jnp.where(half, value, 0.0), jnp.where(half, pltpu.roll(value, 64, axis=1), 0.0))
         for value in (parts_ref[y, 8] for y in range(8))
     ])
+    step = lax.axis_index("tz") * 4096 + iota((8, 128), 1) // 8 * 256 + iota((8, 128), 0)
+    square = jnp.zeros((8, 128), F32)
+    own = iota((8, 128), 0) == iota((8, 128), 1) % 8
+    weights = [jnp.sum(jnp.where(own, weight_ref[index], 0.0), axis=0, keepdims=True) for index in range(LAGS)]
+    for r in range(0, 256, 8):
+        past = weights[LAGS - 1] * far[r : r + 8]
+        for index in range(LAGS - 1):
+            past = past + weights[index] * stack_ref[pl.ds(starts[index] + r, 8), :]
+        valid = (step + r >= LONGEST) & (step + r < steps_all)
+        error = jnp.where(valid, stack_ref[512 + r : 520 + r, :] - past, 0.0)
+        square = square + error * error
+    pair = fold_rows(AR * square)
+    last = iota((8, 128), 0) == 6
     packed = pair_add(packed, (jnp.where(last, pair[0], 0.0), jnp.where(last, pair[1], 0.0)))
     packed = lane_sum(packed)
     lane = iota((8, 128), 1)
@@ -489,7 +512,9 @@
     own_weight = lax.dynamic_slice_in_dim(ar_weight, 8 * series, 8, 0)
     weight = jnp.broadcast_to(own_weight.T[:, :, None], (LAGS, 8, 128))
     observed = observed.T
+    lags = jnp.broadcast_to(lags[:, None], (LAGS, 128))
     context = pltpu.VMEM((48, 8, 128), F32)
+    stack = pltpu.VMEM((768, 128), F32)
     errors = pltpu.VMEM((20, 8, 128), F32)
 
     parts = call(
@@ -515,7 +540,7 @@
     gathered, near = lax.optimization_barrier((gathered, near))
     factors, normal = call(
         functools.partial(normal_kernel, 1.0 / cells_all),
-        (struct(cells, 64), struct(64, 896)),
+        (struct(64, cells), struct(64, 896)),
         (gathered, panel, observed),
     )
     sums = lax.all_to_all(normal.reshape(8, 8, 896), "series", 0, 0)
@@ -548,11 +573,11 @@
     parts = call(product_kernel, struct(8, 9, 8, 128), (wide2, h, own0, own1, own2, near))
     parts = lax.all_to_all(parts, "ty", 0, 0)
     moments = call(
-        functools.partial(moment_kernel, steps_all), struct(64, 1, 128), (parts, weight, lags), (context,)
+        functools.partial(moment_kernel, steps_all), struct(64, 1, 128), (parts, weight, lags), (stack,)
     )
     moments = lax.all_to_all(moments, ("series", "tz"), 0, 0).reshape(64, 128)
     result = call(finish_kernel, struct(64, 512), (moments, first, theta, start_time, wide0, wide1, wide2))
-    return (factors, result)
+    return (factors.T, result)
 
 
 def solution(mesh):

time: 175 us -> 173 us (0.989)
  blocking collectives: 112 us -> 129 us
  starting transfers between devices: 30.5 us -> 21.7 us
  waiting for transfers between devices: 15.5 us -> 7.31 us
  Pallas kernels: 14 us -> 11.9 us
    all_to_all x0 -> x1, blocking collectives: none -> 17.8 us  [per_device(): moments = lax.all_to_all(moments, ('series', 'tz'), 0, 0).reshape(64, 128)]
    all_to_all x1 -> x0, starting transfers between devices: 8.78 us -> none  [per_device(): moments = lax.all_to_all(moments, ('series', 'tz'), 0, 0).reshape(64, 128)]
    all_to_all x1 -> x0, waiting for transfers between devices: 8.43 us -> none  [per_device(): moments = lax.all_to_all(moments, ('series', 'tz'), 0, 0).reshape(64, 128)]
    pallas_call x11, Pallas kernels: 14 us -> 11.9 us  [call(): pl.pallas_call(kernel, out_shape=outs, in_specs=[place] * len(ins), out_s...]
  transfers between devices with their start and end apart: 7 -> 6, of which waited for: 3 -> 2; matrix products, arithmetic and copies ran while one was open for 1% -> 0% of each run, Pallas kernels for 1% -> 0%
where the time goes in v8:
time: 173 us
  blocking collectives  129 us (75%)
  starting transfers between devices  21.7 us (13%)
  Pallas kernels  11.9 us (7%)
  waiting for transfers between devices  7.31 us (4%)
    all_to_all x2, blocking collectives, per_device(): parts = lax.all_to_all(parts, 'ty', 0, 0)  34.1 us
    all_to_all x2, blocking collectives, exchange(): return (plane, neighbour(plane), lax.all_to_all(spread, 'series', 0, 0))  20.5 us
    all_to_all x2, blocking collectives, exchange(): plane = lax.all_to_all(spread, 'ty', 0, 0).reshape(32, 8, 128)  20.3 us
    all_to_all x1, blocking collectives, per_device(): parts = lax.all_to_all(parts, 'tz', 0, 0)  20.2 us
    all_to_all x1, blocking collectives, per_device(): moments = lax.all_to_all(moments, ('series', 'tz'), 0, 0).reshape(64, 128)  17.8 us
    all_to_all x1, blocking collectives, per_device(): gathered = lax.all_to_all(solved, ('ty', 'tz'), 0, 0).reshape(64, 128)  16.5 us
    pallas_call x11, Pallas kernels, call(): pl.pallas_call(kernel, out_shape=outs, in_specs=[place] * len(ins), out_s...  11.9 us
    all_to_all x1, starting transfers between devices, per_device(): sums = lax.all_to_all(normal.reshape(8, 8, 896), 'series', 0, 0)  8.83 us
  transfers between devices with their start and end apart: 6, of which 2 were waited for; matrix products, arithmetic and copies ran while one was open for 0% of the time, Pallas kernels for 0%

profile of v8, /device:TPU:1, one launch (start us, length us, event | category | flops | bytes accessed | tf_op | source)
XLA Modules:
  0.0 172.6 jit_solution(14147103210393218316)
XLA Ops:
  0.6 2.8 %shard_map.68 = f32[8,112,128]{2,1,0:T(8,128)} custom-call(f32[128,512]{1,0:T(8,128)} %panel_ref.1, s32[4,128]{1,0:T(4,128)} %bitcast.15, f32[64,512]{1,0:T(8,128)} %x_ref.3), custom_call_target="tpu_custom_call" | custom-call | tf_op jit(solution)/shard_map/pallas_call | solution.py:32
  3.4 20.3 %all_to_all.55.parts_ref = f32[8,112,128]{2,1,0:T(8,128)S(1)} all-to-all(f32[8,112,128]{2,1,0:T(8,128)} %shard_map.68), channel_id=1, replica_groups=mesh['series'=8,'tz'=8,'ty'=8] {'ty'}, dimensions={0} | all-to-all | bytes 917504 | tf_op jit(solution)/shard_map/all_to_all | solution.py:533
  23.7 0.5 shard_map.69
  24.2 20.2 %all_to_all.56.parts_ref = f32[8,40,128]{2,1,0:T(8,128)S(1)} all-to-all(f32[8,40,128]{2,1,0:T(8,128)S(1)} %get-tuple-element.20), channel_id=1, replica_groups=mesh['series'=8,'tz'=8,'ty'=8] {'tz'}, dimensions={0} | all-to-all | bytes 327680 | tf_op jit(solution)/shard_map/all_to_all | solution.py:535
  44.4 1.7 shard_map.70
  46.2 2.1 %collective-permute-start = (f32[32,8,128]{2,1,0:T(8,128)S(1)}, f32[32,8,128]{2,1,0:T(8,128)S(1)}, u32[]{:S(2)}, u32[]{:S(2)}) collective-permute-start(f32[32,8,128]{2,1,0:T(8,128)S(1)} %get-tuple-element.23.plane_ref), channel_id=1, source_target_pairs={{0,8},{1,9},{2,10},{3,11},{4,60},{5,61},{6,62},{7,63},{8,16},{9,17... | collective-permute-start | bytes 393224 | tf_op jit(solution)/shard_map/ppermute | solution.py:499
  48.3 16.5 %all_to_all.57 = f32[64,1,128]{2,1,0:T(1,128)S(1)} all-to-all(f32[64,1,128]{2,1,0:T(1,128)S(1)} %shard_map.70), channel_id=1, replica_groups=mesh['series'=8,'tz'=8,'ty'=8] {'ty','tz'}, dimensions={0} | all-to-all | bytes 65536 | tf_op jit(solution)/shard_map/all_to_all | solution.py:539
  64.8 1.4 shard_map.71
  66.1 8.8 %all-to-all-start.3 = ((f32[8,8,896]{2,1,0:T(8,128)}), f32[8,8,896]{2,1,0:T(8,128)S(1)}, u32[]{:S(2)}, u32[]{:S(2)}) async-start(f32[8,8,896]{2,1,0:T(8,128)} %bitcast.3), calls=%async_computation.3 | async-start | bytes 458752 | tf_op jit(solution)/shard_map/all_to_all | solution.py:546
  75.0 0.7 copy-done.3
  75.6 0.1 copy.10.all_ref
  75.8 0.6 copy-done.4
  76.5 0.1 broadcast_in_dim.4.weight_ref
  76.5 0.8 shard_map.72
  77.4 3.8 %all-to-all-done.3.sums_ref = f32[8,8,896]{2,1,0:T(8,128)S(1)} async-done(((f32[8,8,896]{2,1,0:T(8,128)}), f32[8,8,896]{2,1,0:T(8,128)S(1)}, u32[]{:S(2)}, u32[]{:S(2)}) %all-to-all-start.3) | async-done | bytes 229408 | tf_op jit(solution)/shard_map/all_to_all | solution.py:546
  81.2 0.3 shard_map.73
  81.4 10.1 %all_to_all.58 = f32[8,4,8,128]{3,2,1,0:T(8,128)S(1)} all-to-all(f32[8,4,8,128]{3,2,1,0:T(8,128)S(1)} %get-tuple-element.30), channel_id=1, replica_groups=mesh['series'=8,'tz'=8,'ty'=8] {'ty'}, dimensions={0} | all-to-all | bytes 262144 | tf_op jit(solution)/shard_map/all_to_all | solution.py:503
  91.6 2.2 %collective-permute-start.1 = (f32[32,8,128]{2,1,0:T(8,128)S(1)}, f32[32,8,128]{2,1,0:T(8,128)S(1)}, u32[]{:S(2)}, u32[]{:S(2)}) collective-permute-start(f32[32,8,128]{2,1,0:T(8,128)S(1)} %bitcast.9), channel_id=1, source_target_pairs={{0,8},{1,9},{2,10},{3,11},{4,60},{5,61},{6,62},{7,63},{8,16},{9,17... | collective-permute-start | bytes 393224 | tf_op jit(solution)/shard_map/ppermute | solution.py:499
  93.8 10.2 %all_to_all.59.wide_ref.wide0_ref = f32[8,4,8,128]{3,2,1,0:T(8,128)S(1)} all-to-all(f32[8,4,8,128]{3,2,1,0:T(8,128)S(1)} %get-tuple-element.30), channel_id=1, replica_groups=mesh['series'=8,'tz'=8,'ty'=8] {'series'}, dimensions={0} | all-to-all | bytes 262144 | tf_op jit(solution)/shard_map/all_to_all | solution.py:504
  104.0 0.8 shard_map.74
  104.9 10.1 %all_to_all.60 = f32[8,4,8,128]{3,2,1,0:T(8,128)S(1)} all-to-all(f32[8,4,8,128]{3,2,1,0:T(8,128)S(1)} %get-tuple-element.33), channel_id=1, replica_groups=mesh['series'=8,'tz'=8,'ty'=8] {'ty'}, dimensions={0} | all-to-all | bytes 262144 | tf_op jit(solution)/shard_map/all_to_all | solution.py:503
  115.0 2.2 %collective-permute-start.2 = (f32[32,8,128]{2,1,0:T(8,128)S(1)}, f32[32,8,128]{2,1,0:T(8,128)S(1)}, u32[]{:S(2)}, u32[]{:S(2)}) collective-permute-start(f32[32,8,128]{2,1,0:T(8,128)S(1)} %bitcast.11), channel_id=1, source_target_pairs={{0,8},{1,9},{2,10},{3,11},{4,60},{5,61},{6,62},{7,63},{8,16},{9,17... | collective-permute-start | bytes 393224 | tf_op jit(solution)/shard_map/ppermute | solution.py:499
  117.2 10.2 %all_to_all.61.wide_ref.wide1_ref = f32[8,4,8,128]{3,2,1,0:T(8,128)S(1)} all-to-all(f32[8,4,8,128]{3,2,1,0:T(8,128)S(1)} %get-tuple-element.33), channel_id=1, replica_groups=mesh['series'=8,'tz'=8,'ty'=8] {'series'}, dimensions={0} | all-to-all | bytes 262144 | tf_op jit(solution)/shard_map/all_to_all | solution.py:504
  127.5 1.5 shard_map.75
  128.9 4.1 %all-to-all-start.8 = ((f32[8,4,8,128]{3,2,1,0:T(8,128)}), f32[8,4,8,128]{3,2,1,0:T(8,128)S(1)}, u32[]{:S(2)}, u32[]{:S(2)}) async-start(f32[8,4,8,128]{3,2,1,0:T(8,128)} %get-tuple-element.34), calls=%async_computation.8 | async-start | bytes 262144 | tf_op jit(solution)/shard_map/all_to_all | solution.py:572
  133.1 2.2 %collective-permute-start.3 = (f32[4,8,128]{2,1,0:T(8,128)S(1)}, f32[4,8,128]{2,1,0:T(8,128)S(1)}, u32[]{:S(2)}, u32[]{:S(2)}) collective-permute-start(f32[4,8,128]{2,1,0:T(8,128)S(1)} %get-tuple-element.37.u2_ref), channel_id=1, source_target_pairs={{0,8},{8,16},{16,24},{24,32},{32,40},{40,48},{48,56},{56,0},{1,9},... | collective-permute-start | bytes 49160 | tf_op jit(solution)/shard_map/ppermute | solution.py:571
  135.3 3.5 %collective-permute-done.3.near_ref = f32[4,8,128]{2,1,0:T(8,128)S(1)} collective-permute-done((f32[4,8,128]{2,1,0:T(8,128)S(1)}, f32[4,8,128]{2,1,0:T(8,128)S(1)}, u32[]{:S(2)}, u32[]{:S(2)}) %collective-permute-start.3) | collective-permute-done | bytes 16416 | tf_op jit(solution)/shard_map/ppermute | solution.py:571
  138.8 0.3 shard_map.76
  139.2 13.8 %all_to_all.62.parts_ref = f32[8,9,8,128]{3,2,1,0:T(8,128)S(1)} all-to-all(f32[8,9,8,128]{3,2,1,0:T(8,128)S(1)} %shard_map.76), channel_id=1, replica_groups=mesh['series'=8,'tz'=8,'ty'=8] {'ty'}, dimensions={0} | all-to-all | bytes 589824 | tf_op jit(solution)/shard_map/all_to_all | solution.py:574
  152.9 0.8 shard_map.77
  153.7 17.8 %all_to_all.63 = f32[64,1,128]{2,1,0:T(1,128)S(1)} all-to-all(f32[64,1,128]{2,1,0:T(1,128)S(1)} %shard_map.77), channel_id=1, replica_groups=mesh['series'=8,'tz'=8,'ty'=8] {'series','tz'}, dimensions={0} | all-to-all | bytes 65536 | tf_op jit(solution)/shard_map/all_to_all | solution.py:578
  171.5 1.0 shard_map.78
  (14 shorter events, 0.2 us)
Async XLA Ops:
  24.2 40.5 %copy-start.1 = (f32[128,512]{1,0:T(8,128)S(1)}, f32[128,512]{1,0:T(8,128)}, u32[]{:S(2)}) copy-start(f32[128,512]{1,0:T(8,128)} %panel_ref.1) | copy-start | bytes 786436
  46.2 18.6 %collective-permute-start = (f32[32,8,128]{2,1,0:T(8,128)S(1)}, f32[32,8,128]{2,1,0:T(8,128)S(1)}, u32[]{:S(2)}, u32[]{:S(2)}) collective-permute-start(f32[32,8,128]{2,1,0:T(8,128)S(1)} %get-tuple-element.23.plane_ref), channel_id=1, source_target_pairs={{0,8},{1,9},{2,10},{3,11},{4,60},{5,61},{6,62},{7,63},{8,16},{9,17... | collective-permute-start | bytes 393224 | tf_op jit(solution)/shard_map/ppermute | solution.py:499
  48.3 16.5 %copy-start.2 = (s32[128,4]{0,1:T(4,128)S(1)}, s32[128,4]{0,1:T(4,128)}, u32[]{:S(2)}) copy-start(s32[128,4]{0,1:T(4,128)} %param.6) | copy-start | bytes 6148
  66.1 15.0 %all-to-all-start.3 = ((f32[8,8,896]{2,1,0:T(8,128)}), f32[8,8,896]{2,1,0:T(8,128)S(1)}, u32[]{:S(2)}, u32[]{:S(2)}) async-start(f32[8,8,896]{2,1,0:T(8,128)} %bitcast.3), calls=%async_computation.3 | async-start | bytes 458752 | tf_op jit(solution)/shard_map/all_to_all | solution.py:546
  75.0 0.7 copy-start.3
  75.7 0.7 copy-start.4
  76.5 4.6 %copy-start = (f32[64,512]{1,0:T(8,128)S(1)}, f32[64,512]{1,0:T(8,128)}, u32[]{:S(2)}) copy-start(f32[64,512]{1,0:T(8,128)} %x_ref.3) | copy-start | bytes 393220
  91.6 12.5 %collective-permute-start.1 = (f32[32,8,128]{2,1,0:T(8,128)S(1)}, f32[32,8,128]{2,1,0:T(8,128)S(1)}, u32[]{:S(2)}, u32[]{:S(2)}) collective-permute-start(f32[32,8,128]{2,1,0:T(8,128)S(1)} %bitcast.9), channel_id=1, source_target_pairs={{0,8},{1,9},{2,10},{3,11},{4,60},{5,61},{6,62},{7,63},{8,16},{9,17... | collective-permute-start | bytes 393224 | tf_op jit(solution)/shard_map/ppermute | solution.py:499
  115.0 12.4 %collective-permute-start.2 = (f32[32,8,128]{2,1,0:T(8,128)S(1)}, f32[32,8,128]{2,1,0:T(8,128)S(1)}, u32[]{:S(2)}, u32[]{:S(2)}) collective-permute-start(f32[32,8,128]{2,1,0:T(8,128)S(1)} %bitcast.11), channel_id=1, source_target_pairs={{0,8},{1,9},{2,10},{3,11},{4,60},{5,61},{6,62},{7,63},{8,16},{9,17... | collective-permute-start | bytes 393224 | tf_op jit(solution)/shard_map/ppermute | solution.py:499
  128.9 9.9 %all-to-all-start.8 = ((f32[8,4,8,128]{3,2,1,0:T(8,128)}), f32[8,4,8,128]{3,2,1,0:T(8,128)S(1)}, u32[]{:S(2)}, u32[]{:S(2)}) async-start(f32[8,4,8,128]{3,2,1,0:T(8,128)} %get-tuple-element.34), calls=%async_computation.8 | async-start | bytes 262144 | tf_op jit(solution)/shard_map/all_to_all | solution.py:572
  133.1 5.8 %collective-permute-start.3 = (f32[4,8,128]{2,1,0:T(8,128)S(1)}, f32[4,8,128]{2,1,0:T(8,128)S(1)}, u32[]{:S(2)}, u32[]{:S(2)}) collective-permute-start(f32[4,8,128]{2,1,0:T(8,128)S(1)} %get-tuple-element.37.u2_ref), channel_id=1, source_target_pairs={{0,8},{8,16},{16,24},{24,32},{32,40},{40,48},{48,56},{56,0},{1,9},... | collective-permute-start | bytes 49160 | tf_op jit(solution)/shard_map/ppermute | solution.py:571

commit v9 on v8

--- a/solution.py
+++ b/solution.py
@@ -96,7 +96,7 @@
             out_ref[y, 80 + 8 * q : 88 + 8 * q, :] = own[q]
 
 
-def middle_kernel(parts_ref, out_ref, x_ref):
+def middle_kernel(parts_ref, out_ref, x_ref, send_ref):
     lane = iota((8, 128), 1)
     sub = iota((8, 128), 0)
     left = lane < 64
@@ -120,6 +120,9 @@
                     totals[z] = term if totals[z] is None else totals[z] + term
         for q in range(4):
             x_ref[4 * y + q] = parts_ref[y, 80 + 8 * q : 88 + 8 * q, :]
+    at = jnp.where(lax.axis_index("ty") < 4, 16, 0)
+    for j in range(16):
+        send_ref[j] = x_ref[at + j]
     for z in range(8):
         out_ref[z, 0:32, :] = totals[z]
         out_ref[z, 32:40, :] = jnp.where(sub == 0, diag[z : z + 1], jnp.where(sub == 1, rhs[z : z + 1], 0.0))
@@ -176,7 +179,7 @@
 def normal_kernel(scale, gathered_ref, panel_ref, obs_ref, factors_ref, out_ref):
     pieces = []
     for y in range(8):
-        pair = gathered_ref[8 * y : 8 * y + 8, :]
+        pair = gathered_ref[8 * y : 8 * y + 8, 0, :]
         pieces += [pair[:, 0:64], pair[:, 64:128]]
     factors = jnp.concatenate(pieces, axis=0)
     turned = factors.T
@@ -253,7 +256,7 @@
 ):
     lags = scalars(lags_ref)
     slab, y = place()
-    read = fill_context(plane_ref, near_ref, context_ref, y)
+    read = fill_context(plane_ref, near_ref, context_ref, y, True)
     back = ar_part(read, slab * 512, steps_all, lags, weight_ref, errors_ref)
     for q in range(4):
         out_ref[q] = RIDGE_TIME * read(q) + AR * back[q]
@@ -276,11 +279,11 @@
             out_ref[j, q] = value
 
 
-def fill_context(plane_ref, near_ref, context_ref, y):
+def fill_context(plane_ref, near_ref, context_ref, y, half=False):
     lower = y < 4
     at = jnp.where(lower, 16, 0)
     near_at = jnp.where(lower, 0, 32)
-    near_from = jnp.where(lower, 16, 0)
+    near_from = 0 if half else jnp.where(lower, 16, 0)
     for j in range(32):
         context_ref[at + j] = plane_ref[j]
     for j in range(16):
@@ -531,12 +534,14 @@
         60,
     )
     parts = lax.all_to_all(parts, "ty", 0, 0)
-    parts, plane = call(middle_kernel, (struct(8, 40, 128), struct(32, 8, 128)), (parts,))
+    parts, plane, send = call(
+        middle_kernel, (struct(8, 40, 128), struct(32, 8, 128), struct(16, 8, 128)), (parts,)
+    )
     parts = lax.all_to_all(parts, "tz", 0, 0)
-    solved = call(solve_kernel, struct(64, 1, 128), (parts,))
-    solved, plane = lax.optimization_barrier((solved, plane))
-    near = neighbour(plane)
-    gathered = lax.all_to_all(solved, ("ty", "tz"), 0, 0).reshape(64, 128)
+    solved = call(solve_kernel, struct(64, 4, 128), (parts,))
+    solved, send = lax.optimization_barrier((solved, send))
+    near = neighbour(send)
+    gathered = lax.all_to_all(solved, ("ty", "tz"), 0, 0)
     gathered, near = lax.optimization_barrier((gathered, near))
     factors, normal = call(
         functools.partial(normal_kernel, 1.0 / cells_all),

time: 173 us -> 174 us (level)
  blocking collectives: 129 us -> 114 us
  starting transfers between devices: 21.7 us -> 29.2 us
  waiting for transfers between devices: 7.31 us -> 14.8 us
    all_to_all x1 -> x0, blocking collectives: 16.5 us -> none  [per_device(): gathered = lax.all_to_all(solved, ('ty', 'tz'), 0, 0).reshape(64, 128)]
    all_to_all x0 -> x1, waiting for transfers between devices: none -> 5.08 us  [per_device(): gathered = lax.all_to_all(solved, ('ty', 'tz'), 0, 0)]
    all_to_all x0 -> x1, starting transfers between devices: none -> 4.75 us  [per_device(): gathered = lax.all_to_all(solved, ('ty', 'tz'), 0, 0)]
    ppermute x3, waiting for transfers between devices: 0.01 us -> 3.72 us  [neighbour(): return lax.ppermute(plane, TM, pairs)]
    all_to_all x1, blocking collectives: 17.8 us -> 19.6 us  [per_device(): moments = lax.all_to_all(moments, ('series', 'tz'), 0, 0).reshape(64, 128)]
  transfers between devices with their start and end apart: 6 -> 7, of which waited for: 2 -> 4; matrix products, arithmetic and copies ran while one was open for 0% -> 0% of each run, Pallas kernels for 0% -> 0%
where the time goes in v9:
time: 174 us; the launch traced here: 173 us
  blocking collectives  114 us (66%)
  starting transfers between devices  29.2 us (17%)
  waiting for transfers between devices  14.8 us (9%)
  Pallas kernels  12.6 us (7%)
    all_to_all x2, blocking collectives, per_device(): parts = lax.all_to_all(parts, 'ty', 0, 0)  33.9 us
    all_to_all x2, blocking collectives, exchange(): return (plane, neighbour(plane), lax.all_to_all(spread, 'series', 0, 0))  20.4 us
    all_to_all x2, blocking collectives, exchange(): plane = lax.all_to_all(spread, 'ty', 0, 0).reshape(32, 8, 128)  20.3 us
    all_to_all x1, blocking collectives, per_device(): parts = lax.all_to_all(parts, 'tz', 0, 0)  20 us
    all_to_all x1, blocking collectives, per_device(): moments = lax.all_to_all(moments, ('series', 'tz'), 0, 0).reshape(64, 128)  19.6 us
    pallas_call x11, Pallas kernels, call(): pl.pallas_call(kernel, out_shape=outs, in_specs=[place] * len(ins), out_s...  12.6 us
    all_to_all x1, starting transfers between devices, per_device(): sums = lax.all_to_all(normal.reshape(8, 8, 896), 'series', 0, 0)  9.32 us
    ppermute x3, starting transfers between devices, neighbour(): return lax.ppermute(plane, TM, pairs)  7.42 us
  transfers between devices with their start and end apart: 7, of which 4 were waited for; matrix products, arithmetic and copies ran while one was open for 0% of the time, Pallas kernels for 0%

profile of v9, /device:TPU:1, one launch (start us, length us, event | category | flops | bytes accessed | tf_op | source)
XLA Modules:
  0.0 173.1 jit_solution(17210559602539627429)
XLA Ops:
  0.6 2.8 %shard_map.68 = f32[8,112,128]{2,1,0:T(8,128)} custom-call(f32[128,512]{1,0:T(8,128)} %panel_ref.1, s32[4,128]{1,0:T(4,128)} %bitcast.13, f32[64,512]{1,0:T(8,128)} %x_ref.3), custom_call_target="tpu_custom_call" | custom-call | tf_op jit(solution)/shard_map/pallas_call | solution.py:32
  3.4 20.3 %all_to_all.55.parts_ref = f32[8,112,128]{2,1,0:T(8,128)S(1)} all-to-all(f32[8,112,128]{2,1,0:T(8,128)} %shard_map.68), channel_id=1, replica_groups=mesh['series'=8,'tz'=8,'ty'=8] {'ty'}, dimensions={0} | all-to-all | bytes 917504 | tf_op jit(solution)/shard_map/all_to_all | solution.py:536
  23.7 0.5 shard_map.69
  24.2 20.0 %all_to_all.56.parts_ref = f32[8,40,128]{2,1,0:T(8,128)S(1)} all-to-all(f32[8,40,128]{2,1,0:T(8,128)S(1)} %get-tuple-element.21), channel_id=1, replica_groups=mesh['series'=8,'tz'=8,'ty'=8] {'tz'}, dimensions={0} | all-to-all | bytes 327680 | tf_op jit(solution)/shard_map/all_to_all | solution.py:540
  44.3 2.4 %shard_map.70 = f32[64,4,128]{2,1,0:T(4,128)} custom-call(f32[8,40,128]{2,1,0:T(8,128)S(1)} %all_to_all.56.parts_ref), custom_call_target="tpu_custom_call" | custom-call | tf_op jit(solution)/shard_map/pallas_call | solution.py:32
  46.7 4.8 %all-to-all-start.2 = ((f32[64,4,128]{2,1,0:T(4,128)}), f32[64,4,128]{2,1,0:T(4,128)S(1)}, u32[]{:S(2)}, u32[]{:S(2)}) async-start(f32[64,4,128]{2,1,0:T(4,128)} %shard_map.70), calls=%async_computation.2 | async-start | bytes 262144 | tf_op jit(solution)/shard_map/all_to_all | solution.py:544
  51.4 2.8 %collective-permute-start = (f32[16,8,128]{2,1,0:T(8,128)S(1)}, f32[16,8,128]{2,1,0:T(8,128)S(1)}, u32[]{:S(2)}, u32[]{:S(2)}) collective-permute-start(f32[16,8,128]{2,1,0:T(8,128)S(1)} %get-tuple-element.24), channel_id=1, source_target_pairs={{0,8},{1,9},{2,10},{3,11},{4,60},{5,61},{6,62},{7,63},{8,16},{9,17... | collective-permute-start | bytes 196616 | tf_op jit(solution)/shard_map/ppermute | solution.py:502
  54.2 3.7 %collective-permute-done.near_ref = f32[16,8,128]{2,1,0:T(8,128)S(1)} collective-permute-done((f32[16,8,128]{2,1,0:T(8,128)S(1)}, f32[16,8,128]{2,1,0:T(8,128)S(1)}, u32[]{:S(2)}, u32[]{:S(2)}) %collective-permute-start) | collective-permute-done | bytes 65568 | tf_op jit(solution)/shard_map/ppermute | solution.py:502
  58.0 5.1 %all-to-all-done.2.gathered_ref = f32[64,4,128]{2,1,0:T(4,128)S(1)} async-done(((f32[64,4,128]{2,1,0:T(4,128)}), f32[64,4,128]{2,1,0:T(4,128)S(1)}, u32[]{:S(2)}, u32[]{:S(2)}) %all-to-all-start.2) | async-done | bytes 131104 | tf_op jit(solution)/shard_map/all_to_all | solution.py:544
  63.0 1.4 shard_map.71
  64.4 9.3 %all-to-all-start.3 = ((f32[8,8,896]{2,1,0:T(8,128)}), f32[8,8,896]{2,1,0:T(8,128)S(1)}, u32[]{:S(2)}, u32[]{:S(2)}) async-start(f32[8,8,896]{2,1,0:T(8,128)} %bitcast.2), calls=%async_computation.3 | async-start | bytes 458752 | tf_op jit(solution)/shard_map/all_to_all | solution.py:551
  73.7 0.7 copy-done.3
  74.6 0.6 copy-done.4
  75.3 0.8 shard_map.72
  76.2 3.8 %all-to-all-done.3.sums_ref = f32[8,8,896]{2,1,0:T(8,128)S(1)} async-done(((f32[8,8,896]{2,1,0:T(8,128)}), f32[8,8,896]{2,1,0:T(8,128)S(1)}, u32[]{:S(2)}, u32[]{:S(2)}) %all-to-all-start.3) | async-done | bytes 229408 | tf_op jit(solution)/shard_map/all_to_all | solution.py:551
  79.9 0.3 shard_map.73
  80.2 10.1 %all_to_all.57 = f32[8,4,8,128]{3,2,1,0:T(8,128)S(1)} all-to-all(f32[8,4,8,128]{3,2,1,0:T(8,128)S(1)} %get-tuple-element.32), channel_id=1, replica_groups=mesh['series'=8,'tz'=8,'ty'=8] {'ty'}, dimensions={0} | all-to-all | bytes 262144 | tf_op jit(solution)/shard_map/all_to_all | solution.py:506
  90.4 2.3 %collective-permute-start.1 = (f32[32,8,128]{2,1,0:T(8,128)S(1)}, f32[32,8,128]{2,1,0:T(8,128)S(1)}, u32[]{:S(2)}, u32[]{:S(2)}) collective-permute-start(f32[32,8,128]{2,1,0:T(8,128)S(1)} %bitcast.8), channel_id=1, source_target_pairs={{0,8},{1,9},{2,10},{3,11},{4,60},{5,61},{6,62},{7,63},{8,16},{9,17... | collective-permute-start | bytes 393224 | tf_op jit(solution)/shard_map/ppermute | solution.py:502
  92.7 10.2 %all_to_all.58.wide_ref.wide0_ref = f32[8,4,8,128]{3,2,1,0:T(8,128)S(1)} all-to-all(f32[8,4,8,128]{3,2,1,0:T(8,128)S(1)} %get-tuple-element.32), channel_id=1, replica_groups=mesh['series'=8,'tz'=8,'ty'=8] {'series'}, dimensions={0} | all-to-all | bytes 262144 | tf_op jit(solution)/shard_map/all_to_all | solution.py:507
  102.9 0.8 shard_map.74
  103.7 10.1 %all_to_all.59 = f32[8,4,8,128]{3,2,1,0:T(8,128)S(1)} all-to-all(f32[8,4,8,128]{3,2,1,0:T(8,128)S(1)} %get-tuple-element.35), channel_id=1, replica_groups=mesh['series'=8,'tz'=8,'ty'=8] {'ty'}, dimensions={0} | all-to-all | bytes 262144 | tf_op jit(solution)/shard_map/all_to_all | solution.py:506
  113.9 2.3 %collective-permute-start.2 = (f32[32,8,128]{2,1,0:T(8,128)S(1)}, f32[32,8,128]{2,1,0:T(8,128)S(1)}, u32[]{:S(2)}, u32[]{:S(2)}) collective-permute-start(f32[32,8,128]{2,1,0:T(8,128)S(1)} %bitcast.10), channel_id=1, source_target_pairs={{0,8},{1,9},{2,10},{3,11},{4,60},{5,61},{6,62},{7,63},{8,16},{9,17... | collective-permute-start | bytes 393224 | tf_op jit(solution)/shard_map/ppermute | solution.py:502
  116.2 10.2 %all_to_all.60.wide_ref.wide1_ref = f32[8,4,8,128]{3,2,1,0:T(8,128)S(1)} all-to-all(f32[8,4,8,128]{3,2,1,0:T(8,128)S(1)} %get-tuple-element.35), channel_id=1, replica_groups=mesh['series'=8,'tz'=8,'ty'=8] {'series'}, dimensions={0} | all-to-all | bytes 262144 | tf_op jit(solution)/shard_map/all_to_all | solution.py:507
  126.4 1.5 shard_map.75
  127.9 4.1 %all-to-all-start.8 = ((f32[8,4,8,128]{3,2,1,0:T(8,128)}), f32[8,4,8,128]{3,2,1,0:T(8,128)S(1)}, u32[]{:S(2)}, u32[]{:S(2)}) async-start(f32[8,4,8,128]{3,2,1,0:T(8,128)} %get-tuple-element.36), calls=%async_computation.8 | async-start | bytes 262144 | tf_op jit(solution)/shard_map/all_to_all | solution.py:577
  132.0 3.5 %collective-permute-start.3 = (f32[4,8,128]{2,1,0:T(8,128)S(1)}, f32[4,8,128]{2,1,0:T(8,128)S(1)}, u32[]{:S(2)}, u32[]{:S(2)}) collective-permute-start(f32[4,8,128]{2,1,0:T(8,128)S(1)} %get-tuple-element.39.u2_ref), channel_id=1, source_target_pairs={{0,8},{8,16},{16,24},{24,32},{32,40},{40,48},{48,56},{56,0},{1,9},... | collective-permute-start | bytes 49160 | tf_op jit(solution)/shard_map/ppermute | solution.py:576
  135.6 2.2 %collective-permute-done.3.near_ref = f32[4,8,128]{2,1,0:T(8,128)S(1)} collective-permute-done((f32[4,8,128]{2,1,0:T(8,128)S(1)}, f32[4,8,128]{2,1,0:T(8,128)S(1)}, u32[]{:S(2)}, u32[]{:S(2)}) %collective-permute-start.3) | collective-permute-done | bytes 16416 | tf_op jit(solution)/shard_map/ppermute | solution.py:576
  137.8 0.3 shard_map.76
  138.1 13.6 %all_to_all.61.parts_ref = f32[8,9,8,128]{3,2,1,0:T(8,128)S(1)} all-to-all(f32[8,9,8,128]{3,2,1,0:T(8,128)S(1)} %shard_map.76), channel_id=1, replica_groups=mesh['series'=8,'tz'=8,'ty'=8] {'ty'}, dimensions={0} | all-to-all | bytes 589824 | tf_op jit(solution)/shard_map/all_to_all | solution.py:579
  151.7 0.8 shard_map.77
  152.5 19.6 %all_to_all.62 = f32[64,1,128]{2,1,0:T(1,128)S(1)} all-to-all(f32[64,1,128]{2,1,0:T(1,128)S(1)} %shard_map.77), channel_id=1, replica_groups=mesh['series'=8,'tz'=8,'ty'=8] {'series','tz'}, dimensions={0} | all-to-all | bytes 65536 | tf_op jit(solution)/shard_map/all_to_all | solution.py:583
  172.1 1.0 shard_map.78
  (15 shorter events, 0.3 us)
Async XLA Ops:
  44.3 18.8 %copy-start.1 = (f32[128,512]{1,0:T(8,128)S(1)}, f32[128,512]{1,0:T(8,128)}, u32[]{:S(2)}) copy-start(f32[128,512]{1,0:T(8,128)} %panel_ref.1) | copy-start | bytes 786436
  46.7 16.4 %copy-start.2 = (s32[128,4]{0,1:T(4,128)S(1)}, s32[128,4]{0,1:T(4,128)}, u32[]{:S(2)}) copy-start(s32[128,4]{0,1:T(4,128)} %param.6) | copy-start | bytes 6148
  46.7 16.4 %all-to-all-start.2 = ((f32[64,4,128]{2,1,0:T(4,128)}), f32[64,4,128]{2,1,0:T(4,128)S(1)}, u32[]{:S(2)}, u32[]{:S(2)}) async-start(f32[64,4,128]{2,1,0:T(4,128)} %shard_map.70), calls=%async_computation.2 | async-start | bytes 262144 | tf_op jit(solution)/shard_map/all_to_all | solution.py:544
  51.4 6.5 %collective-permute-start = (f32[16,8,128]{2,1,0:T(8,128)S(1)}, f32[16,8,128]{2,1,0:T(8,128)S(1)}, u32[]{:S(2)}, u32[]{:S(2)}) collective-permute-start(f32[16,8,128]{2,1,0:T(8,128)S(1)} %get-tuple-element.24), channel_id=1, source_target_pairs={{0,8},{1,9},{2,10},{3,11},{4,60},{5,61},{6,62},{7,63},{8,16},{9,17... | collective-permute-start | bytes 196616 | tf_op jit(solution)/shard_map/ppermute | solution.py:502
  64.4 15.5 %all-to-all-start.3 = ((f32[8,8,896]{2,1,0:T(8,128)}), f32[8,8,896]{2,1,0:T(8,128)S(1)}, u32[]{:S(2)}, u32[]{:S(2)}) async-start(f32[8,8,896]{2,1,0:T(8,128)} %bitcast.2), calls=%async_computation.3 | async-start | bytes 458752 | tf_op jit(solution)/shard_map/all_to_all | solution.py:551
  73.7 0.7 copy-start.3
  74.5 0.7 copy-start.4
  75.3 4.6 %copy-start = (f32[64,512]{1,0:T(8,128)S(1)}, f32[64,512]{1,0:T(8,128)}, u32[]{:S(2)}) copy-start(f32[64,512]{1,0:T(8,128)} %x_ref.3) | copy-start | bytes 393220
  90.4 12.5 %collective-permute-start.1 = (f32[32,8,128]{2,1,0:T(8,128)S(1)}, f32[32,8,128]{2,1,0:T(8,128)S(1)}, u32[]{:S(2)}, u32[]{:S(2)}) collective-permute-start(f32[32,8,128]{2,1,0:T(8,128)S(1)} %bitcast.8), channel_id=1, source_target_pairs={{0,8},{1,9},{2,10},{3,11},{4,60},{5,61},{6,62},{7,63},{8,16},{9,17... | collective-permute-start | bytes 393224 | tf_op jit(solution)/shard_map/ppermute | solution.py:502
  113.9 12.5 %collective-permute-start.2 = (f32[32,8,128]{2,1,0:T(8,128)S(1)}, f32[32,8,128]{2,1,0:T(8,128)S(1)}, u32[]{:S(2)}, u32[]{:S(2)}) collective-permute-start(f32[32,8,128]{2,1,0:T(8,128)S(1)} %bitcast.10), channel_id=1, source_target_pairs={{0,8},{1,9},{2,10},{3,11},{4,60},{5,61},{6,62},{7,63},{8,16},{9,17... | collective-permute-start | bytes 393224 | tf_op jit(solution)/shard_map/ppermute | solution.py:502
  127.9 9.9 %all-to-all-start.8 = ((f32[8,4,8,128]{3,2,1,0:T(8,128)}), f32[8,4,8,128]{3,2,1,0:T(8,128)S(1)}, u32[]{:S(2)}, u32[]{:S(2)}) async-start(f32[8,4,8,128]{3,2,1,0:T(8,128)} %get-tuple-element.36), calls=%async_computation.8 | async-start | bytes 262144 | tf_op jit(solution)/shard_map/all_to_all | solution.py:577
  132.0 5.8 %collective-permute-start.3 = (f32[4,8,128]{2,1,0:T(8,128)S(1)}, f32[4,8,128]{2,1,0:T(8,128)S(1)}, u32[]{:S(2)}, u32[]{:S(2)}) collective-permute-start(f32[4,8,128]{2,1,0:T(8,128)S(1)} %get-tuple-element.39.u2_ref), channel_id=1, source_target_pairs={{0,8},{8,16},{16,24},{24,32},{32,40},{40,48},{48,56},{56,0},{1,9},... | collective-permute-start | bytes 49160 | tf_op jit(solution)/shard_map/ppermute | solution.py:576

commit v10 on v8

--- a/solution.py
+++ b/solution.py
@@ -450,15 +450,14 @@
 
 
 def finish_kernel(parts_ref, first_ref, theta_ref, x_ref, wide0_ref, wide1_ref, wide2_ref, out_ref):
-    half = iota((8, 128), 1) < 64
-    pairs = []
-    for j in range(8):
-        part = parts_ref[8 * j : 8 * j + 8, :]
-        other = pltpu.roll(part, 64, axis=1)
-        pairs.append((jnp.where(half, part, other), jnp.where(half, other, part)))
-    total = pair_tree(pairs)
-    for by in (4, 2, 1):
-        total = pair_add(total, (pltpu.roll(total[0], by, axis=0), pltpu.roll(total[1], by, axis=0)))
+    parts = parts_ref[...]
+    other = pltpu.roll(parts, 64, axis=1)
+    half = iota((64, 128), 1) < 64
+    high, low = jnp.where(half, parts, other), jnp.where(half, other, parts)
+    large = 6144.0 * jnp.max(jnp.abs(high), axis=0, keepdims=True)
+    lead = (high + large) - large
+    rest = (high - lead) + low
+    total = two_sum(*[jnp.broadcast_to(jnp.sum(a, axis=0, keepdims=True), (8, 128)) for a in (lead, rest)])
 
     def moment(i):
         return tuple(jnp.broadcast_to(a[:, 8 * i : 8 * i + 1], (8, 128)) for a in total)

time: 173 us -> 173 us (level)
  no operation moved by 1% of the time
where the time goes in v10:
time: 173 us
  blocking collectives  129 us (75%)
  starting transfers between devices  21.7 us (13%)
  Pallas kernels  11.9 us (7%)
  waiting for transfers between devices  7.31 us (4%)
    all_to_all x2, blocking collectives, per_device(): parts = lax.all_to_all(parts, 'ty', 0, 0)  34.1 us
    all_to_all x2, blocking collectives, exchange(): return (plane, neighbour(plane), lax.all_to_all(spread, 'series', 0, 0))  20.5 us
    all_to_all x2, blocking collectives, exchange(): plane = lax.all_to_all(spread, 'ty', 0, 0).reshape(32, 8, 128)  20.3 us
    all_to_all x1, blocking collectives, per_device(): parts = lax.all_to_all(parts, 'tz', 0, 0)  20.2 us
    all_to_all x1, blocking collectives, per_device(): moments = lax.all_to_all(moments, ('series', 'tz'), 0, 0).reshape(64, 128)  17.8 us
    all_to_all x1, blocking collectives, per_device(): gathered = lax.all_to_all(solved, ('ty', 'tz'), 0, 0).reshape(64, 128)  16.5 us
    pallas_call x11, Pallas kernels, call(): pl.pallas_call(kernel, out_shape=outs, in_specs=[place] * len(ins), out_s...  11.9 us
    all_to_all x1, starting transfers between devices, per_device(): sums = lax.all_to_all(normal.reshape(8, 8, 896), 'series', 0, 0)  8.83 us
  transfers between devices with their start and end apart: 6, of which 2 were waited for; matrix products, arithmetic and copies ran while one was open for 0% of the time, Pallas kernels for 0%

profile of v10, /device:TPU:1, one launch (start us, length us, event | category | flops | bytes accessed | tf_op | source)
XLA Modules:
  0.0 172.6 jit_solution(9418206948163974375)
XLA Ops:
  0.6 2.8 %shard_map.68 = f32[8,112,128]{2,1,0:T(8,128)} custom-call(f32[128,512]{1,0:T(8,128)} %panel_ref.1, s32[4,128]{1,0:T(4,128)} %bitcast.15, f32[64,512]{1,0:T(8,128)} %x_ref.3), custom_call_target="tpu_custom_call" | custom-call | tf_op jit(solution)/shard_map/pallas_call | solution.py:32
  3.4 20.3 %all_to_all.55.parts_ref = f32[8,112,128]{2,1,0:T(8,128)S(1)} all-to-all(f32[8,112,128]{2,1,0:T(8,128)} %shard_map.68), channel_id=1, replica_groups=mesh['series'=8,'tz'=8,'ty'=8] {'ty'}, dimensions={0} | all-to-all | bytes 917504 | tf_op jit(solution)/shard_map/all_to_all | solution.py:532
  23.7 0.5 shard_map.69
  24.2 20.2 %all_to_all.56.parts_ref = f32[8,40,128]{2,1,0:T(8,128)S(1)} all-to-all(f32[8,40,128]{2,1,0:T(8,128)S(1)} %get-tuple-element.20), channel_id=1, replica_groups=mesh['series'=8,'tz'=8,'ty'=8] {'tz'}, dimensions={0} | all-to-all | bytes 327680 | tf_op jit(solution)/shard_map/all_to_all | solution.py:534
  44.4 1.7 shard_map.70
  46.2 2.1 %collective-permute-start = (f32[32,8,128]{2,1,0:T(8,128)S(1)}, f32[32,8,128]{2,1,0:T(8,128)S(1)}, u32[]{:S(2)}, u32[]{:S(2)}) collective-permute-start(f32[32,8,128]{2,1,0:T(8,128)S(1)} %get-tuple-element.23.plane_ref), channel_id=1, source_target_pairs={{0,8},{1,9},{2,10},{3,11},{4,60},{5,61},{6,62},{7,63},{8,16},{9,17... | collective-permute-start | bytes 393224 | tf_op jit(solution)/shard_map/ppermute | solution.py:498
  48.3 16.5 %all_to_all.57 = f32[64,1,128]{2,1,0:T(1,128)S(1)} all-to-all(f32[64,1,128]{2,1,0:T(1,128)S(1)} %shard_map.70), channel_id=1, replica_groups=mesh['series'=8,'tz'=8,'ty'=8] {'ty','tz'}, dimensions={0} | all-to-all | bytes 65536 | tf_op jit(solution)/shard_map/all_to_all | solution.py:538
  64.8 1.4 shard_map.71
  66.1 8.8 %all-to-all-start.3 = ((f32[8,8,896]{2,1,0:T(8,128)}), f32[8,8,896]{2,1,0:T(8,128)S(1)}, u32[]{:S(2)}, u32[]{:S(2)}) async-start(f32[8,8,896]{2,1,0:T(8,128)} %bitcast.3), calls=%async_computation.3 | async-start | bytes 458752 | tf_op jit(solution)/shard_map/all_to_all | solution.py:545
  75.0 0.7 copy-done.3
  75.6 0.1 copy.10.all_ref
  75.8 0.6 copy-done.4
  76.5 0.1 broadcast_in_dim.4.weight_ref
  76.5 0.8 shard_map.72
  77.4 3.8 %all-to-all-done.3.sums_ref = f32[8,8,896]{2,1,0:T(8,128)S(1)} async-done(((f32[8,8,896]{2,1,0:T(8,128)}), f32[8,8,896]{2,1,0:T(8,128)S(1)}, u32[]{:S(2)}, u32[]{:S(2)}) %all-to-all-start.3) | async-done | bytes 229408 | tf_op jit(solution)/shard_map/all_to_all | solution.py:545
  81.2 0.3 shard_map.73
  81.4 10.1 %all_to_all.58 = f32[8,4,8,128]{3,2,1,0:T(8,128)S(1)} all-to-all(f32[8,4,8,128]{3,2,1,0:T(8,128)S(1)} %get-tuple-element.30), channel_id=1, replica_groups=mesh['series'=8,'tz'=8,'ty'=8] {'ty'}, dimensions={0} | all-to-all | bytes 262144 | tf_op jit(solution)/shard_map/all_to_all | solution.py:502
  91.6 2.2 %collective-permute-start.1 = (f32[32,8,128]{2,1,0:T(8,128)S(1)}, f32[32,8,128]{2,1,0:T(8,128)S(1)}, u32[]{:S(2)}, u32[]{:S(2)}) collective-permute-start(f32[32,8,128]{2,1,0:T(8,128)S(1)} %bitcast.9), channel_id=1, source_target_pairs={{0,8},{1,9},{2,10},{3,11},{4,60},{5,61},{6,62},{7,63},{8,16},{9,17... | collective-permute-start | bytes 393224 | tf_op jit(solution)/shard_map/ppermute | solution.py:498
  93.8 10.2 %all_to_all.59.wide_ref.wide0_ref = f32[8,4,8,128]{3,2,1,0:T(8,128)S(1)} all-to-all(f32[8,4,8,128]{3,2,1,0:T(8,128)S(1)} %get-tuple-element.30), channel_id=1, replica_groups=mesh['series'=8,'tz'=8,'ty'=8] {'series'}, dimensions={0} | all-to-all | bytes 262144 | tf_op jit(solution)/shard_map/all_to_all | solution.py:503
  104.0 0.8 shard_map.74
  104.9 10.1 %all_to_all.60 = f32[8,4,8,128]{3,2,1,0:T(8,128)S(1)} all-to-all(f32[8,4,8,128]{3,2,1,0:T(8,128)S(1)} %get-tuple-element.33), channel_id=1, replica_groups=mesh['series'=8,'tz'=8,'ty'=8] {'ty'}, dimensions={0} | all-to-all | bytes 262144 | tf_op jit(solution)/shard_map/all_to_all | solution.py:502
  115.0 2.2 %collective-permute-start.2 = (f32[32,8,128]{2,1,0:T(8,128)S(1)}, f32[32,8,128]{2,1,0:T(8,128)S(1)}, u32[]{:S(2)}, u32[]{:S(2)}) collective-permute-start(f32[32,8,128]{2,1,0:T(8,128)S(1)} %bitcast.11), channel_id=1, source_target_pairs={{0,8},{1,9},{2,10},{3,11},{4,60},{5,61},{6,62},{7,63},{8,16},{9,17... | collective-permute-start | bytes 393224 | tf_op jit(solution)/shard_map/ppermute | solution.py:498
  117.2 10.2 %all_to_all.61.wide_ref.wide1_ref = f32[8,4,8,128]{3,2,1,0:T(8,128)S(1)} all-to-all(f32[8,4,8,128]{3,2,1,0:T(8,128)S(1)} %get-tuple-element.33), channel_id=1, replica_groups=mesh['series'=8,'tz'=8,'ty'=8] {'series'}, dimensions={0} | all-to-all | bytes 262144 | tf_op jit(solution)/shard_map/all_to_all | solution.py:503
  127.5 1.5 shard_map.75
  128.9 4.1 %all-to-all-start.8 = ((f32[8,4,8,128]{3,2,1,0:T(8,128)}), f32[8,4,8,128]{3,2,1,0:T(8,128)S(1)}, u32[]{:S(2)}, u32[]{:S(2)}) async-start(f32[8,4,8,128]{3,2,1,0:T(8,128)} %get-tuple-element.34), calls=%async_computation.8 | async-start | bytes 262144 | tf_op jit(solution)/shard_map/all_to_all | solution.py:571
  133.1 2.2 %collective-permute-start.3 = (f32[4,8,128]{2,1,0:T(8,128)S(1)}, f32[4,8,128]{2,1,0:T(8,128)S(1)}, u32[]{:S(2)}, u32[]{:S(2)}) collective-permute-start(f32[4,8,128]{2,1,0:T(8,128)S(1)} %get-tuple-element.37.u2_ref), channel_id=1, source_target_pairs={{0,8},{8,16},{16,24},{24,32},{32,40},{40,48},{48,56},{56,0},{1,9},... | collective-permute-start | bytes 49160 | tf_op jit(solution)/shard_map/ppermute | solution.py:570
  135.3 3.5 %collective-permute-done.3.near_ref = f32[4,8,128]{2,1,0:T(8,128)S(1)} collective-permute-done((f32[4,8,128]{2,1,0:T(8,128)S(1)}, f32[4,8,128]{2,1,0:T(8,128)S(1)}, u32[]{:S(2)}, u32[]{:S(2)}) %collective-permute-start.3) | collective-permute-done | bytes 16416 | tf_op jit(solution)/shard_map/ppermute | solution.py:570
  138.8 0.3 shard_map.76
  139.2 13.8 %all_to_all.62.parts_ref = f32[8,9,8,128]{3,2,1,0:T(8,128)S(1)} all-to-all(f32[8,9,8,128]{3,2,1,0:T(8,128)S(1)} %shard_map.76), channel_id=1, replica_groups=mesh['series'=8,'tz'=8,'ty'=8] {'ty'}, dimensions={0} | all-to-all | bytes 589824 | tf_op jit(solution)/shard_map/all_to_all | solution.py:573
  152.9 0.8 shard_map.77
  153.7 17.8 %all_to_all.63 = f32[64,1,128]{2,1,0:T(1,128)S(1)} all-to-all(f32[64,1,128]{2,1,0:T(1,128)S(1)} %shard_map.77), channel_id=1, replica_groups=mesh['series'=8,'tz'=8,'ty'=8] {'series','tz'}, dimensions={0} | all-to-all | bytes 65536 | tf_op jit(solution)/shard_map/all_to_all | solution.py:577
  171.5 1.0 shard_map.78
  (14 shorter events, 0.2 us)
Async XLA Ops:
  24.2 40.5 %copy-start.1 = (f32[128,512]{1,0:T(8,128)S(1)}, f32[128,512]{1,0:T(8,128)}, u32[]{:S(2)}) copy-start(f32[128,512]{1,0:T(8,128)} %panel_ref.1) | copy-start | bytes 786436
  46.2 18.6 %collective-permute-start = (f32[32,8,128]{2,1,0:T(8,128)S(1)}, f32[32,8,128]{2,1,0:T(8,128)S(1)}, u32[]{:S(2)}, u32[]{:S(2)}) collective-permute-start(f32[32,8,128]{2,1,0:T(8,128)S(1)} %get-tuple-element.23.plane_ref), channel_id=1, source_target_pairs={{0,8},{1,9},{2,10},{3,11},{4,60},{5,61},{6,62},{7,63},{8,16},{9,17... | collective-permute-start | bytes 393224 | tf_op jit(solution)/shard_map/ppermute | solution.py:498
  48.3 16.5 %copy-start.2 = (s32[128,4]{0,1:T(4,128)S(1)}, s32[128,4]{0,1:T(4,128)}, u32[]{:S(2)}) copy-start(s32[128,4]{0,1:T(4,128)} %param.6) | copy-start | bytes 6148
  66.1 15.0 %all-to-all-start.3 = ((f32[8,8,896]{2,1,0:T(8,128)}), f32[8,8,896]{2,1,0:T(8,128)S(1)}, u32[]{:S(2)}, u32[]{:S(2)}) async-start(f32[8,8,896]{2,1,0:T(8,128)} %bitcast.3), calls=%async_computation.3 | async-start | bytes 458752 | tf_op jit(solution)/shard_map/all_to_all | solution.py:545
  75.0 0.7 copy-start.3
  75.7 0.7 copy-start.4
  76.5 4.6 %copy-start = (f32[64,512]{1,0:T(8,128)S(1)}, f32[64,512]{1,0:T(8,128)}, u32[]{:S(2)}) copy-start(f32[64,512]{1,0:T(8,128)} %x_ref.3) | copy-start | bytes 393220
  91.6 12.5 %collective-permute-start.1 = (f32[32,8,128]{2,1,0:T(8,128)S(1)}, f32[32,8,128]{2,1,0:T(8,128)S(1)}, u32[]{:S(2)}, u32[]{:S(2)}) collective-permute-start(f32[32,8,128]{2,1,0:T(8,128)S(1)} %bitcast.9), channel_id=1, source_target_pairs={{0,8},{1,9},{2,10},{3,11},{4,60},{5,61},{6,62},{7,63},{8,16},{9,17... | collective-permute-start | bytes 393224 | tf_op jit(solution)/shard_map/ppermute | solution.py:498
  115.0 12.4 %collective-permute-start.2 = (f32[32,8,128]{2,1,0:T(8,128)S(1)}, f32[32,8,128]{2,1,0:T(8,128)S(1)}, u32[]{:S(2)}, u32[]{:S(2)}) collective-permute-start(f32[32,8,128]{2,1,0:T(8,128)S(1)} %bitcast.11), channel_id=1, source_target_pairs={{0,8},{1,9},{2,10},{3,11},{4,60},{5,61},{6,62},{7,63},{8,16},{9,17... | collective-permute-start | bytes 393224 | tf_op jit(solution)/shard_map/ppermute | solution.py:498
  128.9 9.9 %all-to-all-start.8 = ((f32[8,4,8,128]{3,2,1,0:T(8,128)}), f32[8,4,8,128]{3,2,1,0:T(8,128)S(1)}, u32[]{:S(2)}, u32[]{:S(2)}) async-start(f32[8,4,8,128]{3,2,1,0:T(8,128)} %get-tuple-element.34), calls=%async_computation.8 | async-start | bytes 262144 | tf_op jit(solution)/shard_map/all_to_all | solution.py:571
  133.1 5.8 %collective-permute-start.3 = (f32[4,8,128]{2,1,0:T(8,128)S(1)}, f32[4,8,128]{2,1,0:T(8,128)S(1)}, u32[]{:S(2)}, u32[]{:S(2)}) collective-permute-start(f32[4,8,128]{2,1,0:T(8,128)S(1)} %get-tuple-element.37.u2_ref), channel_id=1, source_target_pairs={{0,8},{8,16},{16,24},{24,32},{32,40},{40,48},{48,56},{56,0},{1,9},... | collective-permute-start | bytes 49160 | tf_op jit(solution)/shard_map/ppermute | solution.py:570

commit v11 on v10

--- a/solution.py
+++ b/solution.py
@@ -374,10 +374,11 @@
 
 
 def fold_rows(value):
-    pair = (value, jnp.zeros_like(value))
-    for by in (4, 2, 1):
-        pair = pair_add(pair, (pltpu.roll(pair[0], by, axis=0), pltpu.roll(pair[1], by, axis=0)))
-    return pair
+    large = 6144.0 * jnp.max(jnp.abs(value), axis=0, keepdims=True)
+    lead = (value + large) - large
+    return two_sum(*[
+        jnp.broadcast_to(jnp.sum(a, axis=0, keepdims=True), (8, 128)) for a in (lead, value - lead)
+    ])
 
 
 def product_kernel(wide_ref, h_ref, u0_ref, u1_ref, u2_ref, near_ref, out_ref):

time: 173 us -> 173 us (level)
  no operation moved by 1% of the time
where the time goes in v11:
time: 173 us
  blocking collectives  129 us (75%)
  starting transfers between devices  21.7 us (13%)
  Pallas kernels  11.9 us (7%)
  waiting for transfers between devices  7.31 us (4%)
    all_to_all x2, blocking collectives, per_device(): parts = lax.all_to_all(parts, 'ty', 0, 0)  34.1 us
    all_to_all x2, blocking collectives, exchange(): return (plane, neighbour(plane), lax.all_to_all(spread, 'series', 0, 0))  20.5 us
    all_to_all x2, blocking collectives, exchange(): plane = lax.all_to_all(spread, 'ty', 0, 0).reshape(32, 8, 128)  20.3 us
    all_to_all x1, blocking collectives, per_device(): parts = lax.all_to_all(parts, 'tz', 0, 0)  20.2 us
    all_to_all x1, blocking collectives, per_device(): moments = lax.all_to_all(moments, ('series', 'tz'), 0, 0).reshape(64, 128)  17.8 us
    all_to_all x1, blocking collectives, per_device(): gathered = lax.all_to_all(solved, ('ty', 'tz'), 0, 0).reshape(64, 128)  16.5 us
    pallas_call x11, Pallas kernels, call(): pl.pallas_call(kernel, out_shape=outs, in_specs=[place] * len(ins), out_s...  11.9 us
    all_to_all x1, starting transfers between devices, per_device(): sums = lax.all_to_all(normal.reshape(8, 8, 896), 'series', 0, 0)  8.83 us
  transfers between devices with their start and end apart: 6, of which 2 were waited for; matrix products, arithmetic and copies ran while one was open for 0% of the time, Pallas kernels for 0%

profile of v11, /device:TPU:1, one launch (start us, length us, event | category | flops | bytes accessed | tf_op | source)
XLA Modules:
  0.0 172.5 jit_solution(1630339521434122703)
XLA Ops:
  0.6 2.8 %shard_map.68 = f32[8,112,128]{2,1,0:T(8,128)} custom-call(f32[128,512]{1,0:T(8,128)} %panel_ref.1, s32[4,128]{1,0:T(4,128)} %bitcast.15, f32[64,512]{1,0:T(8,128)} %x_ref.3), custom_call_target="tpu_custom_call" | custom-call | tf_op jit(solution)/shard_map/pallas_call | solution.py:32
  3.4 20.3 %all_to_all.55.parts_ref = f32[8,112,128]{2,1,0:T(8,128)S(1)} all-to-all(f32[8,112,128]{2,1,0:T(8,128)} %shard_map.68), channel_id=1, replica_groups=mesh['series'=8,'tz'=8,'ty'=8] {'ty'}, dimensions={0} | all-to-all | bytes 917504 | tf_op jit(solution)/shard_map/all_to_all | solution.py:533
  23.7 0.5 shard_map.69
  24.2 20.2 %all_to_all.56.parts_ref = f32[8,40,128]{2,1,0:T(8,128)S(1)} all-to-all(f32[8,40,128]{2,1,0:T(8,128)S(1)} %get-tuple-element.20), channel_id=1, replica_groups=mesh['series'=8,'tz'=8,'ty'=8] {'tz'}, dimensions={0} | all-to-all | bytes 327680 | tf_op jit(solution)/shard_map/all_to_all | solution.py:535
  44.4 1.7 shard_map.70
  46.2 2.1 %collective-permute-start = (f32[32,8,128]{2,1,0:T(8,128)S(1)}, f32[32,8,128]{2,1,0:T(8,128)S(1)}, u32[]{:S(2)}, u32[]{:S(2)}) collective-permute-start(f32[32,8,128]{2,1,0:T(8,128)S(1)} %get-tuple-element.23.plane_ref), channel_id=1, source_target_pairs={{0,8},{1,9},{2,10},{3,11},{4,60},{5,61},{6,62},{7,63},{8,16},{9,17... | collective-permute-start | bytes 393224 | tf_op jit(solution)/shard_map/ppermute | solution.py:499
  48.3 16.5 %all_to_all.57 = f32[64,1,128]{2,1,0:T(1,128)S(1)} all-to-all(f32[64,1,128]{2,1,0:T(1,128)S(1)} %shard_map.70), channel_id=1, replica_groups=mesh['series'=8,'tz'=8,'ty'=8] {'ty','tz'}, dimensions={0} | all-to-all | bytes 65536 | tf_op jit(solution)/shard_map/all_to_all | solution.py:539
  64.8 1.4 shard_map.71
  66.1 8.8 %all-to-all-start.3 = ((f32[8,8,896]{2,1,0:T(8,128)}), f32[8,8,896]{2,1,0:T(8,128)S(1)}, u32[]{:S(2)}, u32[]{:S(2)}) async-start(f32[8,8,896]{2,1,0:T(8,128)} %bitcast.3), calls=%async_computation.3 | async-start | bytes 458752 | tf_op jit(solution)/shard_map/all_to_all | solution.py:546
  75.0 0.7 copy-done.3
  75.6 0.1 copy.10.all_ref
  75.8 0.6 copy-done.4
  76.5 0.1 broadcast_in_dim.4.weight_ref
  76.5 0.8 shard_map.72
  77.4 3.8 %all-to-all-done.3.sums_ref = f32[8,8,896]{2,1,0:T(8,128)S(1)} async-done(((f32[8,8,896]{2,1,0:T(8,128)}), f32[8,8,896]{2,1,0:T(8,128)S(1)}, u32[]{:S(2)}, u32[]{:S(2)}) %all-to-all-start.3) | async-done | bytes 229408 | tf_op jit(solution)/shard_map/all_to_all | solution.py:546
  81.2 0.3 shard_map.73
  81.4 10.1 %all_to_all.58 = f32[8,4,8,128]{3,2,1,0:T(8,128)S(1)} all-to-all(f32[8,4,8,128]{3,2,1,0:T(8,128)S(1)} %get-tuple-element.30), channel_id=1, replica_groups=mesh['series'=8,'tz'=8,'ty'=8] {'ty'}, dimensions={0} | all-to-all | bytes 262144 | tf_op jit(solution)/shard_map/all_to_all | solution.py:503
  91.6 2.2 %collective-permute-start.1 = (f32[32,8,128]{2,1,0:T(8,128)S(1)}, f32[32,8,128]{2,1,0:T(8,128)S(1)}, u32[]{:S(2)}, u32[]{:S(2)}) collective-permute-start(f32[32,8,128]{2,1,0:T(8,128)S(1)} %bitcast.9), channel_id=1, source_target_pairs={{0,8},{1,9},{2,10},{3,11},{4,60},{5,61},{6,62},{7,63},{8,16},{9,17... | collective-permute-start | bytes 393224 | tf_op jit(solution)/shard_map/ppermute | solution.py:499
  93.8 10.2 %all_to_all.59.wide_ref.wide0_ref = f32[8,4,8,128]{3,2,1,0:T(8,128)S(1)} all-to-all(f32[8,4,8,128]{3,2,1,0:T(8,128)S(1)} %get-tuple-element.30), channel_id=1, replica_groups=mesh['series'=8,'tz'=8,'ty'=8] {'series'}, dimensions={0} | all-to-all | bytes 262144 | tf_op jit(solution)/shard_map/all_to_all | solution.py:504
  104.0 0.8 shard_map.74
  104.9 10.1 %all_to_all.60 = f32[8,4,8,128]{3,2,1,0:T(8,128)S(1)} all-to-all(f32[8,4,8,128]{3,2,1,0:T(8,128)S(1)} %get-tuple-element.33), channel_id=1, replica_groups=mesh['series'=8,'tz'=8,'ty'=8] {'ty'}, dimensions={0} | all-to-all | bytes 262144 | tf_op jit(solution)/shard_map/all_to_all | solution.py:503
  115.0 2.2 %collective-permute-start.2 = (f32[32,8,128]{2,1,0:T(8,128)S(1)}, f32[32,8,128]{2,1,0:T(8,128)S(1)}, u32[]{:S(2)}, u32[]{:S(2)}) collective-permute-start(f32[32,8,128]{2,1,0:T(8,128)S(1)} %bitcast.11), channel_id=1, source_target_pairs={{0,8},{1,9},{2,10},{3,11},{4,60},{5,61},{6,62},{7,63},{8,16},{9,17... | collective-permute-start | bytes 393224 | tf_op jit(solution)/shard_map/ppermute | solution.py:499
  117.2 10.2 %all_to_all.61.wide_ref.wide1_ref = f32[8,4,8,128]{3,2,1,0:T(8,128)S(1)} all-to-all(f32[8,4,8,128]{3,2,1,0:T(8,128)S(1)} %get-tuple-element.33), channel_id=1, replica_groups=mesh['series'=8,'tz'=8,'ty'=8] {'series'}, dimensions={0} | all-to-all | bytes 262144 | tf_op jit(solution)/shard_map/all_to_all | solution.py:504
  127.5 1.5 shard_map.75
  128.9 4.1 %all-to-all-start.8 = ((f32[8,4,8,128]{3,2,1,0:T(8,128)}), f32[8,4,8,128]{3,2,1,0:T(8,128)S(1)}, u32[]{:S(2)}, u32[]{:S(2)}) async-start(f32[8,4,8,128]{3,2,1,0:T(8,128)} %get-tuple-element.34), calls=%async_computation.8 | async-start | bytes 262144 | tf_op jit(solution)/shard_map/all_to_all | solution.py:572
  133.1 2.2 %collective-permute-start.3 = (f32[4,8,128]{2,1,0:T(8,128)S(1)}, f32[4,8,128]{2,1,0:T(8,128)S(1)}, u32[]{:S(2)}, u32[]{:S(2)}) collective-permute-start(f32[4,8,128]{2,1,0:T(8,128)S(1)} %get-tuple-element.37.u2_ref), channel_id=1, source_target_pairs={{0,8},{8,16},{16,24},{24,32},{32,40},{40,48},{48,56},{56,0},{1,9},... | collective-permute-start | bytes 49160 | tf_op jit(solution)/shard_map/ppermute | solution.py:571
  135.3 3.5 %collective-permute-done.3.near_ref = f32[4,8,128]{2,1,0:T(8,128)S(1)} collective-permute-done((f32[4,8,128]{2,1,0:T(8,128)S(1)}, f32[4,8,128]{2,1,0:T(8,128)S(1)}, u32[]{:S(2)}, u32[]{:S(2)}) %collective-permute-start.3) | collective-permute-done | bytes 16416 | tf_op jit(solution)/shard_map/ppermute | solution.py:571
  138.8 0.3 shard_map.76
  139.2 13.8 %all_to_all.62.parts_ref = f32[8,9,8,128]{3,2,1,0:T(8,128)S(1)} all-to-all(f32[8,9,8,128]{3,2,1,0:T(8,128)S(1)} %shard_map.76), channel_id=1, replica_groups=mesh['series'=8,'tz'=8,'ty'=8] {'ty'}, dimensions={0} | all-to-all | bytes 589824 | tf_op jit(solution)/shard_map/all_to_all | solution.py:574
  152.9 0.8 shard_map.77
  153.7 17.8 %all_to_all.63 = f32[64,1,128]{2,1,0:T(1,128)S(1)} all-to-all(f32[64,1,128]{2,1,0:T(1,128)S(1)} %shard_map.77), channel_id=1, replica_groups=mesh['series'=8,'tz'=8,'ty'=8] {'series','tz'}, dimensions={0} | all-to-all | bytes 65536 | tf_op jit(solution)/shard_map/all_to_all | solution.py:578
  171.5 1.0 shard_map.78
  (14 shorter events, 0.2 us)
Async XLA Ops:
  24.2 40.5 %copy-start.1 = (f32[128,512]{1,0:T(8,128)S(1)}, f32[128,512]{1,0:T(8,128)}, u32[]{:S(2)}) copy-start(f32[128,512]{1,0:T(8,128)} %panel_ref.1) | copy-start | bytes 786436
  46.2 18.6 %collective-permute-start = (f32[32,8,128]{2,1,0:T(8,128)S(1)}, f32[32,8,128]{2,1,0:T(8,128)S(1)}, u32[]{:S(2)}, u32[]{:S(2)}) collective-permute-start(f32[32,8,128]{2,1,0:T(8,128)S(1)} %get-tuple-element.23.plane_ref), channel_id=1, source_target_pairs={{0,8},{1,9},{2,10},{3,11},{4,60},{5,61},{6,62},{7,63},{8,16},{9,17... | collective-permute-start | bytes 393224 | tf_op jit(solution)/shard_map/ppermute | solution.py:499
  48.3 16.5 %copy-start.2 = (s32[128,4]{0,1:T(4,128)S(1)}, s32[128,4]{0,1:T(4,128)}, u32[]{:S(2)}) copy-start(s32[128,4]{0,1:T(4,128)} %param.6) | copy-start | bytes 6148
  66.1 15.0 %all-to-all-start.3 = ((f32[8,8,896]{2,1,0:T(8,128)}), f32[8,8,896]{2,1,0:T(8,128)S(1)}, u32[]{:S(2)}, u32[]{:S(2)}) async-start(f32[8,8,896]{2,1,0:T(8,128)} %bitcast.3), calls=%async_computation.3 | async-start | bytes 458752 | tf_op jit(solution)/shard_map/all_to_all | solution.py:546
  75.0 0.7 copy-start.3
  75.7 0.7 copy-start.4
  76.5 4.6 %copy-start = (f32[64,512]{1,0:T(8,128)S(1)}, f32[64,512]{1,0:T(8,128)}, u32[]{:S(2)}) copy-start(f32[64,512]{1,0:T(8,128)} %x_ref.3) | copy-start | bytes 393220
  91.6 12.5 %collective-permute-start.1 = (f32[32,8,128]{2,1,0:T(8,128)S(1)}, f32[32,8,128]{2,1,0:T(8,128)S(1)}, u32[]{:S(2)}, u32[]{:S(2)}) collective-permute-start(f32[32,8,128]{2,1,0:T(8,128)S(1)} %bitcast.9), channel_id=1, source_target_pairs={{0,8},{1,9},{2,10},{3,11},{4,60},{5,61},{6,62},{7,63},{8,16},{9,17... | collective-permute-start | bytes 393224 | tf_op jit(solution)/shard_map/ppermute | solution.py:499
  115.0 12.4 %collective-permute-start.2 = (f32[32,8,128]{2,1,0:T(8,128)S(1)}, f32[32,8,128]{2,1,0:T(8,128)S(1)}, u32[]{:S(2)}, u32[]{:S(2)}) collective-permute-start(f32[32,8,128]{2,1,0:T(8,128)S(1)} %bitcast.11), channel_id=1, source_target_pairs={{0,8},{1,9},{2,10},{3,11},{4,60},{5,61},{6,62},{7,63},{8,16},{9,17... | collective-permute-start | bytes 393224 | tf_op jit(solution)/shard_map/ppermute | solution.py:499
  128.9 9.9 %all-to-all-start.8 = ((f32[8,4,8,128]{3,2,1,0:T(8,128)}), f32[8,4,8,128]{3,2,1,0:T(8,128)S(1)}, u32[]{:S(2)}, u32[]{:S(2)}) async-start(f32[8,4,8,128]{3,2,1,0:T(8,128)} %get-tuple-element.34), calls=%async_computation.8 | async-start | bytes 262144 | tf_op jit(solution)/shard_map/all_to_all | solution.py:572
  133.1 5.8 %collective-permute-start.3 = (f32[4,8,128]{2,1,0:T(8,128)S(1)}, f32[4,8,128]{2,1,0:T(8,128)S(1)}, u32[]{:S(2)}, u32[]{:S(2)}) collective-permute-start(f32[4,8,128]{2,1,0:T(8,128)S(1)} %get-tuple-element.37.u2_ref), channel_id=1, source_target_pairs={{0,8},{8,16},{16,24},{24,32},{32,40},{40,48},{48,56},{56,0},{1,9},... | collective-permute-start | bytes 49160 | tf_op jit(solution)/shard_map/ppermute | solution.py:571
